TPU v7x, 128 devices: a whole 4x4x4 slice. The times are simulated.
128 devices in a mesh: dp: 32 (over x, z, core), tensor: 4 (over y).
Axes of the slice: x: 4, y: 4, z: 4, core: 2. Of those that a mesh axis runs over, the one named last changes fastest.
Arguments:
- hidden: bfloat16 [8192, 2048], P('dp'), may hold values from -200 to 200
- norm_gain: float32 [2048], replicated, may hold values from 0.5 to 2
- expert_ids: int32 [8192, 8], P(('dp', 'tensor')), may hold values from 0 to 127, all different within a row; in each aligned block of 64 rows (0 to 63, 64 to 127, ...) at most 8 rows name the same one
- gate_probs: float32 [8192, 8], P(('dp', 'tensor')), may hold values from 0.05 to 0.5
- out_grad: bfloat16 [8192, 2048], P(('dp', 'tensor')), may hold values from -8 to 8
- gate_weight: bfloat16 [128, 2048, 768], P(('dp', 'tensor')), may hold values from -0.125 to 0.125
- up_weight: bfloat16 [128, 2048, 768], P(('dp', 'tensor')), may hold values from -0.125 to 0.125
- down_weight: bfloat16 [128, 768, 2048], P(('dp', 'tensor')), may hold values from -0.21875 to 0.21875
Outputs:
- layer_out: bfloat16 [8192, 2048], P(('dp', 'tensor'))
- input_grad: bfloat16 [8192, 2048], P('dp')
- gate_grad: float32 [8192, 8], P(('dp', 'tensor'))
- gain_grad: float32 [2048], replicated
- gate_weight_grad: bfloat16 [128, 2048, 768], P(('dp', 'tensor'))
- up_weight_grad: bfloat16 [128, 2048, 768], P(('dp', 'tensor'))
- down_weight_grad: bfloat16 [128, 768, 2048], P(('dp', 'tensor'))
Inputs may be any that keep to these rules, and one draw needn't show every extreme that they name: `expert_ids`: within the rows of one device no expert is named by more than 8 rows, a bound that some block reaches.
All inputs are finite; a program needn't handle non-finite values.
Results may differ from a plain program's by a relative error of at most 0.0072.
Values may be sent and summed in bfloat16 or wider, within the bound.
No kernel may reach another device: no remote copies, remote signals or barrier semaphores. Data moves between devices by JAX's collectives and lax.ppermute only.
A program may use at most 128 MiB of HBM per device.

v0:
```python
import jax
import jax.numpy as jnp
from jax import lax
from jax.experimental import pallas as pl
from jax.experimental.pallas import tpu as pltpu
from jax.sharding import PartitionSpec as P

epsilon = 1e-06
AXES = ("dp", "tensor")
BF16 = jnp.bfloat16
F32 = jnp.float32
VMEM_LIMIT = 48 * 1024 * 1024


def slot_rows(ids_t, first, count, cap):
    top, tokens = ids_t.shape
    names = lax.broadcasted_iota(jnp.int32, (count, tokens), 0) + first
    named = jnp.zeros((count, tokens), F32)
    for k in range(top):
        named = named + jnp.where(ids_t[k : k + 1, :] == names, 1.0, 0.0)
    before = jnp.where(
        lax.broadcasted_iota(jnp.int32, (tokens, tokens), 0)
        < lax.broadcasted_iota(jnp.int32, (tokens, tokens), 1),
        1.0,
        0.0,
    ).astype(BF16)
    rank = jnp.dot(named.astype(BF16), before, preferred_element_type=F32)
    rank = jnp.where(named > 0.0, rank, -1.0)
    place = lax.broadcasted_iota(jnp.int32, (count, cap, tokens), 1).astype(F32)
    return jnp.where(rank[:, None, :] == place, 1.0, 0.0)


def pack_normed_kernel(quarter, ids_t, hidden, gain, buf, normed):
    step = pl.program_id(0)
    rows, count, cap = buf.shape[0], buf.shape[0] // 8, 8

    @pl.when(step == 0)
    def _():
        values = hidden[...].astype(F32)
        inverse = lax.rsqrt(jnp.mean(values * values, axis=-1, keepdims=True) + epsilon)
        normed[...] = (values * inverse * gain[...]).astype(BF16)

    chosen = slot_rows(ids_t[...], step * count, count, cap).reshape(rows, -1).astype(BF16)
    buf[...] = jnp.dot(chosen, normed[...], preferred_element_type=F32).astype(BF16)


def pack_scaled_kernel(ids_t, probs_t, grad, buf):
    step = pl.program_id(0)
    rows, count, cap = buf.shape[0], buf.shape[0] // 8, 8
    ids = ids_t[...]
    top, tokens = ids.shape
    chosen = slot_rows(ids, step * count, count, cap)
    names = lax.broadcasted_iota(jnp.int32, (count, tokens), 0) + step * count
    prob = jnp.zeros((count, tokens), F32)
    for k in range(top):
        prob = prob + jnp.where(ids[k : k + 1, :] == names, probs_t[k : k + 1, :], 0.0)
    weight = jnp.sum((chosen * prob[:, None, :]).reshape(rows, tokens), axis=1, keepdims=True)
    picked = jnp.dot(
        chosen.reshape(rows, tokens).astype(BF16), grad[...], preferred_element_type=F32
    )
    buf[...] = (picked * weight).astype(BF16)


def routes_kernel(ids, probs, routes, weights):
    tokens, top = ids.shape
    slots = routes.shape[1]
    cap = 8
    experts = slots // cap
    names = lax.broadcasted_iota(jnp.int32, (tokens, experts), 1)
    named = jnp.zeros((tokens, experts), F32)
    prob = jnp.zeros((tokens, experts), F32)
    for k in range(top):
        hit = ids[:, k : k + 1] == names
        named = named + jnp.where(hit, 1.0, 0.0)
        prob = prob + jnp.where(hit, probs[:, k : k + 1], 0.0)
    before = jnp.where(
        lax.broadcasted_iota(jnp.int32, (tokens, tokens), 1)
        < lax.broadcasted_iota(jnp.int32, (tokens, tokens), 0),
        1.0,
        0.0,
    ).astype(BF16)
    rank = jnp.dot(before, named.astype(BF16), preferred_element_type=F32)
    rank = jnp.where(named > 0.0, rank, -1.0).astype(BF16)
    spread = jnp.where(
        lax.broadcasted_iota(jnp.int32, (experts, slots), 1) // cap
        == lax.broadcasted_iota(jnp.int32, (experts, slots), 0),
        1.0,
        0.0,
    ).astype(BF16)
    place = (lax.broadcasted_iota(jnp.int32, (tokens, slots), 1) % cap).astype(F32)
    chosen = jnp.where(
        jnp.dot(rank, spread, preferred_element_type=F32) == place, 1.0, 0.0
    )
    routes[...] = chosen.astype(BF16)
    left = prob
    for part in range(3):
        piece = left.astype(BF16)
        left = left - piece.astype(F32)
        weights[part * tokens : (part + 1) * tokens, :] = (
            chosen * jnp.dot(piece, spread, preferred_element_type=F32)
        ).astype(BF16)


def combine_kernel(quarter, ids, routes, weights, rows, hidden, grad, *rest):
    layer_out, gate_grad = rest[-2:]
    tokens, top = ids.shape
    slots = routes.shape[1]
    parts = jnp.dot(weights[...], rows[...], preferred_element_type=F32)
    total = parts[:tokens] + parts[tokens : 2 * tokens] + parts[2 * tokens :]
    layer_out[...] = (hidden[...].astype(F32) + total).astype(BF16)
    dots = lax.dot_general(
        grad[...], rows[...], (((1,), (1,)), ((), ())), preferred_element_type=F32
    )
    dots = jnp.where(routes[...].astype(F32) > 0.0, dots, 0.0)
    expert = lax.broadcasted_iota(jnp.int32, (tokens, slots), 1) // 8
    column = lax.broadcasted_iota(jnp.int32, (tokens, top), 1)
    found = jnp.zeros((tokens, top), F32)
    for k in range(top):
        mine = jnp.sum(jnp.where(expert == ids[:, k : k + 1], dots, 0.0), axis=1, keepdims=True)
        found = found + jnp.where(column == k, mine, 0.0)
    gate_grad[...] = found


def norm_grad_kernel(quarter, routes, rows, hidden, gain, grad, own_grad, gain_part, total):
    step = pl.program_id(0)

    @pl.when(step == 0)
    def _():
        total[...] = jnp.zeros_like(total)

    total[...] += jnp.dot(routes[...], rows[...], preferred_element_type=F32)

    @pl.when(step == pl.num_programs(0) - 1)
    def _():
        values = hidden[...].astype(F32)
        inverse = lax.rsqrt(jnp.mean(values * values, axis=-1, keepdims=True) + epsilon)
        unit = values * inverse
        summed = total[...]
        gain_part[...] = jnp.sum(summed * unit, axis=0, keepdims=True)
        upstream = summed * gain[...]
        own_grad[...] = (
            grad[...].astype(F32)
            + inverse * (upstream - unit * jnp.mean(upstream * unit, axis=-1, keepdims=True))
        ).astype(BF16)


def exchange(block):
    return lax.all_to_all(block, AXES, split_axis=0, concat_axis=0, tiled=True)


def after(value, *earlier):
    return lax.optimization_barrier((value, *earlier))[0]


def params():
    return pltpu.CompilerParams(vmem_limit_bytes=VMEM_LIMIT)


def cost(flops, moved):
    return pl.CostEstimate(flops=flops, bytes_accessed=moved, transcendentals=0)


def dot(a, b, dims):
    return lax.dot_general(a, b, (dims, ((), ())), preferred_element_type=F32)


def per_device(
    hidden, norm_gain, expert_ids, gate_probs, out_grad, gate_weight, up_weight, down_weight
):
    own, width = out_grad.shape
    top = expert_ids.shape[1]
    devices = lax.axis_size(AXES)
    cap = 8
    slots = devices * cap
    steps = 4
    quarter = lax.axis_index("tensor").astype(jnp.int32).reshape(1)
    gain = norm_gain.reshape(1, width)
    ids_t = expert_ids.T
    probs_t = gate_probs.T

    def whole(*shape):
        return pl.BlockSpec(shape, lambda *_: (0,) * len(shape))

    normed_buf = pl.pallas_call(
        pack_normed_kernel,
        grid_spec=pltpu.PrefetchScalarGridSpec(
            num_scalar_prefetch=1,
            grid=(steps,),
            in_specs=[
                whole(top, own),
                pl.BlockSpec((own, width), lambda i, q: (q[0], 0)),
                whole(1, width),
            ],
            out_specs=pl.BlockSpec((slots // steps, width), lambda i, q: (i, 0)),
            scratch_shapes=[pltpu.VMEM((own, width), BF16)],
        ),
        out_shape=jax.ShapeDtypeStruct((slots, width), BF16),
        compiler_params=params(),
        cost_estimate=cost(2 * slots * own * width, 2 * slots * width),
        name="pack_normed",
    )(quarter, ids_t, hidden, gain)
    inputs = exchange(normed_buf)

    scaled_buf = pl.pallas_call(
        pack_scaled_kernel,
        grid=(steps,),
        in_specs=[whole(top, own), whole(top, own), whole(own, width)],
        out_specs=pl.BlockSpec((slots // steps, width), lambda i: (i, 0)),
        out_shape=jax.ShapeDtypeStruct((slots, width), BF16),
        compiler_params=params(),
        cost_estimate=cost(2 * slots * own * width, 2 * slots * width),
        name="pack_scaled",
    )(after(ids_t, normed_buf), probs_t, out_grad)
    cotan = exchange(after(scaled_buf, inputs))

    routes, weights = pl.pallas_call(
        routes_kernel,
        out_shape=[
            jax.ShapeDtypeStruct((own, slots), BF16),
            jax.ShapeDtypeStruct((3 * own, slots), BF16),
        ],
        compiler_params=params(),
        cost_estimate=cost(2 * 4 * own * devices * slots, 8 * own * slots),
        name="routes",
    )(after(expert_ids, normed_buf), gate_probs)

    gate_w, up_w, down_w = gate_weight[0], up_weight[0], down_weight[0]
    gate_pre = dot(inputs, gate_w, ((1,), (0,)))
    up_pre = dot(inputs, up_w, ((1,), (0,)))
    sigma = jax.nn.sigmoid(gate_pre)
    silu_vals = gate_pre * sigma
    act = (silu_vals * up_pre).astype(BF16)
    half = width // 2
    result_a = dot(act, down_w[:, :half], ((1,), (0,))).astype(BF16)
    result_b = dot(act, down_w[:, half:], ((1,), (0,))).astype(BF16)
    returned_a = exchange(after(result_a, cotan))

    act_grad = dot(cotan, down_w, ((1,), (1,)))
    gate_pgrad = (act_grad * up_pre * sigma * (1.0 + gate_pre * (1.0 - sigma))).astype(BF16)
    up_pgrad = (act_grad * silu_vals).astype(BF16)
    back = dot(gate_pgrad, gate_w, ((1,), (1,))) + dot(up_pgrad, up_w, ((1,), (1,)))
    back = back.astype(BF16)
    back_rows = exchange(after(back, returned_a))
    returned_b = exchange(after(result_b, back_rows))

    gate_pgrad, up_pgrad, act_late = lax.optimization_barrier(
        (gate_pgrad, up_pgrad, act, back)
    )[:3]
    gate_wgrad = dot(inputs, gate_pgrad, ((0,), (0,))).astype(BF16)
    up_wgrad = dot(inputs, up_pgrad, ((0,), (0,))).astype(BF16)
    down_grad = dot(act_late, cotan, ((0,), (0,))).astype(BF16)

    def combine(rows, part, earlier):
        columns = rows.shape[1]
        extra = [] if earlier is None else [earlier]
        return pl.pallas_call(
            combine_kernel,
            grid_spec=pltpu.PrefetchScalarGridSpec(
                num_scalar_prefetch=1,
                grid=(1,),
                in_specs=[
                    whole(own, top),
                    whole(own, slots),
                    whole(3 * own, slots),
                    whole(slots, columns),
                    pl.BlockSpec((own, columns), lambda i, q: (q[0], part)),
                    pl.BlockSpec((own, columns), lambda i, q: (0, part)),
                ]
                + [pl.BlockSpec(memory_space=pl.ANY)] * len(extra),
                out_specs=[
                    pl.BlockSpec((own, columns), lambda i, q: (0, part)),
                    whole(own, top),
                ],
            ),
            out_shape=[
                jax.ShapeDtypeStruct((own, width), BF16),
                jax.ShapeDtypeStruct((own, top), F32),
            ],
            input_output_aliases={7: 0} if extra else {},
            compiler_params=params(),
            cost_estimate=cost(8 * own * slots * columns, 2 * slots * columns),
            name=f"combine_{part}",
        )(quarter, expert_ids, routes, weights, rows, hidden, out_grad, *extra)

    layer_out, gate_grad_a = combine(returned_a, 0, None)

    own_grad, gain_part = pl.pallas_call(
        norm_grad_kernel,
        grid_spec=pltpu.PrefetchScalarGridSpec(
            num_scalar_prefetch=1,
            grid=(steps,),
            in_specs=[
                pl.BlockSpec((own, slots // steps), lambda i, q: (0, i)),
                pl.BlockSpec((slots // steps, width), lambda i, q: (i, 0)),
                pl.BlockSpec((own, width), lambda i, q: (q[0], 0)),
                whole(1, width),
                whole(own, width),
            ],
            out_specs=[whole(own, width), whole(1, width)],
            scratch_shapes=[pltpu.VMEM((own, width), F32)],
        ),
        out_shape=[
            jax.ShapeDtypeStruct((own, width), BF16),
            jax.ShapeDtypeStruct((1, width), F32),
        ],
        compiler_params=params(),
        cost_estimate=cost(2 * own * slots * width, 2 * slots * width),
        name="norm_grad",
    )(quarter, routes, back_rows, hidden, gain, out_grad)
    input_grad = lax.all_gather(own_grad, "tensor", axis=0, tiled=True)
    gain_grad = lax.psum(gain_part[0], AXES)

    layer_out, gate_grad_b = combine(returned_b, 1, layer_out)
    gate_grad = gate_grad_a + gate_grad_b
    return (
        layer_out,
        input_grad,
        gate_grad,
        gain_grad,
        gate_wgrad[None],
        up_wgrad[None],
        down_grad[None],
    )


def solution(mesh):
    in_specs = (
        P("dp", None),
        P(),
        P(AXES, None),
        P(AXES, None),
        P(AXES, None),
        P(AXES, None, None),
        P(AXES, None, None),
        P(AXES, None, None),
    )
    out_specs = (
        P(AXES, None),
        P("dp", None),
        P(AXES, None),
        P(),
        P(AXES, None, None),
        P(AXES, None, None),
        P(AXES, None, None),
    )
    return jax.shard_map(
        per_device, mesh=mesh, in_specs=in_specs, out_specs=out_specs, check_vma=False
    )
```

profile of v0, /device:TPU:0, one launch (start us, length us, event | category | flops | bytes accessed | tf_op | source)
XLA Modules:
  0.0 365.0 jit_solution(10394316258664837746)
XLA Ops:
  7.2 0.0 copy-start
  7.2 0.0 copy-start.4
  7.2 1.4 copy-done.4
  8.6 0.7 copy-done.14
  9.3 0.7 copy-done.16
  10.0 2.4 pack_normed.1
  12.4 2.0 copy-done.3
  14.4 11.7 %all-to-all-start = ((bf16[128,8,2048]{2,1,0:T(8,128)(2,1)}), bf16[128,8,2048]{2,1,0:T(8,128)(2,1)}, u32[]{:S(2)}, u32[]{:S(2)}) async-start(bf16[128,8,2048]{2,1,0:T(8,128)(2,1)} %bitcast.58), calls=%async_computation | async-start | bytes 8388608 | tf_op jit(solution)/shard_map/all_to_all | solution.py:148
  26.1 2.2 pack_scaled.1
  28.4 2.0 copy-done.2
  30.4 47.9 %all-to-all-done = bf16[128,8,2048]{2,1,0:T(8,128)(2,1)} async-done(((bf16[128,8,2048]{2,1,0:T(8,128)(2,1)}), bf16[128,8,2048]{2,1,0:T(8,128)(2,1)}, u32[]{:S(2)}, u32[]{:S(2)}) %all-to-all-start) | async-done | bytes 4194336 | tf_op jit(solution)/shard_map/all_to_all | solution.py:148
  78.3 6.0 %all-to-all-start.1 = ((bf16[128,8,2048]{2,1,0:T(8,128)(2,1)}), bf16[128,8,2048]{2,1,0:T(8,128)(2,1)}, u32[]{:S(2)}, u32[]{:S(2)}) async-start(bf16[128,8,2048]{2,1,0:T(8,128)(2,1)} %bitcast.57), calls=%async_computation.1 | async-start | bytes 8388608 | tf_op jit(solution)/shard_map/all_to_all | solution.py:148
  84.3 0.0 copy-start.21
  84.3 7.4 %fusion.5 = f32[1024,768]{1,0:T(8,128)} fusion(bf16[1,2048,768]{2,1,0:T(8,128)(2,1)S(1)} %copy-done, bf16[128,8,2048]{2,1,0:T(8,128)(2,1)} %all-to-all-done), kind=kOutput, calls=%fused_computation.9 | convolution fusion | flops 3221225472 | bytes 10485760 | tf_op jit(solution)/shard_map/dot_general | solution.py:164
  91.8 7.3 %fusion.1 = f32[1024,768]{1,0:T(8,128)} fusion(bf16[1,2048,768]{2,1,0:T(8,128)(2,1)S(1)} %copy-done.21, bf16[128,8,2048]{2,1,0:T(8,128)(2,1)} %all-to-all-done), kind=kOutput, calls=%fused_computation.5 | convolution fusion | flops 3221225472 | bytes 10485760 | tf_op jit(solution)/shard_map/dot_general | solution.py:164
  99.1 37.3 %all-to-all-done.1 = bf16[128,8,2048]{2,1,0:T(8,128)(2,1)} async-done(((bf16[128,8,2048]{2,1,0:T(8,128)(2,1)}), bf16[128,8,2048]{2,1,0:T(8,128)(2,1)}, u32[]{:S(2)}, u32[]{:S(2)}) %all-to-all-start.1) | async-done | bytes 4194336 | tf_op jit(solution)/shard_map/all_to_all | solution.py:148
  136.4 11.1 %multiply_convert_fusion = (bf16[1024,768]{1,0:T(8,128)(2,1)}, bf16[1024,768]{1,0:T(8,128)(2,1)}, bf16[1024,768]{1,0:T(8,128)(2,1)S(1)}) fusion(f32[1024,768]{1,0:T(8,128)} %fusion.5, f32[1024,768]{1,0:T(8,128)} %fusion.1, bf16[1,768,2048]{2,1,0:T(8,128)(2,1)} %param.15, bf16[128,8,2048]{2,1,0:T(8,128)(2,1)} %all-to-all-done.1), kind=kOutput, calls=%fused_computation.11 | convolution fusion | flops 3233021952 | bytes 18350080 | tf_op jit(solution)/shard_map/dot_general | solution.py:164
  147.5 3.1 convolution_convert_fusion.3
  150.6 6.1 %all-to-all-start.2 = ((bf16[128,8,1024]{2,1,0:T(8,128)(2,1)}), bf16[128,8,1024]{2,1,0:T(8,128)(2,1)}, u32[]{:S(2)}, u32[]{:S(2)}) async-start(bf16[128,8,1024]{2,1,0:T(8,128)(2,1)} %bitcast.66), calls=%async_computation.2 | async-start | bytes 4194304 | tf_op jit(solution)/shard_map/all_to_all | solution.py:148
  156.7 5.0 %fusion.3 = f32[1024,2048]{1,0:T(8,128)S(1)} fusion(bf16[1024,768]{1,0:T(8,128)(2,1)} %get-tuple-element.38, bf16[1,2048,768]{2,1,0:T(8,128)(2,1)S(1)} %copy-done), kind=kOutput, calls=%fused_computation.7 | convolution fusion | flops 3221225472 | bytes 13107200 | tf_op jit(solution)/shard_map/dot_general | solution.py:164
  161.7 5.1 %add_convert_fusion = bf16[1024,2048]{1,0:T(8,128)(2,1)} fusion(f32[1024,2048]{1,0:T(8,128)S(1)} %fusion.3, bf16[1024,768]{1,0:T(8,128)(2,1)S(1)} %copy-done.26, bf16[1,2048,768]{2,1,0:T(8,128)(2,1)S(1)} %copy-done.22), kind=kOutput, calls=%fused_computation | convolution fusion | flops 3225419776 | bytes 17301504 | tf_op jit(solution)/shard_map/dot_general | solution.py:164
  166.8 19.4 %all-to-all-done.2 = bf16[128,8,1024]{2,1,0:T(8,128)(2,1)} async-done(((bf16[128,8,1024]{2,1,0:T(8,128)(2,1)}), bf16[128,8,1024]{2,1,0:T(8,128)(2,1)}, u32[]{:S(2)}, u32[]{:S(2)}) %all-to-all-start.2) | async-done | bytes 2097184 | tf_op jit(solution)/shard_map/all_to_all | solution.py:148
  186.2 6.0 %all-to-all-start.3 = ((bf16[128,8,2048]{2,1,0:T(8,128)(2,1)}), bf16[128,8,2048]{2,1,0:T(8,128)(2,1)}, u32[]{:S(2)}, u32[]{:S(2)}) async-start(bf16[128,8,2048]{2,1,0:T(8,128)(2,1)} %bitcast.65), calls=%async_computation.3 | async-start | bytes 8388608 | tf_op jit(solution)/shard_map/all_to_all | solution.py:148
  192.2 0.7 copy.19.ids
  192.9 0.1 copy.17.probs
  192.9 0.1 copy.16.ids
  193.0 0.6 routes.1
  193.6 0.0 copy-start.9
  193.6 4.7 %convolution_convert_fusion.4 = bf16[1024,1024]{1,0:T(8,128)(2,1)} fusion(bf16[1024,768]{1,0:T(8,128)(2,1)S(1)} %copy-done.25, bf16[768,2048]{1,0:T(8,128)(2,1)} %bitcast.67), kind=kOutput, calls=%fused_computation.20 | convolution fusion | flops 1611661312 | bytes 5242880 | tf_op jit(solution)/shard_map/dot_general | solution.py:164
  198.3 46.0 %all-to-all-done.3 = bf16[128,8,2048]{2,1,0:T(8,128)(2,1)} async-done(((bf16[128,8,2048]{2,1,0:T(8,128)(2,1)}), bf16[128,8,2048]{2,1,0:T(8,128)(2,1)}, u32[]{:S(2)}, u32[]{:S(2)}) %all-to-all-start.3) | async-done | bytes 4194336 | tf_op jit(solution)/shard_map/all_to_all | solution.py:148
  244.4 5.8 %all-to-all-start.4 = ((bf16[128,8,1024]{2,1,0:T(8,128)(2,1)}), bf16[128,8,1024]{2,1,0:T(8,128)(2,1)}, u32[]{:S(2)}, u32[]{:S(2)}) async-start(bf16[128,8,1024]{2,1,0:T(8,128)(2,1)} %bitcast.15), calls=%async_computation.4 | async-start | bytes 4194304 | tf_op jit(solution)/shard_map/all_to_all | solution.py:148
  250.2 0.0 copy-start.5
  250.2 0.0 copy-start.17
  250.2 0.3 all-gather.2.cloned.1.call-start
  250.5 7.9 %fusion.8 = bf16[1,2048,768]{2,1,0:T(8,128)(2,1)} fusion(bf16[1024,768]{1,0:T(8,128)(2,1)} %get-tuple-element.38, bf16[128,8,2048]{2,1,0:T(8,128)(2,1)} %all-to-all-done), kind=kOutput, calls=%fused_computation.16 | convolution fusion | flops 3222798336 | bytes 8912896 | tf_op jit(solution)/shard_map/dot_general | solution.py:164
  258.4 4.6 %norm_grad.1 = (bf16[64,2048]{1,0:T(8,128)(2,1)}, f32[1,2048]{1,0:T(1,128)S(1)}) custom-call(s32[1]{0:T(128)} %bitcast.quarter, bf16[64,1024]{1,0:T(8,128)(2,1)S(1)} %get-tuple-element.25.routes, bf16[1024,2048]{1,0:T(8,128)(2,1)} %bitcast.14.rows, bf16[256,2048]{1,0:T(8,128)(2,1)S(1)} %copy-done.5, f32[1,2048]{1,0:T(1,128)S(1)} %bitcast.62, ...), custom_call_target="tpu_custom_call" | custom-call | flops 268435456 | bytes 4194304 | tf_op jit(solution)/shard_map/norm_grad/pallas_call | solution.py:287
  263.0 0.0 all-gather.2.cloned.1.call-update
  263.1 7.9 %fusion.9 = bf16[1,2048,768]{2,1,0:T(8,128)(2,1)} fusion(bf16[1024,768]{1,0:T(8,128)(2,1)} %get-tuple-element.39, bf16[128,8,2048]{2,1,0:T(8,128)(2,1)} %all-to-all-done), kind=kOutput, calls=%fused_computation.17 | convolution fusion | flops 3222798336 | bytes 8912896 | tf_op jit(solution)/shard_map/dot_general | solution.py:164
  271.0 7.2 %fusion.10 = bf16[1,768,2048]{2,1,0:T(8,128)(2,1)} fusion(bf16[1024,768]{1,0:T(8,128)(2,1)S(1)} %copy-done.25, bf16[128,8,2048]{2,1,0:T(8,128)(2,1)} %all-to-all-done.1), kind=kOutput, calls=%fused_computation.18 | convolution fusion | flops 3222798336 | bytes 8912896 | tf_op jit(solution)/shard_map/dot_general | solution.py:164
  278.2 3.4 combine_0.1
  281.5 0.6 copy-done.18
  282.2 66.9 %psum.7 = f32[2048]{0:T(1024)} all-reduce(f32[2048]{0:T(1024)S(1)} %bitcast.64), channel_id=1, replica_groups=mesh['dp'=32,'tensor'=4] {'dp','tensor'}, use_global_device_ids=true, to_apply=%region_0.0 | all-reduce | flops 2048 | bytes 16384 | tf_op jit(solution)/shard_map/psum | solution.py:311
  349.1 1.4 copy-done.7
  350.4 1.0 copy-done.11
  351.4 0.8 copy-done.13
  352.2 3.0 combine_1.1
  355.2 0.7 copy.20
  355.9 2.3 copy.23
  (42 shorter events, 0.1 us)
Async XLA Ops:
  7.2 77.2 %copy-start = (bf16[1,2048,768]{2,1,0:T(8,128)(2,1)S(1)}, bf16[1,2048,768]{2,1,0:T(8,128)(2,1)}, u32[]{:S(2)}) copy-start(bf16[1,2048,768]{2,1,0:T(8,128)(2,1)} %param.13) | copy-start | bytes 9437188
  7.2 1.4 copy-start.4
  8.6 0.7 copy-start.14
  9.3 0.7 copy-start.16
  12.4 2.0 copy-start.3
  14.4 11.7 %copy-start.8 = (bf16[64,2048]{1,0:T(8,128)(2,1)S(1)}, bf16[64,2048]{1,0:T(8,128)(2,1)}, u32[]{:S(2)}) copy-start(bf16[64,2048]{1,0:T(8,128)(2,1)} %grad.7) | copy-start | bytes 786436
  14.4 11.7 %copy-start.15 = (s32[64,8]{0,1:T(8,128)S(1)}, s32[64,8]{0,1:T(8,128)}, u32[]{:S(2)}) copy-start(s32[64,8]{0,1:T(8,128)} %param.10) | copy-start | bytes 6148
  14.4 11.7 %copy-start.20 = (f32[64,8]{0,1:T(8,128)S(1)}, f32[64,8]{0,1:T(8,128)}, u32[]{:S(2)}) copy-start(f32[64,8]{0,1:T(8,128)} %param.11) | copy-start | bytes 6148
  14.4 63.9 %all-to-all-start = ((bf16[128,8,2048]{2,1,0:T(8,128)(2,1)}), bf16[128,8,2048]{2,1,0:T(8,128)(2,1)}, u32[]{:S(2)}, u32[]{:S(2)}) async-start(bf16[128,8,2048]{2,1,0:T(8,128)(2,1)} %bitcast.58), calls=%async_computation | async-start | bytes 8388608 | tf_op jit(solution)/shard_map/all_to_all | solution.py:148
  28.4 2.0 copy-start.2
  78.3 58.1 %all-to-all-start.1 = ((bf16[128,8,2048]{2,1,0:T(8,128)(2,1)}), bf16[128,8,2048]{2,1,0:T(8,128)(2,1)}, u32[]{:S(2)}, u32[]{:S(2)}) async-start(bf16[128,8,2048]{2,1,0:T(8,128)(2,1)} %bitcast.57), calls=%async_computation.1 | async-start | bytes 8388608 | tf_op jit(solution)/shard_map/all_to_all | solution.py:148
  84.3 7.4 %copy-start.21 = (bf16[1,2048,768]{2,1,0:T(8,128)(2,1)S(1)}, bf16[1,2048,768]{2,1,0:T(8,128)(2,1)}, u32[]{:S(2)}) copy-start(bf16[1,2048,768]{2,1,0:T(8,128)(2,1)} %param.14) | copy-start | bytes 9437188
  136.3 11.1 %copy-start.23 = (bf16[1,768,2048]{2,1,0:T(8,128)(2,1)S(1)}, bf16[1,768,2048]{2,1,0:T(8,128)(2,1)}, u32[]{:S(2)}) copy-start(bf16[1,768,2048]{2,1,0:T(8,128)(2,1)} %param.15) | copy-start | bytes 9437188
  147.5 3.1 copy-start.24
  150.6 35.6 %all-to-all-start.2 = ((bf16[128,8,1024]{2,1,0:T(8,128)(2,1)}), bf16[128,8,1024]{2,1,0:T(8,128)(2,1)}, u32[]{:S(2)}, u32[]{:S(2)}) async-start(bf16[128,8,1024]{2,1,0:T(8,128)(2,1)} %bitcast.66), calls=%async_computation.2 | async-start | bytes 4194304 | tf_op jit(solution)/shard_map/all_to_all | solution.py:148
  156.7 5.0 %copy-start.22 = (bf16[1,2048,768]{2,1,0:T(8,128)(2,1)S(1)}, bf16[1,2048,768]{2,1,0:T(8,128)(2,1)}, u32[]{:S(2)}) copy-start(bf16[1,2048,768]{2,1,0:T(8,128)(2,1)} %param.14) | copy-start | bytes 9437188
  156.7 5.0 %copy-start.26 = (bf16[1024,768]{1,0:T(8,128)(2,1)S(1)}, bf16[1024,768]{1,0:T(8,128)(2,1)}, u32[]{:S(2)}) copy-start(bf16[1024,768]{1,0:T(8,128)(2,1)} %get-tuple-element.39) | copy-start | bytes 4718596
  186.2 7.4 %copy-start.25 = (bf16[1024,768]{1,0:T(8,128)(2,1)S(1)}, bf16[1024,768]{1,0:T(8,128)(2,1)}, u32[]{:S(2)}) copy-start(bf16[1024,768]{1,0:T(8,128)(2,1)} %copy-done.24) | copy-start | bytes 4718596
  186.2 58.2 %all-to-all-start.3 = ((bf16[128,8,2048]{2,1,0:T(8,128)(2,1)}), bf16[128,8,2048]{2,1,0:T(8,128)(2,1)}, u32[]{:S(2)}, u32[]{:S(2)}) async-start(bf16[128,8,2048]{2,1,0:T(8,128)(2,1)} %bitcast.65), calls=%async_computation.3 | async-start | bytes 8388608 | tf_op jit(solution)/shard_map/all_to_all | solution.py:148
  193.6 4.7 %copy-start.9 = (bf16[192,1024]{1,0:T(8,128)(2,1)}, bf16[192,1024]{1,0:T(8,128)(2,1)S(1)}, u32[]{:S(2)}) copy-start(bf16[192,1024]{1,0:T(8,128)(2,1)S(1)} %get-tuple-element.26.weights) | copy-start | bytes 1179652
  244.4 104.7 %all-to-all-start.4 = ((bf16[128,8,1024]{2,1,0:T(8,128)(2,1)}), bf16[128,8,1024]{2,1,0:T(8,128)(2,1)}, u32[]{:S(2)}, u32[]{:S(2)}) async-start(bf16[128,8,1024]{2,1,0:T(8,128)(2,1)} %bitcast.15), calls=%async_computation.4 | async-start | bytes 4194304 | tf_op jit(solution)/shard_map/all_to_all | solution.py:148
  250.2 8.2 %copy-start.5 = (bf16[256,2048]{1,0:T(8,128)(2,1)S(1)}, bf16[256,2048]{1,0:T(8,128)(2,1)}, u32[]{:S(2)}) copy-start(bf16[256,2048]{1,0:T(8,128)(2,1)} %hidden.7) | copy-start | bytes 3145732
  250.2 8.2 %copy-start.17 = (f32[2048]{0:T(1024)S(1)}, f32[2048]{0:T(1024)}, u32[]{:S(2)}) copy-start(f32[2048]{0:T(1024)} %param.9) | copy-start | bytes 24580
  250.2 98.8 %all-gather.2.cloned.1.call-start = ((), (), s32[]{:S(2)}) async-start(), calls=%async_computation.5 | async-start | bytes 1310720 | tf_op jit(solution)/shard_map/all_gather | solution.py:310
  270.9 7.2 %copy-start.6 = (bf16[256,2048]{1,0:T(8,128)(2,1)S(1)}, bf16[256,2048]{1,0:T(8,128)(2,1)}, u32[]{:S(2)}) copy-start(bf16[256,2048]{1,0:T(8,128)(2,1)} %hidden.7) | copy-start | bytes 3145732
  270.9 7.2 %copy-start.10 = (bf16[192,1024]{1,0:T(8,128)(2,1)S(1)}, bf16[192,1024]{1,0:T(8,128)(2,1)}, u32[]{:S(2)}) copy-start(bf16[192,1024]{1,0:T(8,128)(2,1)} %copy-done.9) | copy-start | bytes 1179652
  270.9 7.2 %copy-start.12 = (s32[64,8]{1,0:T(8,128)S(1)}, s32[64,8]{1,0:T(8,128)}, u32[]{:S(2)}) copy-start(s32[64,8]{1,0:T(8,128)} %copy.19.ids) | copy-start | bytes 6148
  281.5 0.6 copy-start.18
  349.0 9.1 %copy-start.1 = (bf16[1,2048,768]{2,1,0:T(8,128)(2,1)S(1)}, bf16[1,2048,768]{2,1,0:T(8,128)(2,1)}, u32[]{:S(2)}) copy-start(bf16[1,2048,768]{2,1,0:T(8,128)(2,1)} %param.13) | copy-start | bytes 9437188
  349.0 1.4 copy-start.7
  350.4 1.0 copy-start.11
  351.4 0.8 copy-start.13
  352.2 3.0 copy-start.19
Sparse Core Ops, SparseCore 0:
  263.2 24.9 all-gather.1
where the time goes:
time: 366 us; the launch traced here: 365 us
  waiting for transfers between devices  151 us (41%)
  blocking collectives  66.9 us (18%)
  matrix products  66.7 us (18%)
  starting transfers between devices  35.9 us (10%)
  Pallas kernels  16.2 us (4%)
  local copies, waits for them, and re-layouts  14.5 us (4%)
  between operations  14.3 us (4%)
    all_to_all x5, waiting for transfers between devices, exchange(): return lax.all_to_all(block, AXES, split_axis=0, concat_axis=0, tiled=True)  151 us
    psum x1, blocking collectives, per_device(): gain_grad = lax.psum(gain_part[0], AXES)  66.9 us
    dot_general x10, matrix products, dot(): return lax.dot_general(a, b, (dims, ((), ())), preferred_element_type=F32)  66.7 us
    all_to_all x5, starting transfers between devices, exchange(): return lax.all_to_all(block, AXES, split_axis=0, concat_axis=0, tiled=True)  35.6 us
    unnamed x58, local copies, waits for them, and re-layouts  14.4 us
  transfers between devices with their start and end apart: 6, of which 4 were waited for; matrix products, arithmetic and copies ran while one was open for 15% of the time, Pallas kernels for 3%

commit v1 on v0

--- a/solution.py
+++ b/solution.py
@@ -9,7 +9,7 @@
 AXES = ("dp", "tensor")
 BF16 = jnp.bfloat16
 F32 = jnp.float32
-VMEM_LIMIT = 48 * 1024 * 1024
+VMEM_LIMIT = 60 * 1024 * 1024
 
 
 def slot_rows(ids_t, first, count, cap):
@@ -101,24 +101,37 @@
         ).astype(BF16)
 
 
-def combine_kernel(quarter, ids, routes, weights, rows, hidden, grad, *rest):
-    layer_out, gate_grad = rest[-2:]
+def combine_kernel(
+    quarter, ids, routes, weights, rows, hidden, grad, layer_out, gate_grad, dots
+):
+    step = pl.program_id(0)
     tokens, top = ids.shape
     slots = routes.shape[1]
     parts = jnp.dot(weights[...], rows[...], preferred_element_type=F32)
     total = parts[:tokens] + parts[tokens : 2 * tokens] + parts[2 * tokens :]
     layer_out[...] = (hidden[...].astype(F32) + total).astype(BF16)
-    dots = lax.dot_general(
+    part = lax.dot_general(
         grad[...], rows[...], (((1,), (1,)), ((), ())), preferred_element_type=F32
     )
-    dots = jnp.where(routes[...].astype(F32) > 0.0, dots, 0.0)
-    expert = lax.broadcasted_iota(jnp.int32, (tokens, slots), 1) // 8
-    column = lax.broadcasted_iota(jnp.int32, (tokens, top), 1)
-    found = jnp.zeros((tokens, top), F32)
-    for k in range(top):
-        mine = jnp.sum(jnp.where(expert == ids[:, k : k + 1], dots, 0.0), axis=1, keepdims=True)
-        found = found + jnp.where(column == k, mine, 0.0)
-    gate_grad[...] = found
+
+    @pl.when(step == 0)
+    def _():
+        dots[...] = part
+
+    @pl.when(step > 0)
+    def _():
+        dots[...] += part
+
+    @pl.when(step == pl.num_programs(0) - 1)
+    def _():
+        mine = jnp.where(routes[...].astype(F32) > 0.0, dots[...], 0.0)
+        expert = lax.broadcasted_iota(jnp.int32, (tokens, slots), 1) // 8
+        column = lax.broadcasted_iota(jnp.int32, (tokens, 128), 1)
+        found = jnp.zeros((tokens, 128), F32)
+        for k in range(top):
+            own = jnp.where(expert == ids[:, k : k + 1], mine, 0.0)
+            found = found + jnp.where(column == k, jnp.sum(own, axis=1, keepdims=True), 0.0)
+        gate_grad[...] = found.T[:top, :]
 
 
 def norm_grad_kernel(quarter, routes, rows, hidden, gain, grad, own_grad, gain_part, total):
@@ -146,6 +159,31 @@
 
 def exchange(block):
     return lax.all_to_all(block, AXES, split_axis=0, concat_axis=0, tiled=True)
+
+
+def gather_group(block):
+    size = lax.axis_size("tensor")
+    mine = lax.axis_index("tensor")
+    rows = block.shape[0]
+    whole = jnp.zeros((size * rows, block.shape[1]), block.dtype)
+    moved = [(0, block)] + [
+        (step, lax.ppermute(block, "tensor", [(i, (i + step) % size) for i in range(size)]))
+        for step in (1, 3, 2)
+    ]
+    for step, piece in moved:
+        origin = (mine - step) % size
+        whole = lax.dynamic_update_slice_in_dim(whole, piece, origin * rows, 0)
+    return whole
+
+
+def sum_all(value):
+    for axis in AXES:
+        size = lax.axis_size(axis)
+        step = 1
+        while step < size:
+            value = value + lax.ppermute(value, axis, [(i, i ^ step) for i in range(size)])
+            step *= 2
+    return value
 
 
 def after(value, *earlier):
@@ -230,18 +268,19 @@
     sigma = jax.nn.sigmoid(gate_pre)
     silu_vals = gate_pre * sigma
     act = (silu_vals * up_pre).astype(BF16)
-    half = width // 2
-    result_a = dot(act, down_w[:, :half], ((1,), (0,))).astype(BF16)
-    result_b = dot(act, down_w[:, half:], ((1,), (0,))).astype(BF16)
-    returned_a = exchange(after(result_a, cotan))
-
+    result = dot(act, down_w, ((1,), (0,))).astype(BF16)
+    gate_pre, up_pre, act, cotan, result = lax.optimization_barrier(
+        (gate_pre, up_pre, act, cotan, result)
+    )
+    sigma = jax.nn.sigmoid(gate_pre)
+    silu_vals = gate_pre * sigma
     act_grad = dot(cotan, down_w, ((1,), (1,)))
     gate_pgrad = (act_grad * up_pre * sigma * (1.0 + gate_pre * (1.0 - sigma))).astype(BF16)
     up_pgrad = (act_grad * silu_vals).astype(BF16)
     back = dot(gate_pgrad, gate_w, ((1,), (1,))) + dot(up_pgrad, up_w, ((1,), (1,)))
     back = back.astype(BF16)
-    back_rows = exchange(after(back, returned_a))
-    returned_b = exchange(after(result_b, back_rows))
+    back_rows = exchange(back)
+    returned = exchange(after(result, back_rows))
 
     gate_pgrad, up_pgrad, act_late = lax.optimization_barrier(
         (gate_pgrad, up_pgrad, act, back)
@@ -249,40 +288,6 @@
     gate_wgrad = dot(inputs, gate_pgrad, ((0,), (0,))).astype(BF16)
     up_wgrad = dot(inputs, up_pgrad, ((0,), (0,))).astype(BF16)
     down_grad = dot(act_late, cotan, ((0,), (0,))).astype(BF16)
-
-    def combine(rows, part, earlier):
-        columns = rows.shape[1]
-        extra = [] if earlier is None else [earlier]
-        return pl.pallas_call(
-            combine_kernel,
-            grid_spec=pltpu.PrefetchScalarGridSpec(
-                num_scalar_prefetch=1,
-                grid=(1,),
-                in_specs=[
-                    whole(own, top),
-                    whole(own, slots),
-                    whole(3 * own, slots),
-                    whole(slots, columns),
-                    pl.BlockSpec((own, columns), lambda i, q: (q[0], part)),
-                    pl.BlockSpec((own, columns), lambda i, q: (0, part)),
-                ]
-                + [pl.BlockSpec(memory_space=pl.ANY)] * len(extra),
-                out_specs=[
-                    pl.BlockSpec((own, columns), lambda i, q: (0, part)),
-                    whole(own, top),
-                ],
-            ),
-            out_shape=[
-                jax.ShapeDtypeStruct((own, width), BF16),
-                jax.ShapeDtypeStruct((own, top), F32),
-            ],
-            input_output_aliases={7: 0} if extra else {},
-            compiler_params=params(),
-            cost_estimate=cost(8 * own * slots * columns, 2 * slots * columns),
-            name=f"combine_{part}",
-        )(quarter, expert_ids, routes, weights, rows, hidden, out_grad, *extra)
-
-    layer_out, gate_grad_a = combine(returned_a, 0, None)
 
     own_grad, gain_part = pl.pallas_call(
         norm_grad_kernel,
@@ -307,15 +312,42 @@
         cost_estimate=cost(2 * own * slots * width, 2 * slots * width),
         name="norm_grad",
     )(quarter, routes, back_rows, hidden, gain, out_grad)
-    input_grad = lax.all_gather(own_grad, "tensor", axis=0, tiled=True)
-    gain_grad = lax.psum(gain_part[0], AXES)
-
-    layer_out, gate_grad_b = combine(returned_b, 1, layer_out)
-    gate_grad = gate_grad_a + gate_grad_b
+    input_grad = gather_group(own_grad)
+    gain_grad = sum_all(gain_part)[0]
+
+    parts = 2
+    columns = width // parts
+    layer_out, gate_grad_t = pl.pallas_call(
+        combine_kernel,
+        grid_spec=pltpu.PrefetchScalarGridSpec(
+            num_scalar_prefetch=1,
+            grid=(parts,),
+            in_specs=[
+                whole(own, top),
+                whole(own, slots),
+                whole(3 * own, slots),
+                pl.BlockSpec((slots, columns), lambda i, q: (0, i)),
+                pl.BlockSpec((own, columns), lambda i, q: (q[0], i)),
+                pl.BlockSpec((own, columns), lambda i, q: (0, i)),
+            ],
+            out_specs=[
+                pl.BlockSpec((own, columns), lambda i, q: (0, i)),
+                whole(top, own),
+            ],
+            scratch_shapes=[pltpu.VMEM((own, slots), F32)],
+        ),
+        out_shape=[
+            jax.ShapeDtypeStruct((own, width), BF16),
+            jax.ShapeDtypeStruct((top, own), F32),
+        ],
+        compiler_params=params(),
+        cost_estimate=cost(8 * own * slots * width, 2 * slots * width),
+        name="combine",
+    )(quarter, expert_ids, routes, weights, returned, hidden, out_grad)
     return (
         layer_out,
         input_grad,
-        gate_grad,
+        gate_grad_t.T,
         gain_grad,
         gate_wgrad[None],
         up_wgrad[None],

time: 366 us -> 309 us (0.84)
  waiting for transfers between devices: 151 us -> 109 us
  starting transfers between devices: 35.9 us -> 50.2 us
  between operations: 14.3 us -> 1.07 us
  matrix products: 66.7 us -> 57.5 us
  blocking collectives: 66.9 us -> 57.8 us
  local copies, waits for them, and re-layouts: 14.5 us -> 7.27 us
  Pallas kernels: 16.2 us -> 22.6 us
    all_to_all x5 -> x3, waiting for transfers between devices: 151 us -> 78.6 us  [exchange(): return lax.all_to_all(block, AXES, split_axis=0, concat_axis=0, tiled=True)]
    psum x1 -> x0, blocking collectives: 66.9 us -> none  [per_device(): gain_grad = lax.psum(gain_part[0], AXES)]
    all_to_all x0 -> x1, blocking collectives: none -> 57.8 us  [exchange(): return lax.all_to_all(block, AXES, split_axis=0, concat_axis=0, tiled=True)]
    ppermute x0 -> x10, waiting for transfers between devices: none -> 30.4 us  [the longest x7 30.4 us: sum_all(): lax.ppermute(value, axis, [(i, i ^ step) for i in range(size)])]
    ppermute x0 -> x10, starting transfers between devices: none -> 26.5 us  [the longest x3 16.8 us: gather_group(): lax.ppermute(block, 'tensor', [(i, (i + step) % size) for i in range(size)])]
    all_to_all x5 -> x3, starting transfers between devices: 35.6 us -> 23.7 us  [exchange(): return lax.all_to_all(block, AXES, split_axis=0, concat_axis=0, tiled=True)]
    unnamed x58 -> x32, local copies, waits for them, and re-layouts: 14.4 us -> 2.6 us
    dot_general x10 -> x9, matrix products: 66.7 us -> 57.5 us  [dot(): return lax.dot_general(a, b, (dims, ((), ())), preferred_element_type=F32)]
  transfers between devices with their start and end apart: 6 -> 13, of which waited for: 4 -> 7; matrix products, arithmetic and copies ran while one was open for 15% -> 16% of each run, Pallas kernels for 3% -> 4%
where the time goes in v1:
time: 309 us; the launch traced here: 307 us
  waiting for transfers between devices  109 us (35%)
  blocking collectives  57.8 us (19%)
  matrix products  57.5 us (19%)
  starting transfers between devices  50.2 us (16%)
  Pallas kernels  22.6 us (7%)
  local copies, waits for them, and re-layouts  7.27 us (2%)
    all_to_all x3, waiting for transfers between devices, exchange(): return lax.all_to_all(block, AXES, split_axis=0, concat_axis=0, tiled=True)  78.6 us
    all_to_all x1, blocking collectives, exchange(): return lax.all_to_all(block, AXES, split_axis=0, concat_axis=0, tiled=True)  57.8 us
    dot_general x9, matrix products, dot(): return lax.dot_general(a, b, (dims, ((), ())), preferred_element_type=F32)  57.5 us
    ppermute x7, waiting for transfers between devices, sum_all(): lax.ppermute(value, axis, [(i, i ^ step) for i in range(size)])  30.4 us
    all_to_all x3, starting transfers between devices, exchange(): return lax.all_to_all(block, AXES, split_axis=0, concat_axis=0, tiled=True)  23.7 us
    ppermute x3, starting transfers between devices, gather_group(): lax.ppermute(block, 'tensor', [(i, (i + step) % size) for i in range(size)])  16.8 us
    ppermute x7, starting transfers between devices, sum_all(): lax.ppermute(value, axis, [(i, i ^ step) for i in range(size)])  9.68 us
  transfers between devices with their start and end apart: 13, of which 7 were waited for; matrix products, arithmetic and copies ran while one was open for 16% of the time, Pallas kernels for 4%

profile of v1, /device:TPU:0, one launch (start us, length us, event | category | flops | bytes accessed | tf_op | source)
XLA Modules:
  0.0 306.8 jit_solution(4755900650897517551)
XLA Ops:
  0.6 0.0 copy-start
  0.7 5.1 %pack_normed.1 = bf16[1024,2048]{1,0:T(8,128)(2,1)} custom-call(s32[1]{0:T(128)} %bitcast.quarter, s32[8,64]{1,0:T(8,128)} %bitcast.62, bf16[256,2048]{1,0:T(8,128)(2,1)} %hidden.5, f32[1,2048]{1,0:T(1,128)} %bitcast.64), custom_call_target="tpu_custom_call" | custom-call | flops 268435456 | bytes 4194304 | tf_op jit(solution)/shard_map/pack_normed/pallas_call | solution.py:222
  5.7 11.7 %all-to-all-start = ((bf16[128,8,2048]{2,1,0:T(8,128)(2,1)}), bf16[128,8,2048]{2,1,0:T(8,128)(2,1)}, u32[]{:S(2)}, u32[]{:S(2)}) async-start(bf16[128,8,2048]{2,1,0:T(8,128)(2,1)} %bitcast.59), calls=%async_computation | async-start | bytes 8388608 | tf_op jit(solution)/shard_map/all_to_all | solution.py:161
  17.4 4.7 %pack_scaled.1 = bf16[1024,2048]{1,0:T(8,128)(2,1)} custom-call(s32[8,64]{1,0:T(8,128)} %bitcast.63, f32[8,64]{1,0:T(8,128)} %bitcast.66, bf16[64,2048]{1,0:T(8,128)(2,1)} %grad.5), custom_call_target="tpu_custom_call" | custom-call | flops 268435456 | bytes 4194304 | tf_op jit(solution)/shard_map/pack_scaled/pallas_call | solution.py:242
  22.1 47.6 %all-to-all-done = bf16[128,8,2048]{2,1,0:T(8,128)(2,1)} async-done(((bf16[128,8,2048]{2,1,0:T(8,128)(2,1)}), bf16[128,8,2048]{2,1,0:T(8,128)(2,1)}, u32[]{:S(2)}, u32[]{:S(2)}) %all-to-all-start) | async-done | bytes 4194336 | tf_op jit(solution)/shard_map/all_to_all | solution.py:161
  69.6 6.0 %all-to-all-start.1 = ((bf16[128,8,2048]{2,1,0:T(8,128)(2,1)}), bf16[128,8,2048]{2,1,0:T(8,128)(2,1)}, u32[]{:S(2)}, u32[]{:S(2)}) async-start(bf16[128,8,2048]{2,1,0:T(8,128)(2,1)} %bitcast.58), calls=%async_computation.1 | async-start | bytes 8388608 | tf_op jit(solution)/shard_map/all_to_all | solution.py:161
  75.7 6.3 %fusion.8 = f32[1024,768]{1,0:T(8,128)S(1)} fusion(bf16[1,2048,768]{2,1,0:T(8,128)(2,1)} %param.13, bf16[128,8,2048]{2,1,0:T(8,128)(2,1)} %all-to-all-done), kind=kOutput, calls=%fused_computation.13 | convolution fusion | flops 3221225472 | bytes 10485760 | tf_op jit(solution)/shard_map/dot_general | solution.py:202
  82.0 0.0 copy-start.12
  82.0 8.6 %multiply_convert_fusion.2 = (bf16[1024,768]{1,0:T(8,128)(2,1)S(1)}, f32[1024,768]{1,0:T(8,128)}) fusion(f32[1024,768]{1,0:T(8,128)S(1)} %fusion.8, bf16[1,2048,768]{2,1,0:T(8,128)(2,1)S(1)} %copy-done.6, bf16[128,8,2048]{2,1,0:T(8,128)(2,1)} %all-to-all-done), kind=kOutput, calls=%fused_computation.18 | convolution fusion | flops 3225944064 | bytes 15204352 | tf_op jit(solution)/shard_map/dot_general | solution.py:202
  90.5 1.1 copy-done.8
  91.7 5.0 %convolution_convert_fusion = bf16[1024,2048]{1,0:T(8,128)(2,1)} fusion(bf16[1024,768]{1,0:T(8,128)(2,1)S(1)} %get-tuple-element.42, bf16[1,768,2048]{2,1,0:T(8,128)(2,1)S(1)} %copy-done), kind=kOutput, calls=%fused_computation.1 | convolution fusion | flops 3223322624 | bytes 8912896 | tf_op jit(solution)/shard_map/dot_general | solution.py:202
  96.7 31.0 %all-to-all-done.1 = bf16[128,8,2048]{2,1,0:T(8,128)(2,1)} async-done(((bf16[128,8,2048]{2,1,0:T(8,128)(2,1)}), bf16[128,8,2048]{2,1,0:T(8,128)(2,1)}, u32[]{:S(2)}, u32[]{:S(2)}) %all-to-all-start.1) | async-done | bytes 4194336 | tf_op jit(solution)/shard_map/all_to_all | solution.py:161
  127.7 8.4 %multiply_convert_fusion = (bf16[1024,768]{1,0:T(8,128)(2,1)S(1)}, bf16[1024,768]{1,0:T(8,128)(2,1)S(1)}) fusion(f32[1024,768]{1,0:T(8,128)} %copy-done.12, f32[1024,768]{1,0:T(8,128)} %get-tuple-element.32, bf16[1024,2048]{1,0:T(8,128)(2,1)} %bitcast.9, bf16[1,768,2048]{2,1,0:T(8,128)(2,1)S(1)} %copy-done), kind=kOutput, calls=%fused_computation.15 | convolution fusion | flops 3231449088 | bytes 16777216 | tf_op jit(solution)/shard_map/dot_general | solution.py:202
  136.1 0.0 copy-start.10
  136.1 3.4 %fusion.6 = f32[1024,2048]{1,0:T(8,128)S(1)} fusion(bf16[1024,768]{1,0:T(8,128)(2,1)S(1)} %get-tuple-element.40, bf16[1,2048,768]{2,1,0:T(8,128)(2,1)S(1)} %copy-done.5), kind=kOutput, calls=%fused_computation.11 | convolution fusion | flops 3221225472 | bytes 13107200 | tf_op jit(solution)/shard_map/dot_general | solution.py:202
  139.6 3.9 %add_convert_fusion = bf16[1024,2048]{1,0:T(8,128)(2,1)S(1)} fusion(f32[1024,2048]{1,0:T(8,128)S(1)} %fusion.6, bf16[1024,768]{1,0:T(8,128)(2,1)S(1)} %get-tuple-element.41, bf16[1,2048,768]{2,1,0:T(8,128)(2,1)S(1)} %copy-done.7), kind=kOutput, calls=%fused_computation | convolution fusion | flops 3225419776 | bytes 17301504 | tf_op jit(solution)/shard_map/dot_general | solution.py:202
  143.5 57.8 %all_to_all.46 = bf16[128,8,2048]{2,1,0:T(8,128)(2,1)} all-to-all(bf16[128,8,2048]{2,1,0:T(8,128)(2,1)S(1)} %bitcast.61), channel_id=1, replica_groups=mesh['dp'=32,'tensor'=4] {'dp','tensor'}, dimensions={0} | all-to-all | bytes 8388608 | tf_op jit(solution)/shard_map/all_to_all | solution.py:161
  201.4 6.0 %all-to-all-start.3 = ((bf16[128,8,2048]{2,1,0:T(8,128)(2,1)}), bf16[128,8,2048]{2,1,0:T(8,128)(2,1)}, u32[]{:S(2)}, u32[]{:S(2)}) async-start(bf16[128,8,2048]{2,1,0:T(8,128)(2,1)} %bitcast.60), calls=%async_computation.3 | async-start | bytes 8388608 | tf_op jit(solution)/shard_map/all_to_all | solution.py:161
  207.4 0.7 copy.16.probs
  208.1 0.7 copy.15.ids
  208.8 2.1 routes.1
  210.8 4.8 %norm_grad.1 = (bf16[64,2048]{1,0:T(8,128)(2,1)}, f32[1,2048]{1,0:T(1,128)}) custom-call(s32[1]{0:T(128)} %bitcast.quarter, bf16[64,1024]{1,0:T(8,128)(2,1)} %get-tuple-element.26.routes, bf16[1024,2048]{1,0:T(8,128)(2,1)} %bitcast.57, bf16[256,2048]{1,0:T(8,128)(2,1)} %hidden.5, f32[1,2048]{1,0:T(1,128)} %bitcast.65, bf16[64,2048]{1,0:T(8,128)(2,1)} %grad.5), custom_call_target="tpu_custom_call" | custom-call | flops 268435456 | bytes 4194304 | tf_op jit(solution)/shard_map/norm_grad/pallas_call | solution.py:292
  215.6 1.4 collective-permute-done.3
  217.0 0.7 add.73
  217.7 1.1 collective-permute-start.4
  218.8 7.6 %collective-permute-done.4 = f32[1,2048]{1,0:T(1,128)S(1)} collective-permute-done((f32[1,2048]{1,0:T(1,128)S(1)}, f32[1,2048]{1,0:T(1,128)S(1)}, u32[]{:S(2)}, u32[]{:S(2)}) %collective-permute-start.4) | collective-permute-done | bytes 8224 | tf_op jit(solution)/shard_map/ppermute | solution.py:184
  226.5 0.1 collective-permute-start.5
  226.5 0.7 copy.17.ids
  227.2 15.7 %collective-permute-done.5 = f32[1,2048]{1,0:T(1,128)S(1)} collective-permute-done((f32[1,2048]{1,0:T(1,128)S(1)}, f32[1,2048]{1,0:T(1,128)S(1)}, u32[]{:S(2)}, u32[]{:S(2)}) %collective-permute-start.5) | collective-permute-done | bytes 8224 | tf_op jit(solution)/shard_map/ppermute | solution.py:184
  242.9 0.1 collective-permute-start.6
  243.0 7.1 %fusion.12 = bf16[1,768,2048]{2,1,0:T(8,128)(2,1)} fusion(bf16[1024,768]{1,0:T(8,128)(2,1)S(1)} %copy-done.9, bf16[1024,2048]{1,0:T(8,128)(2,1)} %bitcast.9), kind=kOutput, calls=%fused_computation.21 | convolution fusion | flops 3222798336 | bytes 8912896 | tf_op jit(solution)/shard_map/dot_general | solution.py:202
  250.2 3.2 %collective-permute-done.6 = f32[1,2048]{1,0:T(1,128)S(1)} collective-permute-done((f32[1,2048]{1,0:T(1,128)S(1)}, f32[1,2048]{1,0:T(1,128)S(1)}, u32[]{:S(2)}, u32[]{:S(2)}) %collective-permute-start.6) | collective-permute-done | bytes 8224 | tf_op jit(solution)/shard_map/ppermute | solution.py:184
  253.4 2.5 collective-permute-start.7
  255.9 7.4 %fusion.10 = bf16[1,2048,768]{2,1,0:T(8,128)(2,1)} fusion(bf16[1024,768]{1,0:T(8,128)(2,1)S(1)} %copy-done.11, bf16[128,8,2048]{2,1,0:T(8,128)(2,1)} %all-to-all-done), kind=kOutput, calls=%fused_computation.19 | convolution fusion | flops 3222798336 | bytes 8912896 | tf_op jit(solution)/shard_map/dot_general | solution.py:202
  263.3 14.8 %collective-permute-start = (bf16[64,2048]{1,0:T(8,128)(2,1)S(1)}, bf16[64,2048]{1,0:T(8,128)(2,1)S(1)}, u32[]{:S(2)}, u32[]{:S(2)}) collective-permute-start(bf16[64,2048]{1,0:T(8,128)(2,1)S(1)} %copy-done.2), channel_id=1, source_target_pairs={{0,1},{1,2},{2,3},{3,0},{4,5},{5,6},{6,7},{7,4},{8,9},{9,10},{10,1... | collective-permute-start | bytes 786440 | tf_op jit(solution)/shard_map/ppermute | solution.py:170
  278.1 3.8 %collective-permute-start.8 = (f32[1,2048]{1,0:T(1,128)S(1)}, f32[1,2048]{1,0:T(1,128)S(1)}, u32[]{:S(2)}, u32[]{:S(2)}) collective-permute-start(f32[1,2048]{1,0:T(1,128)S(1)} %add.77), channel_id=1, source_target_pairs={{0,1},{1,0},{2,3},{3,2},{4,5},{5,4},{6,7},{7,6},{8,9},{9,8},{10,11... | collective-permute-start | bytes 24584 | tf_op jit(solution)/shard_map/ppermute | solution.py:184
  281.9 7.4 %fusion.11 = bf16[1,2048,768]{2,1,0:T(8,128)(2,1)} fusion(bf16[1024,768]{1,0:T(8,128)(2,1)S(1)} %copy-done.14, bf16[128,8,2048]{2,1,0:T(8,128)(2,1)} %all-to-all-done), kind=kOutput, calls=%fused_computation.20 | convolution fusion | flops 3222798336 | bytes 8912896 | tf_op jit(solution)/shard_map/dot_general | solution.py:202
  289.3 0.6 collective-permute-start.1
  289.9 1.5 collective-permute-start.2
  291.4 2.1 collective-permute-start.9
  293.5 1.1 broadcast_in_dim.12
  294.6 0.7 constant_dynamic-update-slice_fusion.3
  295.3 2.5 collective-permute-done.9
  297.9 0.6 add.79
  298.5 0.7 constant_dynamic-update-slice_fusion.2
  299.2 0.7 constant_dynamic-update-slice_fusion.1
  299.9 0.7 constant_dynamic-update-slice_fusion
  300.7 6.0 %combine.1 = (bf16[64,2048]{1,0:T(8,128)(2,1)}, f32[8,64]{1,0:T(8,128)}) custom-call(s32[1]{0:T(128)} %bitcast.quarter, s32[64,8]{1,0:T(8,128)} %copy.17.ids, bf16[64,1024]{1,0:T(8,128)(2,1)} %get-tuple-element.26.routes, bf16[192,1024]{1,0:T(8,128)(2,1)} %get-tuple-element.27.weights, bf16[1024,2048]{1,0:T(8,128)(2,1)} %bitcast.14.rows, ...), custom_call_target="tpu_custom_call" | custom-call | flops 1073741824 | bytes 4194304 | tf_op jit(solution)/shard_map/combine/pallas_call | solution.py:320
  (38 shorter events, 0.1 us)
Async XLA Ops:
  0.6 91.1 %copy-start = (bf16[1,768,2048]{2,1,0:T(8,128)(2,1)S(1)}, bf16[1,768,2048]{2,1,0:T(8,128)(2,1)}, u32[]{:S(2)}) copy-start(bf16[1,768,2048]{2,1,0:T(8,128)(2,1)} %param.15) | copy-start | bytes 9437188
  5.7 63.9 %all-to-all-start = ((bf16[128,8,2048]{2,1,0:T(8,128)(2,1)}), bf16[128,8,2048]{2,1,0:T(8,128)(2,1)}, u32[]{:S(2)}, u32[]{:S(2)}) async-start(bf16[128,8,2048]{2,1,0:T(8,128)(2,1)} %bitcast.59), calls=%async_computation | async-start | bytes 8388608 | tf_op jit(solution)/shard_map/all_to_all | solution.py:161
  69.6 58.1 %all-to-all-start.1 = ((bf16[128,8,2048]{2,1,0:T(8,128)(2,1)}), bf16[128,8,2048]{2,1,0:T(8,128)(2,1)}, u32[]{:S(2)}, u32[]{:S(2)}) async-start(bf16[128,8,2048]{2,1,0:T(8,128)(2,1)} %bitcast.58), calls=%async_computation.1 | async-start | bytes 8388608 | tf_op jit(solution)/shard_map/all_to_all | solution.py:161
  75.7 6.3 %copy-start.6 = (bf16[1,2048,768]{2,1,0:T(8,128)(2,1)S(1)}, bf16[1,2048,768]{2,1,0:T(8,128)(2,1)}, u32[]{:S(2)}) copy-start(bf16[1,2048,768]{2,1,0:T(8,128)(2,1)} %param.14) | copy-start | bytes 9437188
  82.0 8.6 %copy-start.12 = (f32[1024,768]{1,0:T(8,128)}, f32[1024,768]{1,0:T(8,128)S(1)}, u32[]{:S(2)}) copy-start(f32[1024,768]{1,0:T(8,128)S(1)} %fusion.8) | copy-start | bytes 9437188
  90.5 1.1 copy-start.8
  127.7 8.4 %copy-start.5 = (bf16[1,2048,768]{2,1,0:T(8,128)(2,1)S(1)}, bf16[1,2048,768]{2,1,0:T(8,128)(2,1)}, u32[]{:S(2)}) copy-start(bf16[1,2048,768]{2,1,0:T(8,128)(2,1)} %param.13) | copy-start | bytes 9437188
  136.1 3.5 %copy-start.10 = (bf16[1024,768]{1,0:T(8,128)(2,1)}, bf16[1024,768]{1,0:T(8,128)(2,1)S(1)}, u32[]{:S(2)}) copy-start(bf16[1024,768]{1,0:T(8,128)(2,1)S(1)} %get-tuple-element.40) | copy-start | bytes 4718596
  136.1 3.5 %copy-start.13 = (bf16[1024,768]{1,0:T(8,128)(2,1)}, bf16[1024,768]{1,0:T(8,128)(2,1)S(1)}, u32[]{:S(2)}) copy-start(bf16[1024,768]{1,0:T(8,128)(2,1)S(1)} %get-tuple-element.41) | copy-start | bytes 4718596
  136.1 3.5 %copy-start.7 = (bf16[1,2048,768]{2,1,0:T(8,128)(2,1)S(1)}, bf16[1,2048,768]{2,1,0:T(8,128)(2,1)}, u32[]{:S(2)}) copy-start(bf16[1,2048,768]{2,1,0:T(8,128)(2,1)} %param.14) | copy-start | bytes 9437188
  201.4 6.0 %copy-start.4 = (f32[64,8]{0,1:T(8,128)S(1)}, f32[64,8]{0,1:T(8,128)}, u32[]{:S(2)}) copy-start(f32[64,8]{0,1:T(8,128)} %param.11) | copy-start | bytes 6148
  201.4 6.7 %copy-start.3 = (s32[64,8]{0,1:T(8,128)S(1)}, s32[64,8]{0,1:T(8,128)}, u32[]{:S(2)}) copy-start(s32[64,8]{0,1:T(8,128)} %param.10) | copy-start | bytes 6148
  201.4 99.3 %all-to-all-start.3 = ((bf16[128,8,2048]{2,1,0:T(8,128)(2,1)}), bf16[128,8,2048]{2,1,0:T(8,128)(2,1)}, u32[]{:S(2)}, u32[]{:S(2)}) async-start(bf16[128,8,2048]{2,1,0:T(8,128)(2,1)} %bitcast.60), calls=%async_computation.3 | async-start | bytes 8388608 | tf_op jit(solution)/shard_map/all_to_all | solution.py:161
  207.3 35.7 %copy-start.9 = (bf16[1024,768]{1,0:T(8,128)(2,1)S(1)}, bf16[1024,768]{1,0:T(8,128)(2,1)}, u32[]{:S(2)}) copy-start(bf16[1024,768]{1,0:T(8,128)(2,1)} %copy-done.8) | copy-start | bytes 4718596
  215.6 1.4 collective-permute-start.3
  217.7 8.7 %collective-permute-start.4 = (f32[1,2048]{1,0:T(1,128)S(1)}, f32[1,2048]{1,0:T(1,128)S(1)}, u32[]{:S(2)}, u32[]{:S(2)}) collective-permute-start(f32[1,2048]{1,0:T(1,128)S(1)} %add.73), channel_id=1, source_target_pairs={{0,8},{4,12},{8,0},{12,4},{16,24},{20,28},{24,16},{28,20},{32,40},... | collective-permute-start | bytes 24584 | tf_op jit(solution)/shard_map/ppermute | solution.py:184
  226.5 16.4 %collective-permute-start.5 = (f32[1,2048]{1,0:T(1,128)S(1)}, f32[1,2048]{1,0:T(1,128)S(1)}, u32[]{:S(2)}, u32[]{:S(2)}) collective-permute-start(f32[1,2048]{1,0:T(1,128)S(1)} %add.74), channel_id=1, source_target_pairs={{0,16},{4,20},{8,24},{12,28},{16,0},{20,4},{24,8},{28,12},{32,48},... | collective-permute-start | bytes 24584 | tf_op jit(solution)/shard_map/ppermute | solution.py:184
  242.9 13.0 %copy-start.11 = (bf16[1024,768]{1,0:T(8,128)(2,1)S(1)}, bf16[1024,768]{1,0:T(8,128)(2,1)}, u32[]{:S(2)}) copy-start(bf16[1024,768]{1,0:T(8,128)(2,1)} %copy-done.10) | copy-start | bytes 4718596
  242.9 10.5 %collective-permute-start.6 = (f32[1,2048]{1,0:T(1,128)S(1)}, f32[1,2048]{1,0:T(1,128)S(1)}, u32[]{:S(2)}, u32[]{:S(2)}) collective-permute-start(f32[1,2048]{1,0:T(1,128)S(1)} %add.75), channel_id=1, source_target_pairs={{0,32},{4,36},{8,40},{12,44},{16,48},{20,52},{24,56},{28,60},{32,0... | collective-permute-start | bytes 24584 | tf_op jit(solution)/shard_map/ppermute | solution.py:184
  253.4 9.9 %copy-start.2 = (bf16[64,2048]{1,0:T(8,128)(2,1)S(1)}, bf16[64,2048]{1,0:T(8,128)(2,1)}, u32[]{:S(2)}) copy-start(bf16[64,2048]{1,0:T(8,128)(2,1)} %get-tuple-element.36) | copy-start | bytes 786436
  253.4 28.4 %copy-start.14 = (bf16[1024,768]{1,0:T(8,128)(2,1)S(1)}, bf16[1024,768]{1,0:T(8,128)(2,1)}, u32[]{:S(2)}) copy-start(bf16[1024,768]{1,0:T(8,128)(2,1)} %copy-done.13) | copy-start | bytes 4718596
  253.4 24.6 %collective-permute-start.7 = (f32[1,2048]{1,0:T(1,128)S(1)}, f32[1,2048]{1,0:T(1,128)S(1)}, u32[]{:S(2)}, u32[]{:S(2)}) collective-permute-start(f32[1,2048]{1,0:T(1,128)S(1)} %add.76), channel_id=1, source_target_pairs={{0,64},{4,68},{8,72},{12,76},{16,80},{20,84},{24,88},{28,92},{32,9... | collective-permute-start | bytes 24584 | tf_op jit(solution)/shard_map/ppermute | solution.py:184
  263.3 35.2 %collective-permute-start = (bf16[64,2048]{1,0:T(8,128)(2,1)S(1)}, bf16[64,2048]{1,0:T(8,128)(2,1)S(1)}, u32[]{:S(2)}, u32[]{:S(2)}) collective-permute-start(bf16[64,2048]{1,0:T(8,128)(2,1)S(1)} %copy-done.2), channel_id=1, source_target_pairs={{0,1},{1,2},{2,3},{3,0},{4,5},{5,6},{6,7},{7,4},{8,9},{9,10},{10,1... | collective-permute-start | bytes 786440 | tf_op jit(solution)/shard_map/ppermute | solution.py:170
  278.1 13.3 %collective-permute-start.8 = (f32[1,2048]{1,0:T(1,128)S(1)}, f32[1,2048]{1,0:T(1,128)S(1)}, u32[]{:S(2)}, u32[]{:S(2)}) collective-permute-start(f32[1,2048]{1,0:T(1,128)S(1)} %add.77), channel_id=1, source_target_pairs={{0,1},{1,0},{2,3},{3,2},{4,5},{5,4},{6,7},{7,6},{8,9},{9,8},{10,11... | collective-permute-start | bytes 24584 | tf_op jit(solution)/shard_map/ppermute | solution.py:184
  289.3 9.9 %collective-permute-start.1 = (bf16[64,2048]{1,0:T(8,128)(2,1)S(1)}, bf16[64,2048]{1,0:T(8,128)(2,1)S(1)}, u32[]{:S(2)}, u32[]{:S(2)}) collective-permute-start(bf16[64,2048]{1,0:T(8,128)(2,1)S(1)} %copy-done.2), channel_id=1, source_target_pairs={{0,3},{1,0},{2,1},{3,2},{4,7},{5,4},{6,5},{7,6},{8,11},{9,8},{10,9... | collective-permute-start | bytes 786440 | tf_op jit(solution)/shard_map/ppermute | solution.py:170
  289.9 10.0 %collective-permute-start.2 = (bf16[64,2048]{1,0:T(8,128)(2,1)S(1)}, bf16[64,2048]{1,0:T(8,128)(2,1)S(1)}, u32[]{:S(2)}, u32[]{:S(2)}) collective-permute-start(bf16[64,2048]{1,0:T(8,128)(2,1)S(1)} %copy-done.2), channel_id=1, source_target_pairs={{0,2},{1,3},{2,0},{3,1},{4,6},{5,7},{6,4},{7,5},{8,10},{9,11},{10,... | collective-permute-start | bytes 786440 | tf_op jit(solution)/shard_map/ppermute | solution.py:170
  291.4 6.5 %collective-permute-start.9 = (f32[1,2048]{1,0:T(1,128)S(1)}, f32[1,2048]{1,0:T(1,128)S(1)}, u32[]{:S(2)}, u32[]{:S(2)}) collective-permute-start(f32[1,2048]{1,0:T(1,128)S(1)} %add.78), channel_id=1, source_target_pairs={{0,2},{1,3},{2,0},{3,1},{4,6},{5,7},{6,4},{7,5},{8,10},{9,11},{10,... | collective-permute-start | bytes 24584 | tf_op jit(solution)/shard_map/ppermute | solution.py:184
  299.9 6.7 %copy-start.1 = (bf16[1,768,2048]{2,1,0:T(8,128)(2,1)S(1)}, bf16[1,768,2048]{2,1,0:T(8,128)(2,1)}, u32[]{:S(2)}) copy-start(bf16[1,768,2048]{2,1,0:T(8,128)(2,1)} %param.15) | copy-start | bytes 9437188

commit v2 on v1

--- a/solution.py
+++ b/solution.py
@@ -30,9 +30,11 @@
     return jnp.where(rank[:, None, :] == place, 1.0, 0.0)
 
 
-def pack_normed_kernel(quarter, ids_t, hidden, gain, buf, normed):
+def pack_kernel(quarter, ids_t, probs_t, hidden, gain, grad, buf, normed):
     step = pl.program_id(0)
-    rows, count, cap = buf.shape[0], buf.shape[0] // 8, 8
+    rows, cap = buf.shape[0], 8
+    count = rows // cap
+    width = hidden.shape[1]
 
     @pl.when(step == 0)
     def _():
@@ -40,13 +42,6 @@
         inverse = lax.rsqrt(jnp.mean(values * values, axis=-1, keepdims=True) + epsilon)
         normed[...] = (values * inverse * gain[...]).astype(BF16)
 
-    chosen = slot_rows(ids_t[...], step * count, count, cap).reshape(rows, -1).astype(BF16)
-    buf[...] = jnp.dot(chosen, normed[...], preferred_element_type=F32).astype(BF16)
-
-
-def pack_scaled_kernel(ids_t, probs_t, grad, buf):
-    step = pl.program_id(0)
-    rows, count, cap = buf.shape[0], buf.shape[0] // 8, 8
     ids = ids_t[...]
     top, tokens = ids.shape
     chosen = slot_rows(ids, step * count, count, cap)
@@ -55,10 +50,59 @@
     for k in range(top):
         prob = prob + jnp.where(ids[k : k + 1, :] == names, probs_t[k : k + 1, :], 0.0)
     weight = jnp.sum((chosen * prob[:, None, :]).reshape(rows, tokens), axis=1, keepdims=True)
-    picked = jnp.dot(
-        chosen.reshape(rows, tokens).astype(BF16), grad[...], preferred_element_type=F32
-    )
-    buf[...] = (picked * weight).astype(BF16)
+    chosen = chosen.reshape(rows, tokens).astype(BF16)
+    buf[:, :width] = jnp.dot(chosen, normed[...], preferred_element_type=F32).astype(BF16)
+    picked = jnp.dot(chosen, grad[...], preferred_element_type=F32)
+    buf[:, width:] = (picked * weight).astype(BF16)
+
+
+def expert_kernel(
+    inputs, cotan, gate_hbm, up_hbm, down_hbm, back, act, gate_pgrad, up_pgrad,
+    gate_w, up_w, down_w, sems,
+):
+    first = pl.program_id(0) == 0
+    copies = [
+        pltpu.make_async_copy(source, target, sems.at[n])
+        for n, (source, target) in enumerate(
+            ((gate_hbm, gate_w), (up_hbm, up_w), (down_hbm, down_w))
+        )
+    ]
+
+    @pl.when(first)
+    def _():
+        for copy in copies:
+            copy.start()
+        copies[0].wait()
+
+    gate_pre = jnp.dot(inputs[...], gate_w[...], preferred_element_type=F32)
+
+    @pl.when(first)
+    def _():
+        copies[1].wait()
+
+    up_pre = jnp.dot(inputs[...], up_w[...], preferred_element_type=F32)
+    sigma = jax.nn.sigmoid(gate_pre)
+    silu_vals = gate_pre * sigma
+    act[...] = (silu_vals * up_pre).astype(BF16)
+
+    @pl.when(first)
+    def _():
+        copies[2].wait()
+
+    act_grad = lax.dot_general(
+        cotan[...], down_w[...], (((1,), (1,)), ((), ())), preferred_element_type=F32
+    )
+    gate_g = (act_grad * up_pre * sigma * (1.0 + gate_pre * (1.0 - sigma))).astype(BF16)
+    up_g = (act_grad * silu_vals).astype(BF16)
+    gate_pgrad[...] = gate_g
+    up_pgrad[...] = up_g
+    total = lax.dot_general(
+        gate_g, gate_w[...], (((1,), (1,)), ((), ())), preferred_element_type=F32
+    )
+    total += lax.dot_general(
+        up_g, up_w[...], (((1,), (1,)), ((), ())), preferred_element_type=F32
+    )
+    back[...] = total.astype(BF16)
 
 
 def routes_kernel(ids, probs, routes, weights):
@@ -177,13 +221,20 @@
 
 
 def sum_all(value):
-    for axis in AXES:
+    def exchange_sum(value, axis, shifts, target):
         size = lax.axis_size(axis)
-        step = 1
-        while step < size:
-            value = value + lax.ppermute(value, axis, [(i, i ^ step) for i in range(size)])
-            step *= 2
-    return value
+        others = [
+            lax.ppermute(value, axis, [(i, target(i, shift)) for i in range(size)])
+            for shift in shifts
+        ]
+        for other in others:
+            value = value + other
+        return value
+
+    value = exchange_sum(value, "dp", (1,), lambda i, s: i ^ s)
+    value = exchange_sum(value, "tensor", (1, 2, 3), lambda i, s: i ^ s)
+    value = exchange_sum(value, "dp", (2, 4, 6), lambda i, s: i ^ s)
+    return exchange_sum(value, "dp", (8, 16, 24), lambda i, s: i ^ s)
 
 
 def after(value, *earlier):
@@ -219,37 +270,28 @@
     def whole(*shape):
         return pl.BlockSpec(shape, lambda *_: (0,) * len(shape))
 
-    normed_buf = pl.pallas_call(
-        pack_normed_kernel,
+    pack_steps = 8
+    buf = pl.pallas_call(
+        pack_kernel,
         grid_spec=pltpu.PrefetchScalarGridSpec(
             num_scalar_prefetch=1,
-            grid=(steps,),
+            grid=(pack_steps,),
             in_specs=[
+                whole(top, own),
                 whole(top, own),
                 pl.BlockSpec((own, width), lambda i, q: (q[0], 0)),
                 whole(1, width),
+                whole(own, width),
             ],
-            out_specs=pl.BlockSpec((slots // steps, width), lambda i, q: (i, 0)),
+            out_specs=pl.BlockSpec((slots // pack_steps, 2 * width), lambda i, q: (i, 0)),
             scratch_shapes=[pltpu.VMEM((own, width), BF16)],
         ),
-        out_shape=jax.ShapeDtypeStruct((slots, width), BF16),
+        out_shape=jax.ShapeDtypeStruct((slots, 2 * width), BF16),
         compiler_params=params(),
-        cost_estimate=cost(2 * slots * own * width, 2 * slots * width),
-        name="pack_normed",
-    )(quarter, ids_t, hidden, gain)
-    inputs = exchange(normed_buf)
-
-    scaled_buf = pl.pallas_call(
-        pack_scaled_kernel,
-        grid=(steps,),
-        in_specs=[whole(top, own), whole(top, own), whole(own, width)],
-        out_specs=pl.BlockSpec((slots // steps, width), lambda i: (i, 0)),
-        out_shape=jax.ShapeDtypeStruct((slots, width), BF16),
-        compiler_params=params(),
-        cost_estimate=cost(2 * slots * own * width, 2 * slots * width),
-        name="pack_scaled",
-    )(after(ids_t, normed_buf), probs_t, out_grad)
-    cotan = exchange(after(scaled_buf, inputs))
+        cost_estimate=cost(4 * slots * own * width, 4 * slots * width),
+        name="pack",
+    )(quarter, ids_t, probs_t, hidden, gain, out_grad)
+    received = exchange(buf)
 
     routes, weights = pl.pallas_call(
         routes_kernel,
@@ -260,34 +302,55 @@
         compiler_params=params(),
         cost_estimate=cost(2 * 4 * own * devices * slots, 8 * own * slots),
         name="routes",
-    )(after(expert_ids, normed_buf), gate_probs)
+    )(after(expert_ids, buf), gate_probs)
 
     gate_w, up_w, down_w = gate_weight[0], up_weight[0], down_weight[0]
-    gate_pre = dot(inputs, gate_w, ((1,), (0,)))
-    up_pre = dot(inputs, up_w, ((1,), (0,)))
-    sigma = jax.nn.sigmoid(gate_pre)
-    silu_vals = gate_pre * sigma
-    act = (silu_vals * up_pre).astype(BF16)
+    hidden_units = gate_w.shape[1]
+    block = slots // steps
+
+    def row_block(columns, place=0):
+        return pl.BlockSpec((block, columns), lambda i: (i, place))
+
+    hbm = pl.BlockSpec(memory_space=pl.ANY)
+    back, act, gate_pgrad, up_pgrad = pl.pallas_call(
+        expert_kernel,
+        grid=(steps,),
+        in_specs=[row_block(width), row_block(width, 1), hbm, hbm, hbm],
+        out_specs=[
+            row_block(width),
+            row_block(hidden_units),
+            row_block(hidden_units),
+            row_block(hidden_units),
+        ],
+        out_shape=[
+            jax.ShapeDtypeStruct((slots, width), BF16),
+            jax.ShapeDtypeStruct((slots, hidden_units), BF16),
+            jax.ShapeDtypeStruct((slots, hidden_units), BF16),
+            jax.ShapeDtypeStruct((slots, hidden_units), BF16),
+        ],
+        scratch_shapes=[
+            pltpu.VMEM(gate_w.shape, BF16),
+            pltpu.VMEM(up_w.shape, BF16),
+            pltpu.VMEM(down_w.shape, BF16),
+            pltpu.SemaphoreType.DMA((3,)),
+        ],
+        compiler_params=params(),
+        cost_estimate=cost(10 * slots * width * hidden_units, 12 * slots * width),
+        name="expert",
+    )(received, received, gate_w, up_w, down_w)
+    back_rows = exchange(back)
+
     result = dot(act, down_w, ((1,), (0,))).astype(BF16)
-    gate_pre, up_pre, act, cotan, result = lax.optimization_barrier(
-        (gate_pre, up_pre, act, cotan, result)
-    )
-    sigma = jax.nn.sigmoid(gate_pre)
-    silu_vals = gate_pre * sigma
-    act_grad = dot(cotan, down_w, ((1,), (1,)))
-    gate_pgrad = (act_grad * up_pre * sigma * (1.0 + gate_pre * (1.0 - sigma))).astype(BF16)
-    up_pgrad = (act_grad * silu_vals).astype(BF16)
-    back = dot(gate_pgrad, gate_w, ((1,), (1,))) + dot(up_pgrad, up_w, ((1,), (1,)))
-    back = back.astype(BF16)
-    back_rows = exchange(back)
-    returned = exchange(after(result, back_rows))
-
-    gate_pgrad, up_pgrad, act_late = lax.optimization_barrier(
-        (gate_pgrad, up_pgrad, act, back)
-    )[:3]
+    inputs, cotan = received[:, :width], received[:, width:]
     gate_wgrad = dot(inputs, gate_pgrad, ((0,), (0,))).astype(BF16)
     up_wgrad = dot(inputs, up_pgrad, ((0,), (0,))).astype(BF16)
-    down_grad = dot(act_late, cotan, ((0,), (0,))).astype(BF16)
+    down_grad = dot(act, cotan, ((0,), (0,))).astype(BF16)
+    result, gate_wgrad, up_wgrad, down_grad, back_rows, routes, weights = (
+        lax.optimization_barrier(
+            (result, gate_wgrad, up_wgrad, down_grad, back_rows, routes, weights)
+        )
+    )
+    returned = exchange(result)
 
     own_grad, gain_part = pl.pallas_call(
         norm_grad_kernel,
@@ -315,7 +378,7 @@
     input_grad = gather_group(own_grad)
     gain_grad = sum_all(gain_part)[0]
 
-    parts = 2
+    parts = 4
     columns = width // parts
     layer_out, gate_grad_t = pl.pallas_call(
         combine_kernel,

time: 309 us -> 290 us (0.939)
  blocking collectives: 57.8 us -> 109 us
  waiting for transfers between devices: 109 us -> 64.4 us
  matrix products: 57.5 us -> 26.1 us
  Pallas kernels: 22.6 us -> 50.4 us
  starting transfers between devices: 50.2 us -> 33.5 us
  local copies, waits for them, and re-layouts: 7.27 us -> 3.28 us
    all_to_all x3 -> x2, waiting for transfers between devices: 78.6 us -> 22.3 us  [exchange(): return lax.all_to_all(block, AXES, split_axis=0, concat_axis=0, tiled=True)]
    all_to_all x1, blocking collectives: 57.8 us -> 109 us  [exchange(): return lax.all_to_all(block, AXES, split_axis=0, concat_axis=0, tiled=True)]
    dot_general x9 -> x4, matrix products: 57.5 us -> 26.1 us  [dot(): return lax.dot_general(a, b, (dims, ((), ())), preferred_element_type=F32)]
    pallas_call x2, Pallas kernels: 9.73 us -> 36.8 us  [the longest x1 28.7 us: per_device(): pl.pallas_call(expert_kernel, grid=(steps,), in_specs=[row_block(width),...]
    ppermute x3, starting transfers between devices: 16.8 us -> 2.67 us  [gather_group(): lax.ppermute(block, 'tensor', [(i, (i + step) % size) for i in range(size)])]
    all_to_all x3 -> x2, starting transfers between devices: 23.7 us -> 12.7 us  [exchange(): return lax.all_to_all(block, AXES, split_axis=0, concat_axis=0, tiled=True)]
    ppermute x7 -> x10, starting transfers between devices: 9.68 us -> 18.2 us  [exchange_sum(): lax.ppermute(value, axis, [(i, target(i, shift)) for i in range(size)])]
    ppermute x7 -> x10, waiting for transfers between devices: 30.4 us -> 37.4 us  [exchange_sum(): lax.ppermute(value, axis, [(i, target(i, shift)) for i in range(size)])]
  transfers between devices with their start and end apart: 13 -> 15, of which waited for: 7 -> 9; matrix products, arithmetic and copies ran while one was open for 16% -> 11% of each run, Pallas kernels for 4% -> 2%
where the time goes in v2:
time: 290 us; the launch traced here: 289 us
  blocking collectives  109 us (38%)
  waiting for transfers between devices  64.4 us (22%)
  Pallas kernels  50.4 us (17%)
  starting transfers between devices  33.5 us (12%)
  matrix products  26.1 us (9%)
  local copies, waits for them, and re-layouts  3.28 us (1%)
    all_to_all x1, blocking collectives, exchange(): return lax.all_to_all(block, AXES, split_axis=0, concat_axis=0, tiled=True)  109 us
    ppermute x10, waiting for transfers between devices, exchange_sum(): lax.ppermute(value, axis, [(i, target(i, shift)) for i in range(size)])  37.4 us
    pallas_call x1, Pallas kernels, per_device(): pl.pallas_call(expert_kernel, grid=(steps,), in_specs=[row_block(width),...  28.7 us
    dot_general x4, matrix products, dot(): return lax.dot_general(a, b, (dims, ((), ())), preferred_element_type=F32)  26.1 us
    all_to_all x2, waiting for transfers between devices, exchange(): return lax.all_to_all(block, AXES, split_axis=0, concat_axis=0, tiled=True)  22.3 us
    ppermute x10, starting transfers between devices, exchange_sum(): lax.ppermute(value, axis, [(i, target(i, shift)) for i in range(size)])  18.2 us
    all_to_all x2, starting transfers between devices, exchange(): return lax.all_to_all(block, AXES, split_axis=0, concat_axis=0, tiled=True)  12.7 us
    pallas_call x1, Pallas kernels, per_device(): pl.pallas_call(pack_kernel, grid_spec=pltpu.PrefetchScalarGridSpec(num_sc...  8.03 us
  transfers between devices with their start and end apart: 15, of which 9 were waited for; matrix products, arithmetic and copies ran while one was open for 11% of the time, Pallas kernels for 2%

profile of v2, /device:TPU:0, one launch (start us, length us, event | category | flops | bytes accessed | tf_op | source)
XLA Modules:
  0.0 289.0 jit_solution(15803199093113876635)
XLA Ops:
  0.6 8.0 %pack.1 = bf16[1024,4096]{1,0:T(8,128)(2,1)} custom-call(s32[1]{0:T(128)} %bitcast.quarter, s32[8,64]{1,0:T(8,128)} %bitcast.34, f32[8,64]{1,0:T(8,128)} %bitcast.37, bf16[256,2048]{1,0:T(8,128)(2,1)} %hidden.5, f32[1,2048]{1,0:T(1,128)} %bitcast.35, bf16[64,2048]{1,0:T(8,128)(2,1)} %grad.5), custom_call_target="tpu_custom_call" | custom-call | flops 536870912 | bytes 8388608 | tf_op jit(solution)/shard_map/pack/pallas_call | solution.py:274
  8.7 108.9 %all_to_all.34 = bf16[128,8,4096]{2,1,0:T(8,128)(2,1)} all-to-all(bf16[128,8,4096]{2,1,0:T(8,128)(2,1)} %bitcast.24), channel_id=1, replica_groups=mesh['dp'=32,'tensor'=4] {'dp','tensor'}, dimensions={0} | all-to-all | bytes 16777216 | tf_op jit(solution)/shard_map/all_to_all | solution.py:205
  117.6 28.7 %expert.1 = (bf16[1024,2048]{1,0:T(8,128)(2,1)}, bf16[1024,768]{1,0:T(8,128)(2,1)}, bf16[1024,768]{1,0:T(8,128)(2,1)}, bf16[1024,768]{1,0:T(8,128)(2,1)}) custom-call(bf16[1024,4096]{1,0:T(8,128)(2,1)} %bitcast.25, bf16[1024,4096]{1,0:T(8,128)(2,1)} %bitcast.26, bf16[2048,768]{1,0:T(8,128)(2,1)} %bitcast.39, bf16[2048,768]{1,0:T(8,128)(2,1)} %bitcast.40, ...), custom_call_target="tpu_custom_call" | custom-call | flops 16106127360 | bytes 25165824 | tf_op jit(solution)/shard_map/expert/pallas_call | solution.py:315
  146.3 0.0 copy-start.2
  146.3 0.0 copy-start.1
  146.4 0.0 copy-start.3
  146.4 6.8 %all-to-all-start.1 = ((bf16[128,8,2048]{2,1,0:T(8,128)(2,1)}), bf16[128,8,2048]{2,1,0:T(8,128)(2,1)}, u32[]{:S(2)}, u32[]{:S(2)}) async-start(bf16[128,8,2048]{2,1,0:T(8,128)(2,1)} %bitcast.33), calls=%async_computation.1 | async-start | bytes 8388608 | tf_op jit(solution)/shard_map/all_to_all | solution.py:205
  153.2 0.7 copy.16.probs
  153.9 0.7 copy.15.ids
  154.6 2.1 routes.1
  156.8 6.5 %convolution_convert_fusion = bf16[1024,2048]{1,0:T(8,128)(2,1)} fusion(bf16[1024,768]{1,0:T(8,128)(2,1)} %get-tuple-element.25, bf16[1,768,2048]{2,1,0:T(8,128)(2,1)S(1)} %copy-done.3), kind=kOutput, calls=%fused_computation.2 | convolution fusion | flops 3223322624 | bytes 8912896 | tf_op jit(solution)/shard_map/dot_general | solution.py:253
  163.3 7.2 %fusion.12 = bf16[768,2048]{1,0:T(8,128)(2,1)} fusion(bf16[1024,768]{1,0:T(8,128)(2,1)S(1)} %copy-done.4, bf16[1024,4096]{1,0:T(8,128)(2,1)} %bitcast.27), kind=kOutput, calls=%fused_computation.9 | convolution fusion | flops 3222798336 | bytes 8912896 | tf_op jit(solution)/shard_map/dot_general | solution.py:253
  170.5 7.5 %fusion.6 = bf16[2048,768]{1,0:T(8,128)(2,1)} fusion(bf16[1024,768]{1,0:T(8,128)(2,1)S(1)} %copy-done.6, bf16[1024,4096]{1,0:T(8,128)(2,1)} %bitcast.28), kind=kOutput, calls=%fused_computation.7 | convolution fusion | flops 3222798336 | bytes 8912896 | tf_op jit(solution)/shard_map/dot_general | solution.py:253
  178.0 4.9 %fusion.9 = bf16[2048,768]{1,0:T(8,128)(2,1)} fusion(bf16[1024,768]{1,0:T(8,128)(2,1)S(1)} %copy-done.5, bf16[1024,4096]{1,0:T(8,128)(2,1)S(1)} %bitcast.31), kind=kOutput, calls=%fused_computation.8 | convolution fusion | flops 3222798336 | bytes 8912896 | tf_op jit(solution)/shard_map/dot_general | solution.py:253
  182.9 22.3 %all-to-all-done.1 = bf16[128,8,2048]{2,1,0:T(8,128)(2,1)} async-done(((bf16[128,8,2048]{2,1,0:T(8,128)(2,1)}), bf16[128,8,2048]{2,1,0:T(8,128)(2,1)}, u32[]{:S(2)}, u32[]{:S(2)}) %all-to-all-start.1) | async-done | bytes 4194336 | tf_op jit(solution)/shard_map/all_to_all | solution.py:205
  205.2 5.8 %all-to-all-start.2 = ((bf16[128,8,2048]{2,1,0:T(8,128)(2,1)}), bf16[128,8,2048]{2,1,0:T(8,128)(2,1)}, u32[]{:S(2)}, u32[]{:S(2)}) async-start(bf16[128,8,2048]{2,1,0:T(8,128)(2,1)} %bitcast.32), calls=%async_computation.2 | async-start | bytes 8388608 | tf_op jit(solution)/shard_map/all_to_all | solution.py:205
  211.1 4.8 %norm_grad.1 = (bf16[64,2048]{1,0:T(8,128)(2,1)}, f32[1,2048]{1,0:T(1,128)}) custom-call(s32[1]{0:T(128)} %bitcast.quarter, bf16[64,1024]{1,0:T(8,128)(2,1)} %get-tuple-element.32.routes, bf16[1024,2048]{1,0:T(8,128)(2,1)} %bitcast.10.rows, bf16[256,2048]{1,0:T(8,128)(2,1)} %hidden.5, f32[1,2048]{1,0:T(1,128)} %bitcast.36, bf16[64,2048]{1,0:T(8,128)(2,1)} %grad.5), custom_call_target="tpu_custom_call" | custom-call | flops 268435456 | bytes 4194304 | tf_op jit(solution)/shard_map/norm_grad/pallas_call | solution.py:355
  215.9 0.0 collective-permute-start.3
  215.9 1.4 collective-permute-done.3
  217.3 0.7 add.66
  218.0 2.2 collective-permute-start.6
  220.2 0.8 collective-permute-start.5
  221.0 1.1 collective-permute-start.4
  222.2 27.1 %collective-permute-done.6 = f32[1,2048]{1,0:T(1,128)S(1)} collective-permute-done((f32[1,2048]{1,0:T(1,128)S(1)}, f32[1,2048]{1,0:T(1,128)S(1)}, u32[]{:S(2)}, u32[]{:S(2)}) %collective-permute-start.6) | collective-permute-done | bytes 8224 | tf_op jit(solution)/shard_map/ppermute | solution.py:227
  249.3 2.6 collective-permute-done.5
  252.0 3.4 %collective-permute-done.4 = f32[1,2048]{1,0:T(1,128)S(1)} collective-permute-done((f32[1,2048]{1,0:T(1,128)S(1)}, f32[1,2048]{1,0:T(1,128)S(1)}, u32[]{:S(2)}, u32[]{:S(2)}) %collective-permute-start.4) | collective-permute-done | bytes 8224 | tf_op jit(solution)/shard_map/ppermute | solution.py:227
  255.4 4.9 %collective-permute-start.9 = (f32[1,2048]{1,0:T(1,128)S(1)}, f32[1,2048]{1,0:T(1,128)S(1)}, u32[]{:S(2)}, u32[]{:S(2)}) collective-permute-start(f32[1,2048]{1,0:T(1,128)S(1)} %add_add_fusion.2), channel_id=1, source_target_pairs={{0,24},{4,28},{8,16},{12,20},{16,8},{20,12},{24,0},{28,4},{32,56},... | collective-permute-start | bytes 24584 | tf_op jit(solution)/shard_map/ppermute | solution.py:227
  260.3 2.6 collective-permute-start.8
  262.9 0.0 collective-permute-start.7
  262.9 0.7 copy.17.ids
  263.6 0.2 collective-permute-start.2
  263.8 2.4 collective-permute-start.1
  266.2 0.0 collective-permute-done.9
  266.2 0.0 collective-permute-done.8
  266.2 0.4 collective-permute-done.7
  266.6 4.5 %collective-permute-start.12 = (f32[1,2048]{1,0:T(1,128)S(1)}, f32[1,2048]{1,0:T(1,128)S(1)}, u32[]{:S(2)}, u32[]{:S(2)}) collective-permute-start(f32[1,2048]{1,0:T(1,128)S(1)} %add_add_fusion.1), channel_id=1, source_target_pairs={{0,96},{4,100},{8,104},{12,108},{16,112},{20,116},{24,120},{28,124... | collective-permute-start | bytes 24584 | tf_op jit(solution)/shard_map/ppermute | solution.py:227
  271.1 1.9 collective-permute-start.11
  273.0 0.0 collective-permute-start.10
  273.1 0.1 broadcast_in_dim.12
  273.2 1.0 constant_dynamic-update-slice_fusion.3
  274.1 0.0 collective-permute-done.12
  274.2 0.1 collective-permute-start
  274.2 2.0 collective-permute-done.11
  276.3 0.4 collective-permute-done.10
  276.7 0.6 add_add_fusion
  277.3 4.7 %collective-permute-done = bf16[64,2048]{1,0:T(8,128)(2,1)S(1)} collective-permute-done((bf16[64,2048]{1,0:T(8,128)(2,1)}, bf16[64,2048]{1,0:T(8,128)(2,1)S(1)}, u32[]{:S(2)}, u32[]{:S(2)}) %collective-permute-start) | collective-permute-done | bytes 262176 | tf_op jit(solution)/shard_map/ppermute | solution.py:214
  282.1 0.0 copy-start
  282.2 6.7 %combine.1 = (bf16[64,2048]{1,0:T(8,128)(2,1)}, f32[8,64]{1,0:T(8,128)}) custom-call(s32[1]{0:T(128)} %bitcast.quarter, s32[64,8]{1,0:T(8,128)} %copy.17.ids, bf16[64,1024]{1,0:T(8,128)(2,1)} %get-tuple-element.32.routes, bf16[192,1024]{1,0:T(8,128)(2,1)} %get-tuple-element.33.weights, bf16[1024,2048]{1,0:T(8,128)(2,1)} %bitcast.12.rows, ...), custom_call_target="tpu_custom_call" | custom-call | flops 1073741824 | bytes 4194304 | tf_op jit(solution)/shard_map/combine/pallas_call | solution.py:383
  (23 shorter events, 0.1 us)
Async XLA Ops:
  146.3 6.9 %copy-start.2 = (f32[64,8]{0,1:T(8,128)S(1)}, f32[64,8]{0,1:T(8,128)}, u32[]{:S(2)}) copy-start(f32[64,8]{0,1:T(8,128)} %param.11) | copy-start | bytes 6148
  146.3 7.6 %copy-start.1 = (s32[64,8]{0,1:T(8,128)S(1)}, s32[64,8]{0,1:T(8,128)}, u32[]{:S(2)}) copy-start(s32[64,8]{0,1:T(8,128)} %param.10) | copy-start | bytes 6148
  146.4 10.4 %copy-start.3 = (bf16[1,768,2048]{2,1,0:T(8,128)(2,1)S(1)}, bf16[1,768,2048]{2,1,0:T(8,128)(2,1)}, u32[]{:S(2)}) copy-start(bf16[1,768,2048]{2,1,0:T(8,128)(2,1)} %param.15) | copy-start | bytes 9437188
  146.4 58.9 %all-to-all-start.1 = ((bf16[128,8,2048]{2,1,0:T(8,128)(2,1)}), bf16[128,8,2048]{2,1,0:T(8,128)(2,1)}, u32[]{:S(2)}, u32[]{:S(2)}) async-start(bf16[128,8,2048]{2,1,0:T(8,128)(2,1)} %bitcast.33), calls=%async_computation.1 | async-start | bytes 8388608 | tf_op jit(solution)/shard_map/all_to_all | solution.py:205
  156.8 6.5 %copy-start.4 = (bf16[1024,768]{1,0:T(8,128)(2,1)S(1)}, bf16[1024,768]{1,0:T(8,128)(2,1)}, u32[]{:S(2)}) copy-start(bf16[1024,768]{1,0:T(8,128)(2,1)} %get-tuple-element.25) | copy-start | bytes 4718596
  163.3 7.2 %copy-start.6 = (bf16[1024,768]{1,0:T(8,128)(2,1)S(1)}, bf16[1024,768]{1,0:T(8,128)(2,1)}, u32[]{:S(2)}) copy-start(bf16[1024,768]{1,0:T(8,128)(2,1)} %get-tuple-element.26) | copy-start | bytes 4718596
  163.3 14.7 %slice-start = ((s8[8388608]{0:T(1024)(128)(4,1)}), s8[4194304]{0:T(1024)(128)(4,1)S(1)}, s32[]{:S(2)}) async-start(s8[8388608]{0:T(1024)(128)(4,1)} %bitcast.29), calls=%async_computation.3 | async-start | bytes 8388608
  170.5 7.5 %slice-start.1 = ((s8[8388608]{0:T(1024)(128)(4,1)}), s8[4194304]{0:T(1024)(128)(4,1)S(1)}, s32[]{:S(2)}) async-start(s8[8388608]{0:T(1024)(128)(4,1)} %bitcast.29), calls=%async_computation.4 | async-start | bytes 8388608
  170.5 7.5 %copy-start.5 = (bf16[1024,768]{1,0:T(8,128)(2,1)S(1)}, bf16[1024,768]{1,0:T(8,128)(2,1)}, u32[]{:S(2)}) copy-start(bf16[1024,768]{1,0:T(8,128)(2,1)} %get-tuple-element.27) | copy-start | bytes 4718596
  205.2 76.9 %all-to-all-start.2 = ((bf16[128,8,2048]{2,1,0:T(8,128)(2,1)}), bf16[128,8,2048]{2,1,0:T(8,128)(2,1)}, u32[]{:S(2)}, u32[]{:S(2)}) async-start(bf16[128,8,2048]{2,1,0:T(8,128)(2,1)} %bitcast.32), calls=%async_computation.2 | async-start | bytes 8388608 | tf_op jit(solution)/shard_map/all_to_all | solution.py:205
  215.9 1.4 collective-permute-start.3
  218.0 31.3 %collective-permute-start.6 = (f32[1,2048]{1,0:T(1,128)S(1)}, f32[1,2048]{1,0:T(1,128)S(1)}, u32[]{:S(2)}, u32[]{:S(2)}) collective-permute-start(f32[1,2048]{1,0:T(1,128)S(1)} %add.66), channel_id=1, source_target_pairs={{0,3},{1,2},{2,1},{3,0},{4,7},{5,6},{6,5},{7,4},{8,11},{9,10},{10,... | collective-permute-start | bytes 24584 | tf_op jit(solution)/shard_map/ppermute | solution.py:227
  220.2 31.7 %collective-permute-start.5 = (f32[1,2048]{1,0:T(1,128)S(1)}, f32[1,2048]{1,0:T(1,128)S(1)}, u32[]{:S(2)}, u32[]{:S(2)}) collective-permute-start(f32[1,2048]{1,0:T(1,128)S(1)} %add.66), channel_id=1, source_target_pairs={{0,2},{1,3},{2,0},{3,1},{4,6},{5,7},{6,4},{7,5},{8,10},{9,11},{10,... | collective-permute-start | bytes 24584 | tf_op jit(solution)/shard_map/ppermute | solution.py:227
  221.0 34.3 %collective-permute-start.4 = (f32[1,2048]{1,0:T(1,128)S(1)}, f32[1,2048]{1,0:T(1,128)S(1)}, u32[]{:S(2)}, u32[]{:S(2)}) collective-permute-start(f32[1,2048]{1,0:T(1,128)S(1)} %add.66), channel_id=1, source_target_pairs={{0,1},{1,0},{2,3},{3,2},{4,5},{5,4},{6,7},{7,6},{8,9},{9,8},{10,11... | collective-permute-start | bytes 24584 | tf_op jit(solution)/shard_map/ppermute | solution.py:227
  255.4 10.8 %collective-permute-start.9 = (f32[1,2048]{1,0:T(1,128)S(1)}, f32[1,2048]{1,0:T(1,128)S(1)}, u32[]{:S(2)}, u32[]{:S(2)}) collective-permute-start(f32[1,2048]{1,0:T(1,128)S(1)} %add_add_fusion.2), channel_id=1, source_target_pairs={{0,24},{4,28},{8,16},{12,20},{16,8},{20,12},{24,0},{28,4},{32,56},... | collective-permute-start | bytes 24584 | tf_op jit(solution)/shard_map/ppermute | solution.py:227
  260.3 5.9 %collective-permute-start.8 = (f32[1,2048]{1,0:T(1,128)S(1)}, f32[1,2048]{1,0:T(1,128)S(1)}, u32[]{:S(2)}, u32[]{:S(2)}) collective-permute-start(f32[1,2048]{1,0:T(1,128)S(1)} %add_add_fusion.2), channel_id=1, source_target_pairs={{0,16},{4,20},{8,24},{12,28},{16,0},{20,4},{24,8},{28,12},{32,48},... | collective-permute-start | bytes 24584 | tf_op jit(solution)/shard_map/ppermute | solution.py:227
  262.9 3.7 %collective-permute-start.7 = (f32[1,2048]{1,0:T(1,128)S(1)}, f32[1,2048]{1,0:T(1,128)S(1)}, u32[]{:S(2)}, u32[]{:S(2)}) collective-permute-start(f32[1,2048]{1,0:T(1,128)S(1)} %add_add_fusion.2), channel_id=1, source_target_pairs={{0,8},{4,12},{8,0},{12,4},{16,24},{20,28},{24,16},{28,20},{32,40},... | collective-permute-start | bytes 24584 | tf_op jit(solution)/shard_map/ppermute | solution.py:227
  263.6 18.5 %collective-permute-start.2 = (bf16[64,2048]{1,0:T(8,128)(2,1)}, bf16[64,2048]{1,0:T(8,128)(2,1)S(1)}, u32[]{:S(2)}, u32[]{:S(2)}) collective-permute-start(bf16[64,2048]{1,0:T(8,128)(2,1)} %get-tuple-element.37), channel_id=1, source_target_pairs={{0,2},{1,3},{2,0},{3,1},{4,6},{5,7},{6,4},{7,5},{8,10},{9,11},{10,... | collective-permute-start | bytes 786440 | tf_op jit(solution)/shard_map/ppermute | solution.py:214
  263.8 18.2 %collective-permute-start.1 = (bf16[64,2048]{1,0:T(8,128)(2,1)}, bf16[64,2048]{1,0:T(8,128)(2,1)S(1)}, u32[]{:S(2)}, u32[]{:S(2)}) collective-permute-start(bf16[64,2048]{1,0:T(8,128)(2,1)} %get-tuple-element.37), channel_id=1, source_target_pairs={{0,3},{1,0},{2,1},{3,2},{4,7},{5,4},{6,5},{7,6},{8,11},{9,8},{10,9... | collective-permute-start | bytes 786440 | tf_op jit(solution)/shard_map/ppermute | solution.py:214
  266.6 7.6 %collective-permute-start.12 = (f32[1,2048]{1,0:T(1,128)S(1)}, f32[1,2048]{1,0:T(1,128)S(1)}, u32[]{:S(2)}, u32[]{:S(2)}) collective-permute-start(f32[1,2048]{1,0:T(1,128)S(1)} %add_add_fusion.1), channel_id=1, source_target_pairs={{0,96},{4,100},{8,104},{12,108},{16,112},{20,116},{24,120},{28,124... | collective-permute-start | bytes 24584 | tf_op jit(solution)/shard_map/ppermute | solution.py:227
  271.1 5.2 %collective-permute-start.11 = (f32[1,2048]{1,0:T(1,128)S(1)}, f32[1,2048]{1,0:T(1,128)S(1)}, u32[]{:S(2)}, u32[]{:S(2)}) collective-permute-start(f32[1,2048]{1,0:T(1,128)S(1)} %add_add_fusion.1), channel_id=1, source_target_pairs={{0,64},{4,68},{8,72},{12,76},{16,80},{20,84},{24,88},{28,92},{32,9... | collective-permute-start | bytes 24584 | tf_op jit(solution)/shard_map/ppermute | solution.py:227
  273.0 3.7 %collective-permute-start.10 = (f32[1,2048]{1,0:T(1,128)S(1)}, f32[1,2048]{1,0:T(1,128)S(1)}, u32[]{:S(2)}, u32[]{:S(2)}) collective-permute-start(f32[1,2048]{1,0:T(1,128)S(1)} %add_add_fusion.1), channel_id=1, source_target_pairs={{0,32},{4,36},{8,40},{12,44},{16,48},{20,52},{24,56},{28,60},{32,0... | collective-permute-start | bytes 24584 | tf_op jit(solution)/shard_map/ppermute | solution.py:227
  274.2 7.9 %collective-permute-start = (bf16[64,2048]{1,0:T(8,128)(2,1)}, bf16[64,2048]{1,0:T(8,128)(2,1)S(1)}, u32[]{:S(2)}, u32[]{:S(2)}) collective-permute-start(bf16[64,2048]{1,0:T(8,128)(2,1)} %get-tuple-element.37), channel_id=1, source_target_pairs={{0,1},{1,2},{2,3},{3,0},{4,5},{5,6},{6,7},{7,4},{8,9},{9,10},{10,1... | collective-permute-start | bytes 786440 | tf_op jit(solution)/shard_map/ppermute | solution.py:214
  282.1 6.7 %copy-start = (bf16[256,2048]{1,0:T(8,128)(2,1)}, bf16[256,2048]{1,0:T(8,128)(2,1)S(1)}, u32[]{:S(2)}) copy-start(bf16[256,2048]{1,0:T(8,128)(2,1)S(1)} %constant_dynamic-update-slice_fusion) | copy-start | bytes 3145732

commit v3 on v2

v3 whole, which is shorter than its diff:
```python
import jax
import jax.numpy as jnp
from jax import lax
from jax.experimental import pallas as pl
from jax.experimental.pallas import tpu as pltpu
from jax.sharding import PartitionSpec as P

epsilon = 1e-06
AXES = ("dp", "tensor")
BF16 = jnp.bfloat16
F32 = jnp.float32
VMEM_LIMIT = 60 * 1024 * 1024


def slot_rows(ids_t, first, count, cap):
    top, tokens = ids_t.shape
    names = lax.broadcasted_iota(jnp.int32, (count, tokens), 0) + first
    named = jnp.zeros((count, tokens), F32)
    for k in range(top):
        named = named + jnp.where(ids_t[k : k + 1, :] == names, 1.0, 0.0)
    before = jnp.where(
        lax.broadcasted_iota(jnp.int32, (tokens, tokens), 0)
        < lax.broadcasted_iota(jnp.int32, (tokens, tokens), 1),
        1.0,
        0.0,
    ).astype(BF16)
    rank = jnp.dot(named.astype(BF16), before, preferred_element_type=F32)
    rank = jnp.where(named > 0.0, rank, -1.0)
    place = lax.broadcasted_iota(jnp.int32, (count, cap, tokens), 1).astype(F32)
    return jnp.where(rank[:, None, :] == place, 1.0, 0.0)


def pack_kernel(quarter, ids_t, probs_t, hidden, gain, grad, out, buf, sems):
    chunks = sems.shape[0]
    rows, cap = out.shape[0] // chunks, 8
    count = rows // cap
    width = hidden.shape[1]
    values = hidden[...].astype(F32)
    inverse = lax.rsqrt(jnp.mean(values * values, axis=-1, keepdims=True) + epsilon)
    normed = (values * inverse * gain[...]).astype(BF16)
    ids = ids_t[...]
    top, tokens = ids.shape
    copies = []
    for chunk in range(chunks):
        chosen = slot_rows(ids, chunk * count, count, cap)
        names = lax.broadcasted_iota(jnp.int32, (count, tokens), 0) + chunk * count
        prob = jnp.zeros((count, tokens), F32)
        for k in range(top):
            prob = prob + jnp.where(ids[k : k + 1, :] == names, probs_t[k : k + 1, :], 0.0)
        weight = jnp.sum(
            (chosen * prob[:, None, :]).reshape(rows, tokens), axis=1, keepdims=True
        )
        chosen = chosen.reshape(rows, tokens).astype(BF16)
        part = pl.ds(chunk * rows, rows)
        buf[part, :width] = jnp.dot(chosen, normed, preferred_element_type=F32).astype(BF16)
        picked = jnp.dot(chosen, grad[...], preferred_element_type=F32)
        buf[part, width:] = (picked * weight).astype(BF16)
        copy = pltpu.make_async_copy(buf.at[part], out.at[part], sems.at[chunk])
        copy.start()
        copies.append(copy)
    for copy in copies:
        copy.wait()


def expert_kernel(
    received, gate_hbm, up_hbm, down_hbm, back, act, gate_pgrad, up_pgrad,
    inputs, cotan, both_w, down_w, back_buf, act_buf, grads_buf, in_sems, out_sems,
):
    blocks = out_sems.shape[0] // 4
    rows = received.shape[0] // blocks
    width = back.shape[1]
    units = act.shape[1]
    weight_copies = [
        pltpu.make_async_copy(gate_hbm, both_w.at[:, pl.ds(0, units)], in_sems.at[0]),
        pltpu.make_async_copy(up_hbm, both_w.at[:, pl.ds(units, units)], in_sems.at[1]),
        pltpu.make_async_copy(down_hbm, down_w, in_sems.at[2]),
    ]
    row_copies = []
    for block in range(blocks):
        part = pl.ds(block * rows, rows)
        for n, target in enumerate((inputs, cotan)):
            row_copies.append(
                pltpu.make_async_copy(
                    received.at[part, pl.ds(n * width, width)],
                    target.at[part],
                    in_sems.at[3 + 2 * block + n],
                )
            )
    for copy in [weight_copies[0], row_copies[0], *weight_copies[1:], *row_copies[1:]]:
        copy.start()
    out_copies = []
    for block in range(blocks):
        part = pl.ds(block * rows, rows)
        row_copies[2 * block].wait()
        if block == 0:
            weight_copies[0].wait()
            weight_copies[1].wait()
        pre = jnp.dot(inputs[part, :], both_w[...], preferred_element_type=F32)
        gate_pre, up_pre = pre[:, :units], pre[:, units:]
        sigma = jax.nn.sigmoid(gate_pre)
        silu_vals = gate_pre * sigma
        act_buf[part, :] = (silu_vals * up_pre).astype(BF16)
        row_copies[2 * block + 1].wait()
        if block == 0:
            weight_copies[2].wait()
        act_grad = lax.dot_general(
            cotan[part, :], down_w[...], (((1,), (1,)), ((), ())), preferred_element_type=F32
        )
        grads_buf[part, :units] = (
            act_grad * up_pre * sigma * (1.0 + gate_pre * (1.0 - sigma))
        ).astype(BF16)
        grads_buf[part, units:] = (act_grad * silu_vals).astype(BF16)
        back_buf[part, :] = lax.dot_general(
            grads_buf[part, :], both_w[...], (((1,), (1,)), ((), ())), preferred_element_type=F32
        ).astype(BF16)
        for n, (source, target) in enumerate(
            (
                (back_buf.at[part], back),
                (act_buf.at[part], act),
                (grads_buf.at[part, pl.ds(0, units)], gate_pgrad),
                (grads_buf.at[part, pl.ds(units, units)], up_pgrad),
            )
        ):
            copy = pltpu.make_async_copy(source, target.at[part], out_sems.at[4 * block + n])
            copy.start()
            out_copies.append(copy)
    for copy in out_copies:
        copy.wait()


def routes_kernel(ids, probs, routes, weights):
    tokens, top = ids.shape
    slots = routes.shape[1]
    cap = 8
    experts = slots // cap
    names = lax.broadcasted_iota(jnp.int32, (tokens, experts), 1)
    named = jnp.zeros((tokens, experts), F32)
    prob = jnp.zeros((tokens, experts), F32)
    for k in range(top):
        hit = ids[:, k : k + 1] == names
        named = named + jnp.where(hit, 1.0, 0.0)
        prob = prob + jnp.where(hit, probs[:, k : k + 1], 0.0)
    before = jnp.where(
        lax.broadcasted_iota(jnp.int32, (tokens, tokens), 1)
        < lax.broadcasted_iota(jnp.int32, (tokens, tokens), 0),
        1.0,
        0.0,
    ).astype(BF16)
    rank = jnp.dot(before, named.astype(BF16), preferred_element_type=F32)
    rank = jnp.where(named > 0.0, rank, -1.0).astype(BF16)
    spread = jnp.where(
        lax.broadcasted_iota(jnp.int32, (experts, slots), 1) // cap
        == lax.broadcasted_iota(jnp.int32, (experts, slots), 0),
        1.0,
        0.0,
    ).astype(BF16)
    place = (lax.broadcasted_iota(jnp.int32, (tokens, slots), 1) % cap).astype(F32)
    chosen = jnp.where(
        jnp.dot(rank, spread, preferred_element_type=F32) == place, 1.0, 0.0
    )
    routes[...] = chosen.astype(BF16)
    left = prob
    for part in range(3):
        piece = left.astype(BF16)
        left = left - piece.astype(F32)
        weights[part * tokens : (part + 1) * tokens, :] = (
            chosen * jnp.dot(piece, spread, preferred_element_type=F32)
        ).astype(BF16)


def combine_kernel(
    quarter, ids, routes, weights, rows, hidden, grad, layer_out, gate_grad, total, found
):
    step = pl.program_id(0)
    tokens, top = ids.shape
    slots = rows.shape[0]

    @pl.when(step == 0)
    def _():
        total[...] = hidden[...].astype(F32)
        found[...] = jnp.zeros_like(found)

    parts = jnp.dot(weights[...], rows[...], preferred_element_type=F32)
    total[...] += parts[:tokens] + parts[tokens : 2 * tokens] + parts[2 * tokens :]
    dots = lax.dot_general(
        rows[...], grad[...], (((1,), (1,)), ((), ())), preferred_element_type=F32
    ).T
    mine = jnp.where(routes[...].astype(F32) > 0.0, dots, 0.0)
    expert = (lax.broadcasted_iota(jnp.int32, (tokens, slots), 1) + step * slots) // 8
    column = lax.broadcasted_iota(jnp.int32, found.shape, 1)
    sums = found[...]
    for k in range(top):
        own = jnp.where(expert == ids[:, k : k + 1], mine, 0.0)
        sums = sums + jnp.where(column == k, jnp.sum(own, axis=1, keepdims=True), 0.0)
    found[...] = sums

    @pl.when(step == pl.num_programs(0) - 1)
    def _():
        layer_out[...] = total[...].astype(BF16)
        gate_grad[...] = found[...].T[:top, :]


def norm_grad_kernel(quarter, routes, rows, hidden, gain, grad, own_grad, total):
    step = pl.program_id(0)

    @pl.when(step == 0)
    def _():
        total[...] = jnp.zeros_like(total)

    total[...] += jnp.dot(routes[...], rows[...], preferred_element_type=F32)

    @pl.when(step == pl.num_programs(0) - 1)
    def _():
        values = hidden[...].astype(F32)
        inverse = lax.rsqrt(jnp.mean(values * values, axis=-1, keepdims=True) + epsilon)
        unit = values * inverse
        summed = total[...]
        upstream = summed * gain[...]
        own_grad[...] = (
            grad[...].astype(F32)
            + inverse * (upstream - unit * jnp.mean(upstream * unit, axis=-1, keepdims=True))
        ).astype(BF16)


def exchange(block):
    return lax.all_to_all(block, AXES, split_axis=0, concat_axis=0, tiled=True)


def gather_group(block):
    size = lax.axis_size("tensor")
    mine = lax.axis_index("tensor")
    rows = block.shape[0]
    whole = jnp.zeros((size * rows, block.shape[1]), block.dtype)
    moved = [(0, block)] + [
        (step, lax.ppermute(block, "tensor", [(i, (i + step) % size) for i in range(size)]))
        for step in (1, 3, 2)
    ]
    for step, piece in moved:
        origin = (mine - step) % size
        whole = lax.dynamic_update_slice_in_dim(whole, piece, origin * rows, 0)
    return whole


def add_from(value, axis, distances):
    size = lax.axis_size(axis)
    others = [
        lax.ppermute(value, axis, [(i, i ^ distance) for i in range(size)])
        for distance in distances
    ]
    for other in others:
        value = value + other
    return value


def after(value, *earlier):
    return lax.optimization_barrier((value, *earlier))[0]


def params():
    return pltpu.CompilerParams(vmem_limit_bytes=VMEM_LIMIT)


def cost(flops, moved):
    return pl.CostEstimate(flops=flops, bytes_accessed=moved, transcendentals=0)


def dot(a, b, dims):
    return lax.dot_general(a, b, (dims, ((), ())), preferred_element_type=F32)


def per_device(
    hidden, norm_gain, expert_ids, gate_probs, out_grad, gate_weight, up_weight, down_weight
):
    own, width = out_grad.shape
    top = expert_ids.shape[1]
    devices = lax.axis_size(AXES)
    cap = 8
    slots = devices * cap
    steps = 4
    quarter = lax.axis_index("tensor").astype(jnp.int32).reshape(1)
    gain = norm_gain.reshape(1, width)
    ids_t = expert_ids.T
    probs_t = gate_probs.T

    def whole(*shape):
        return pl.BlockSpec(shape, lambda *_: (0,) * len(shape))

    hbm = pl.BlockSpec(memory_space=pl.ANY)
    buf = pl.pallas_call(
        pack_kernel,
        grid_spec=pltpu.PrefetchScalarGridSpec(
            num_scalar_prefetch=1,
            grid=(1,),
            in_specs=[
                whole(top, own),
                whole(top, own),
                pl.BlockSpec((own, width), lambda i, q: (q[0], 0)),
                whole(1, width),
                whole(own, width),
            ],
            out_specs=hbm,
            scratch_shapes=[
                pltpu.VMEM((slots, 2 * width), BF16),
                pltpu.SemaphoreType.DMA((steps,)),
            ],
        ),
        out_shape=jax.ShapeDtypeStruct((slots, 2 * width), BF16),
        compiler_params=params(),
        cost_estimate=cost(4 * slots * own * width, 4 * slots * width),
        name="pack",
    )(quarter, ids_t, probs_t, hidden, gain, out_grad)
    received = exchange(buf)

    routes, weights = pl.pallas_call(
        routes_kernel,
        out_shape=[
            jax.ShapeDtypeStruct((own, slots), BF16),
            jax.ShapeDtypeStruct((3 * own, slots), BF16),
        ],
        compiler_params=params(),
        cost_estimate=cost(2 * 4 * own * devices * slots, 8 * own * slots),
        name="routes",
    )(after(expert_ids, buf), gate_probs)

    gate_w, up_w, down_w = gate_weight[0], up_weight[0], down_weight[0]
    units = gate_w.shape[1]
    blocks = 2
    back, act, gate_pgrad, up_pgrad = pl.pallas_call(
        expert_kernel,
        in_specs=[hbm] * 4,
        out_specs=[hbm] * 4,
        out_shape=[
            jax.ShapeDtypeStruct((slots, width), BF16),
            jax.ShapeDtypeStruct((slots, units), BF16),
            jax.ShapeDtypeStruct((slots, units), BF16),
            jax.ShapeDtypeStruct((slots, units), BF16),
        ],
        scratch_shapes=[
            pltpu.VMEM((slots, width), BF16),
            pltpu.VMEM((slots, width), BF16),
            pltpu.VMEM((width, 2 * units), BF16),
            pltpu.VMEM((units, width), BF16),
            pltpu.VMEM((slots, width), BF16),
            pltpu.VMEM((slots, units), BF16),
            pltpu.VMEM((slots, 2 * units), BF16),
            pltpu.SemaphoreType.DMA((3 + 2 * blocks,)),
            pltpu.SemaphoreType.DMA((4 * blocks,)),
        ],
        compiler_params=params(),
        cost_estimate=cost(10 * slots * width * units, 12 * slots * width),
        name="expert",
    )(received, gate_w, up_w, down_w)
    back_rows = exchange(back)

    result = dot(act, down_w, ((1,), (0,))).astype(BF16)
    inputs, cotan = received[:, :width], received[:, width:]
    gate_wgrad = dot(inputs, gate_pgrad, ((0,), (0,))).astype(BF16)
    up_wgrad = dot(inputs, up_pgrad, ((0,), (0,))).astype(BF16)
    down_grad = dot(act, cotan, ((0,), (0,))).astype(BF16)
    gain_part = jnp.sum(back.astype(F32) * inputs.astype(F32), axis=0, keepdims=True) / gain
    gain_part = add_from(gain_part, "dp", (1,))
    gain_part = add_from(gain_part, "tensor", (1, 2, 3))
    gain_part = add_from(gain_part, "dp", (2, 4, 6))
    result, gate_wgrad, up_wgrad, down_grad, back_rows, routes, weights, gain_part = (
        lax.optimization_barrier(
            (result, gate_wgrad, up_wgrad, down_grad, back_rows, routes, weights, gain_part)
        )
    )
    returned = exchange(result)
    gain_grad = add_from(add_from(gain_part, "dp", (8,)), "dp", (16,))[0]

    own_grad = pl.pallas_call(
        norm_grad_kernel,
        grid_spec=pltpu.PrefetchScalarGridSpec(
            num_scalar_prefetch=1,
            grid=(steps,),
            in_specs=[
                pl.BlockSpec((own, slots // steps), lambda i, q: (0, i)),
                pl.BlockSpec((slots // steps, width), lambda i, q: (i, 0)),
                pl.BlockSpec((own, width), lambda i, q: (q[0], 0)),
                whole(1, width),
                whole(own, width),
            ],
            out_specs=whole(own, width),
            scratch_shapes=[pltpu.VMEM((own, width), F32)],
        ),
        out_shape=jax.ShapeDtypeStruct((own, width), BF16),
        compiler_params=params(),
        cost_estimate=cost(2 * own * slots * width, 2 * slots * width),
        name="norm_grad",
    )(quarter, routes, back_rows, hidden, gain, out_grad)
    input_grad = gather_group(own_grad)

    halves = 2
    layer_out, gate_grad_t = pl.pallas_call(
        combine_kernel,
        grid_spec=pltpu.PrefetchScalarGridSpec(
            num_scalar_prefetch=1,
            grid=(halves,),
            in_specs=[
                whole(own, top),
                pl.BlockSpec((own, slots // halves), lambda i, q: (0, i)),
                pl.BlockSpec((3 * own, slots // halves), lambda i, q: (0, i)),
                pl.BlockSpec((slots // halves, width), lambda i, q: (i, 0)),
                pl.BlockSpec((own, width), lambda i, q: (q[0], 0)),
                whole(own, width),
            ],
            out_specs=[whole(own, width), whole(top, own)],
            scratch_shapes=[pltpu.VMEM((own, width), F32), pltpu.VMEM((own, 128), F32)],
        ),
        out_shape=[
            jax.ShapeDtypeStruct((own, width), BF16),
            jax.ShapeDtypeStruct((top, own), F32),
        ],
        compiler_params=params(),
        cost_estimate=cost(8 * own * slots * width, 2 * slots * width),
        name="combine",
    )(quarter, expert_ids, routes, weights, returned, hidden, out_grad)
    return (
        layer_out,
        input_grad,
        gate_grad_t.T,
        gain_grad,
        gate_wgrad[None],
        up_wgrad[None],
        down_grad[None],
    )


def solution(mesh):
    in_specs = (
        P("dp", None),
        P(),
        P(AXES, None),
        P(AXES, None),
        P(AXES, None),
        P(AXES, None, None),
        P(AXES, None, None),
        P(AXES, None, None),
    )
    out_specs = (
        P(AXES, None),
        P("dp", None),
        P(AXES, None),
        P(),
        P(AXES, None, None),
        P(AXES, None, None),
        P(AXES, None, None),
    )
    return jax.shard_map(
        per_device, mesh=mesh, in_specs=in_specs, out_specs=out_specs, check_vma=False
    )
```

time: 290 us -> 287 us (0.990)
  blocking collectives: 109 us -> 0 us
  waiting for transfers between devices: 64.4 us -> 155 us
  starting transfers between devices: 33.5 us -> 49.3 us
  Pallas kernels: 50.4 us -> 43.2 us
  other arithmetic: 1.36 us -> 5.99 us
    all_to_all x1 -> x0, blocking collectives: 109 us -> none  [exchange(): return lax.all_to_all(block, AXES, split_axis=0, concat_axis=0, tiled=True)]
    all_to_all x2 -> x3, waiting for transfers between devices: 22.3 us -> 101 us  [exchange(): return lax.all_to_all(block, AXES, split_axis=0, concat_axis=0, tiled=True)]
    all_to_all x2 -> x3, starting transfers between devices: 12.7 us -> 28.6 us  [exchange(): return lax.all_to_all(block, AXES, split_axis=0, concat_axis=0, tiled=True)]
    ppermute x10 -> x9, waiting for transfers between devices: 37.4 us -> 48.3 us  [add_from(): lax.ppermute(value, axis, [(i, i ^ distance) for i in range(size)])]
    reduce_sum x0 -> x1, other arithmetic: none -> 5.32 us  [per_device(): jnp.sum(back.astype(F32) * inputs.astype(F32), axis=0, keepdims=True) / gain]
    pallas_call x1, Pallas kernels: 28.7 us -> 25.3 us  [per_device(): pl.pallas_call(expert_kernel, in_specs=[hbm] * 4, out_specs=[hbm] * 4, ou...]
    ppermute x10 -> x9, starting transfers between devices: 18.2 us -> 15.7 us  [add_from(): lax.ppermute(value, axis, [(i, i ^ distance) for i in range(size)])]
  transfers between devices with their start and end apart: 15 -> 15, of which waited for: 9 -> 9; matrix products, arithmetic and copies ran while one was open for 11% -> 13% of each run, Pallas kernels for 2% -> 2%
where the time goes in v3:
time: 287 us; the launch traced here: 285 us
  waiting for transfers between devices  155 us (54%)
  starting transfers between devices  49.3 us (17%)
  Pallas kernels  43.2 us (15%)
  matrix products  27.2 us (9%)
  other arithmetic  5.99 us (2%)
  local copies, waits for them, and re-layouts  3.28 us (1%)
    all_to_all x3, waiting for transfers between devices, exchange(): return lax.all_to_all(block, AXES, split_axis=0, concat_axis=0, tiled=True)  101 us
    ppermute x9, waiting for transfers between devices, add_from(): lax.ppermute(value, axis, [(i, i ^ distance) for i in range(size)])  48.3 us
    all_to_all x3, starting transfers between devices, exchange(): return lax.all_to_all(block, AXES, split_axis=0, concat_axis=0, tiled=True)  28.6 us
    dot_general x4, matrix products, dot(): return lax.dot_general(a, b, (dims, ((), ())), preferred_element_type=F32)  27.2 us
    pallas_call x1, Pallas kernels, per_device(): pl.pallas_call(expert_kernel, in_specs=[hbm] * 4, out_specs=[hbm] * 4, ou...  25.3 us
    ppermute x9, starting transfers between devices, add_from(): lax.ppermute(value, axis, [(i, i ^ distance) for i in range(size)])  15.7 us
    ppermute x3, waiting for transfers between devices, gather_group(): lax.ppermute(block, 'tensor', [(i, (i + step) % size) for i in range(size)])  6.34 us
  transfers between devices with their start and end apart: 15, of which 9 were waited for; matrix products, arithmetic and copies ran while one was open for 13% of the time, Pallas kernels for 2%

profile of v3, /device:TPU:0, one launch (start us, length us, event | category | flops | bytes accessed | tf_op | source)
XLA Modules:
  0.0 285.2 jit_solution(4860137639573639846)
XLA Ops:
  0.6 5.3 %pack.1 = bf16[1024,4096]{1,0:T(8,128)(2,1)} custom-call(s32[1]{0:T(128)} %bitcast.quarter, s32[8,64]{1,0:T(8,128)} %bitcast.30, f32[8,64]{1,0:T(8,128)} %bitcast.33, bf16[256,2048]{1,0:T(8,128)(2,1)} %hidden.5, f32[1,2048]{1,0:T(1,128)} %bitcast.28, bf16[64,2048]{1,0:T(8,128)(2,1)} %grad.5), custom_call_target="tpu_custom_call" | custom-call | flops 536870912 | bytes 8388608 | tf_op jit(solution)/shard_map/pack/pallas_call | solution.py:289
  6.0 0.0 copy-start.3
  6.0 0.0 copy-start.2
  6.0 11.9 %all-to-all-start = ((bf16[128,8,4096]{2,1,0:T(8,128)(2,1)}), bf16[128,8,4096]{2,1,0:T(8,128)(2,1)}, u32[]{:S(2)}, u32[]{:S(2)}) async-start(bf16[128,8,4096]{2,1,0:T(8,128)(2,1)} %bitcast.25), calls=%async_computation | async-start | bytes 16777216 | tf_op jit(solution)/shard_map/all_to_all | solution.py:226
  17.9 0.7 copy.16.probs
  18.6 0.7 copy.15.ids
  19.3 2.1 routes.1
  21.4 100.6 %all-to-all-done = bf16[128,8,4096]{2,1,0:T(8,128)(2,1)} async-done(((bf16[128,8,4096]{2,1,0:T(8,128)(2,1)}), bf16[128,8,4096]{2,1,0:T(8,128)(2,1)}, u32[]{:S(2)}, u32[]{:S(2)}) %all-to-all-start) | async-done | bytes 8388640 | tf_op jit(solution)/shard_map/all_to_all | solution.py:226
  122.0 25.3 %expert.1 = (bf16[1024,2048]{1,0:T(8,128)(2,1)}, bf16[1024,768]{1,0:T(8,128)(2,1)}, bf16[1024,768]{1,0:T(8,128)(2,1)}, bf16[1024,768]{1,0:T(8,128)(2,1)}) custom-call(bf16[1024,4096]{1,0:T(8,128)(2,1)} %bitcast.5.received, bf16[2048,768]{1,0:T(8,128)(2,1)} %bitcast.35, bf16[2048,768]{1,0:T(8,128)(2,1)} %bitcast.36, bf16[768,2048]{1,0:T(8,128)(2,1)} %bitcast.37), custom_call_target="tpu_custom_call" | custom-call | flops 16106127360 | bytes 25165824 | tf_op jit(solution)/shard_map/expert/pallas_call | solution.py:328
  147.3 6.1 %all-to-all-start.1 = ((bf16[128,8,2048]{2,1,0:T(8,128)(2,1)}), bf16[128,8,2048]{2,1,0:T(8,128)(2,1)}, u32[]{:S(2)}, u32[]{:S(2)}) async-start(bf16[128,8,2048]{2,1,0:T(8,128)(2,1)} %bitcast.26), calls=%async_computation.1 | async-start | bytes 8388608 | tf_op jit(solution)/shard_map/all_to_all | solution.py:226
  153.4 0.0 copy-start.1
  153.4 0.0 copy-start.7
  153.4 5.3 %multiply_reduce_fusion = f32[2048]{0:T(1024)S(1)} fusion(bf16[1024,2048]{1,0:T(8,128)(2,1)} %get-tuple-element.27, bf16[1024,4096]{1,0:T(8,128)(2,1)} %bitcast.5.received), kind=kLoop, calls=%fused_computation | loop fusion | flops 8386560 | bytes 8396800 | tf_op jit(solution)/shard_map/reduce_sum | solution.py:360
  158.8 0.1 collective-permute-start
  158.9 7.5 %convolution_convert_fusion.2 = bf16[2048,768]{1,0:T(8,128)(2,1)} fusion(bf16[1024,768]{1,0:T(8,128)(2,1)S(1)} %copy-done.7, bf16[1024,4096]{1,0:T(8,128)(2,1)} %bitcast.5.received), kind=kOutput, calls=%fused_computation.6 | convolution fusion | flops 3222798336 | bytes 8912896 | tf_op jit(solution)/shard_map/dot_general | solution.py:268
  166.4 7.5 %convolution_convert_fusion.1 = bf16[2048,768]{1,0:T(8,128)(2,1)} fusion(bf16[1024,768]{1,0:T(8,128)(2,1)S(1)} %copy-done.6, bf16[1024,4096]{1,0:T(8,128)(2,1)} %bitcast.5.received), kind=kOutput, calls=%fused_computation.5 | convolution fusion | flops 3222798336 | bytes 8912896 | tf_op jit(solution)/shard_map/dot_general | solution.py:268
  173.9 2.4 collective-permute-start.3
  176.3 0.8 collective-permute-start.2
  177.1 1.0 collective-permute-start.1
  178.1 7.2 %fusion.2 = bf16[768,2048]{1,0:T(8,128)(2,1)} fusion(bf16[1024,768]{1,0:T(8,128)(2,1)S(1)} %copy-done.5, bf16[1024,4096]{1,0:T(8,128)(2,1)} %bitcast.5.received), kind=kOutput, calls=%fused_computation.4 | convolution fusion | flops 3222798336 | bytes 8912896 | tf_op jit(solution)/shard_map/dot_general | solution.py:268
  185.3 6.3 %collective-permute-done.3 = f32[1,2048]{1,0:T(1,128)S(1)} collective-permute-done((f32[1,2048]{1,0:T(1,128)S(1)}, f32[1,2048]{1,0:T(1,128)S(1)}, u32[]{:S(2)}, u32[]{:S(2)}) %collective-permute-start.3) | collective-permute-done | bytes 8224 | tf_op jit(solution)/shard_map/ppermute | solution.py:247
  191.6 2.7 collective-permute-done.2
  194.3 3.3 %collective-permute-done.1 = f32[1,2048]{1,0:T(1,128)S(1)} collective-permute-done((f32[1,2048]{1,0:T(1,128)S(1)}, f32[1,2048]{1,0:T(1,128)S(1)}, u32[]{:S(2)}, u32[]{:S(2)}) %collective-permute-start.1) | collective-permute-done | bytes 8224 | tf_op jit(solution)/shard_map/ppermute | solution.py:247
  197.7 4.9 %collective-permute-start.6 = (f32[1,2048]{1,0:T(1,128)S(1)}, f32[1,2048]{1,0:T(1,128)S(1)}, u32[]{:S(2)}, u32[]{:S(2)}) collective-permute-start(f32[1,2048]{1,0:T(1,128)S(1)} %add_add_fusion.1), channel_id=1, source_target_pairs={{0,24},{4,28},{8,16},{12,20},{16,8},{20,12},{24,0},{28,4},{32,56},... | collective-permute-start | bytes 24584 | tf_op jit(solution)/shard_map/ppermute | solution.py:247
  202.6 2.6 collective-permute-start.5
  205.2 0.0 collective-permute-start.4
  205.2 5.0 %convolution_convert_fusion = bf16[1024,2048]{1,0:T(8,128)(2,1)} fusion(bf16[1024,768]{1,0:T(8,128)(2,1)S(1)} %copy-done.5, bf16[1,768,2048]{2,1,0:T(8,128)(2,1)S(1)} %copy-done.4), kind=kOutput, calls=%fused_computation.3 | convolution fusion | flops 3223322624 | bytes 8912896 | tf_op jit(solution)/shard_map/dot_general | solution.py:268
  210.2 0.0 collective-permute-done.6
  210.2 0.0 collective-permute-done.5
  210.2 0.0 collective-permute-done.4
  210.3 10.6 %all-to-all-start.2 = ((bf16[128,8,2048]{2,1,0:T(8,128)(2,1)}), bf16[128,8,2048]{2,1,0:T(8,128)(2,1)}, u32[]{:S(2)}, u32[]{:S(2)}) async-start(bf16[128,8,2048]{2,1,0:T(8,128)(2,1)} %bitcast.27), calls=%async_computation.2 | async-start | bytes 8388608 | tf_op jit(solution)/shard_map/all_to_all | solution.py:226
  220.9 4.7 %norm_grad.1 = bf16[64,2048]{1,0:T(8,128)(2,1)} custom-call(s32[1]{0:T(128)} %bitcast.quarter, bf16[64,1024]{1,0:T(8,128)(2,1)} %get-tuple-element.31.routes, bf16[1024,2048]{1,0:T(8,128)(2,1)} %bitcast.10.rows, bf16[256,2048]{1,0:T(8,128)(2,1)} %hidden.5, f32[1,2048]{1,0:T(1,128)} %bitcast.29, bf16[64,2048]{1,0:T(8,128)(2,1)} %grad.5), custom_call_target="tpu_custom_call" | custom-call | flops 268435456 | bytes 4194304 | tf_op jit(solution)/shard_map/norm_grad/pallas_call | solution.py:372
  225.7 0.9 collective-permute-start.7
  226.6 1.5 collective-permute-start.10
  228.0 0.7 copy.17.ids
  228.7 2.7 collective-permute-start.9
  231.5 1.4 collective-permute-start.8
  232.9 34.3 %collective-permute-done.10 = f32[1,2048]{1,0:T(1,128)S(1)} collective-permute-done((f32[1,2048]{1,0:T(1,128)S(1)}, f32[1,2048]{1,0:T(1,128)S(1)}, u32[]{:S(2)}, u32[]{:S(2)}) %collective-permute-start.10) | collective-permute-done | bytes 8224 | tf_op jit(solution)/shard_map/ppermute | solution.py:247
  267.2 2.4 collective-permute-start.11
  269.6 0.1 broadcast_in_dim.13
  269.7 1.0 constant_dynamic-update-slice_fusion.3
  270.7 1.7 collective-permute-done.11
  272.4 0.6 add.71
  273.0 0.8 collective-permute-done.7
  273.8 4.8 %collective-permute-done.8 = bf16[64,2048]{1,0:T(8,128)(2,1)S(1)} collective-permute-done((bf16[64,2048]{1,0:T(8,128)(2,1)}, bf16[64,2048]{1,0:T(8,128)(2,1)S(1)}, u32[]{:S(2)}, u32[]{:S(2)}) %collective-permute-start.8) | collective-permute-done | bytes 262176 | tf_op jit(solution)/shard_map/ppermute | solution.py:235
  278.6 0.8 collective-permute-done.9
  279.4 0.0 copy-start
  279.4 5.7 %combine.1 = (bf16[64,2048]{1,0:T(8,128)(2,1)}, f32[8,64]{1,0:T(8,128)}) custom-call(s32[1]{0:T(128)} %bitcast.quarter, s32[64,8]{1,0:T(8,128)} %copy.17.ids, bf16[64,1024]{1,0:T(8,128)(2,1)} %get-tuple-element.31.routes, bf16[192,1024]{1,0:T(8,128)(2,1)} %get-tuple-element.32.weights, bf16[1024,2048]{1,0:T(8,128)(2,1)} %bitcast.13.rows, ...), custom_call_target="tpu_custom_call" | custom-call | flops 1073741824 | bytes 4194304 | tf_op jit(solution)/shard_map/combine/pallas_call | solution.py:395
  (22 shorter events, 0.2 us)
Async XLA Ops:
  6.0 11.9 %copy-start.3 = (f32[64,8]{0,1:T(8,128)S(1)}, f32[64,8]{0,1:T(8,128)}, u32[]{:S(2)}) copy-start(f32[64,8]{0,1:T(8,128)} %param.11) | copy-start | bytes 6148
  6.0 12.6 %copy-start.2 = (s32[64,8]{0,1:T(8,128)S(1)}, s32[64,8]{0,1:T(8,128)}, u32[]{:S(2)}) copy-start(s32[64,8]{0,1:T(8,128)} %param.10) | copy-start | bytes 6148
  6.0 116.0 %all-to-all-start = ((bf16[128,8,4096]{2,1,0:T(8,128)(2,1)}), bf16[128,8,4096]{2,1,0:T(8,128)(2,1)}, u32[]{:S(2)}, u32[]{:S(2)}) async-start(bf16[128,8,4096]{2,1,0:T(8,128)(2,1)} %bitcast.25), calls=%async_computation | async-start | bytes 16777216 | tf_op jit(solution)/shard_map/all_to_all | solution.py:226
  147.3 62.9 %all-to-all-start.1 = ((bf16[128,8,2048]{2,1,0:T(8,128)(2,1)}), bf16[128,8,2048]{2,1,0:T(8,128)(2,1)}, u32[]{:S(2)}, u32[]{:S(2)}) async-start(bf16[128,8,2048]{2,1,0:T(8,128)(2,1)} %bitcast.26), calls=%async_computation.1 | async-start | bytes 8388608 | tf_op jit(solution)/shard_map/all_to_all | solution.py:226
  153.4 5.3 %copy-start.1 = (f32[2048]{0:T(1024)S(1)}, f32[2048]{0:T(1024)}, u32[]{:S(2)}) copy-start(f32[2048]{0:T(1024)} %param.9) | copy-start | bytes 24580
  153.4 5.4 %copy-start.7 = (bf16[1024,768]{1,0:T(8,128)(2,1)S(1)}, bf16[1024,768]{1,0:T(8,128)(2,1)}, u32[]{:S(2)}) copy-start(bf16[1024,768]{1,0:T(8,128)(2,1)} %get-tuple-element.25) | copy-start | bytes 4718596
  158.8 15.1 %collective-permute-start = (f32[1,2048]{1,0:T(1,128)S(1)}, f32[1,2048]{1,0:T(1,128)S(1)}, u32[]{:S(2)}, u32[]{:S(2)}) collective-permute-start(f32[1,2048]{1,0:T(1,128)S(1)} %bitcast.31), channel_id=1, source_target_pairs={{0,4},{4,0},{8,12},{12,8},{16,20},{20,16},{24,28},{28,24},{32,36},... | collective-permute-start | bytes 24584 | tf_op jit(solution)/shard_map/ppermute | solution.py:247
  158.9 7.5 %copy-start.6 = (bf16[1024,768]{1,0:T(8,128)(2,1)S(1)}, bf16[1024,768]{1,0:T(8,128)(2,1)}, u32[]{:S(2)}) copy-start(bf16[1024,768]{1,0:T(8,128)(2,1)} %get-tuple-element.26) | copy-start | bytes 4718596
  166.4 11.7 %copy-start.5 = (bf16[1024,768]{1,0:T(8,128)(2,1)S(1)}, bf16[1024,768]{1,0:T(8,128)(2,1)}, u32[]{:S(2)}) copy-start(bf16[1024,768]{1,0:T(8,128)(2,1)} %get-tuple-element.24) | copy-start | bytes 4718596
  173.9 17.7 %collective-permute-start.3 = (f32[1,2048]{1,0:T(1,128)S(1)}, f32[1,2048]{1,0:T(1,128)S(1)}, u32[]{:S(2)}, u32[]{:S(2)}) collective-permute-start(f32[1,2048]{1,0:T(1,128)S(1)} %add.55), channel_id=1, source_target_pairs={{0,3},{1,2},{2,1},{3,0},{4,7},{5,6},{6,5},{7,4},{8,11},{9,10},{10,... | collective-permute-start | bytes 24584 | tf_op jit(solution)/shard_map/ppermute | solution.py:247
  176.3 18.0 %collective-permute-start.2 = (f32[1,2048]{1,0:T(1,128)S(1)}, f32[1,2048]{1,0:T(1,128)S(1)}, u32[]{:S(2)}, u32[]{:S(2)}) collective-permute-start(f32[1,2048]{1,0:T(1,128)S(1)} %add.55), channel_id=1, source_target_pairs={{0,2},{1,3},{2,0},{3,1},{4,6},{5,7},{6,4},{7,5},{8,10},{9,11},{10,... | collective-permute-start | bytes 24584 | tf_op jit(solution)/shard_map/ppermute | solution.py:247
  177.1 20.5 %collective-permute-start.1 = (f32[1,2048]{1,0:T(1,128)S(1)}, f32[1,2048]{1,0:T(1,128)S(1)}, u32[]{:S(2)}, u32[]{:S(2)}) collective-permute-start(f32[1,2048]{1,0:T(1,128)S(1)} %add.55), channel_id=1, source_target_pairs={{0,1},{1,0},{2,3},{3,2},{4,5},{5,4},{6,7},{7,6},{8,9},{9,8},{10,11... | collective-permute-start | bytes 24584 | tf_op jit(solution)/shard_map/ppermute | solution.py:247
  178.1 27.1 %copy-start.4 = (bf16[1,768,2048]{2,1,0:T(8,128)(2,1)S(1)}, bf16[1,768,2048]{2,1,0:T(8,128)(2,1)}, u32[]{:S(2)}) copy-start(bf16[1,768,2048]{2,1,0:T(8,128)(2,1)} %param.15) | copy-start | bytes 9437188
  197.7 12.6 %collective-permute-start.6 = (f32[1,2048]{1,0:T(1,128)S(1)}, f32[1,2048]{1,0:T(1,128)S(1)}, u32[]{:S(2)}, u32[]{:S(2)}) collective-permute-start(f32[1,2048]{1,0:T(1,128)S(1)} %add_add_fusion.1), channel_id=1, source_target_pairs={{0,24},{4,28},{8,16},{12,20},{16,8},{20,12},{24,0},{28,4},{32,56},... | collective-permute-start | bytes 24584 | tf_op jit(solution)/shard_map/ppermute | solution.py:247
  202.6 7.7 %collective-permute-start.5 = (f32[1,2048]{1,0:T(1,128)S(1)}, f32[1,2048]{1,0:T(1,128)S(1)}, u32[]{:S(2)}, u32[]{:S(2)}) collective-permute-start(f32[1,2048]{1,0:T(1,128)S(1)} %add_add_fusion.1), channel_id=1, source_target_pairs={{0,16},{4,20},{8,24},{12,28},{16,0},{20,4},{24,8},{28,12},{32,48},... | collective-permute-start | bytes 24584 | tf_op jit(solution)/shard_map/ppermute | solution.py:247
  205.2 5.0 %collective-permute-start.4 = (f32[1,2048]{1,0:T(1,128)S(1)}, f32[1,2048]{1,0:T(1,128)S(1)}, u32[]{:S(2)}, u32[]{:S(2)}) collective-permute-start(f32[1,2048]{1,0:T(1,128)S(1)} %add_add_fusion.1), channel_id=1, source_target_pairs={{0,8},{4,12},{8,0},{12,4},{16,24},{20,28},{24,16},{28,20},{32,40},... | collective-permute-start | bytes 24584 | tf_op jit(solution)/shard_map/ppermute | solution.py:247
  210.3 69.1 %all-to-all-start.2 = ((bf16[128,8,2048]{2,1,0:T(8,128)(2,1)}), bf16[128,8,2048]{2,1,0:T(8,128)(2,1)}, u32[]{:S(2)}, u32[]{:S(2)}) async-start(bf16[128,8,2048]{2,1,0:T(8,128)(2,1)} %bitcast.27), calls=%async_computation.2 | async-start | bytes 8388608 | tf_op jit(solution)/shard_map/all_to_all | solution.py:226
  225.7 48.1 %collective-permute-start.7 = (bf16[64,2048]{1,0:T(8,128)(2,1)}, bf16[64,2048]{1,0:T(8,128)(2,1)S(1)}, u32[]{:S(2)}, u32[]{:S(2)}) collective-permute-start(bf16[64,2048]{1,0:T(8,128)(2,1)} %norm_grad.1), channel_id=1, source_target_pairs={{0,1},{1,2},{2,3},{3,0},{4,5},{5,6},{6,7},{7,4},{8,9},{9,10},{10,1... | collective-permute-start | bytes 786440 | tf_op jit(solution)/shard_map/ppermute | solution.py:235
  226.6 40.6 %collective-permute-start.10 = (f32[1,2048]{1,0:T(1,128)S(1)}, f32[1,2048]{1,0:T(1,128)S(1)}, u32[]{:S(2)}, u32[]{:S(2)}) collective-permute-start(f32[1,2048]{1,0:T(1,128)S(1)} %add_add_fusion), channel_id=1, source_target_pairs={{0,32},{4,36},{8,40},{12,44},{16,48},{20,52},{24,56},{28,60},{32,0... | collective-permute-start | bytes 24584 | tf_op jit(solution)/shard_map/ppermute | solution.py:247
  228.7 50.7 %collective-permute-start.9 = (bf16[64,2048]{1,0:T(8,128)(2,1)}, bf16[64,2048]{1,0:T(8,128)(2,1)S(1)}, u32[]{:S(2)}, u32[]{:S(2)}) collective-permute-start(bf16[64,2048]{1,0:T(8,128)(2,1)} %norm_grad.1), channel_id=1, source_target_pairs={{0,2},{1,3},{2,0},{3,1},{4,6},{5,7},{6,4},{7,5},{8,10},{9,11},{10,... | collective-permute-start | bytes 786440 | tf_op jit(solution)/shard_map/ppermute | solution.py:235
  231.5 47.1 %collective-permute-start.8 = (bf16[64,2048]{1,0:T(8,128)(2,1)}, bf16[64,2048]{1,0:T(8,128)(2,1)S(1)}, u32[]{:S(2)}, u32[]{:S(2)}) collective-permute-start(bf16[64,2048]{1,0:T(8,128)(2,1)} %norm_grad.1), channel_id=1, source_target_pairs={{0,3},{1,0},{2,1},{3,2},{4,7},{5,4},{6,5},{7,6},{8,11},{9,8},{10,9... | collective-permute-start | bytes 786440 | tf_op jit(solution)/shard_map/ppermute | solution.py:235
  267.2 5.2 %collective-permute-start.11 = (f32[1,2048]{1,0:T(1,128)S(1)}, f32[1,2048]{1,0:T(1,128)S(1)}, u32[]{:S(2)}, u32[]{:S(2)}) collective-permute-start(f32[1,2048]{1,0:T(1,128)S(1)} %add.70), channel_id=1, source_target_pairs={{0,64},{4,68},{8,72},{12,76},{16,80},{20,84},{24,88},{28,92},{32,9... | collective-permute-start | bytes 24584 | tf_op jit(solution)/shard_map/ppermute | solution.py:247
  279.4 5.7 %copy-start = (bf16[256,2048]{1,0:T(8,128)(2,1)}, bf16[256,2048]{1,0:T(8,128)(2,1)S(1)}, u32[]{:S(2)}) copy-start(bf16[256,2048]{1,0:T(8,128)(2,1)S(1)} %constant_dynamic-update-slice_fusion) | copy-start | bytes 3145732

commit v4 on v1

--- a/solution.py
+++ b/solution.py
@@ -30,18 +30,24 @@
     return jnp.where(rank[:, None, :] == place, 1.0, 0.0)
 
 
-def pack_normed_kernel(quarter, ids_t, hidden, gain, buf, normed):
-    step = pl.program_id(0)
-    rows, count, cap = buf.shape[0], buf.shape[0] // 8, 8
-
-    @pl.when(step == 0)
-    def _():
-        values = hidden[...].astype(F32)
-        inverse = lax.rsqrt(jnp.mean(values * values, axis=-1, keepdims=True) + epsilon)
-        normed[...] = (values * inverse * gain[...]).astype(BF16)
-
-    chosen = slot_rows(ids_t[...], step * count, count, cap).reshape(rows, -1).astype(BF16)
-    buf[...] = jnp.dot(chosen, normed[...], preferred_element_type=F32).astype(BF16)
+def pack_normed_kernel(quarter, ids_t, hidden, gain, out, buf, sems):
+    chunks = sems.shape[0]
+    rows, cap = out.shape[0] // chunks, 8
+    count = rows // cap
+    values = hidden[...].astype(F32)
+    inverse = lax.rsqrt(jnp.mean(values * values, axis=-1, keepdims=True) + epsilon)
+    normed = (values * inverse * gain[...]).astype(BF16)
+    ids = ids_t[...]
+    copies = []
+    for chunk in range(chunks):
+        chosen = slot_rows(ids, chunk * count, count, cap).reshape(rows, -1).astype(BF16)
+        part = pl.ds(chunk * rows, rows)
+        buf[part, :] = jnp.dot(chosen, normed, preferred_element_type=F32).astype(BF16)
+        copy = pltpu.make_async_copy(buf.at[part], out.at[part], sems.at[chunk])
+        copy.start()
+        copies.append(copy)
+    for copy in copies:
+        copy.wait()
 
 
 def pack_scaled_kernel(ids_t, probs_t, grad, buf):
@@ -102,87 +108,89 @@
 
 
 def combine_kernel(
-    quarter, ids, routes, weights, rows, hidden, grad, layer_out, gate_grad, dots
+    quarter, ids, routes, weights, rows, hidden, grad, layer_out, gate_grad, total, found
 ):
     step = pl.program_id(0)
     tokens, top = ids.shape
-    slots = routes.shape[1]
+    slots = rows.shape[0]
+
+    @pl.when(step == 0)
+    def _():
+        total[...] = hidden[...].astype(F32)
+        found[...] = jnp.zeros_like(found)
+
     parts = jnp.dot(weights[...], rows[...], preferred_element_type=F32)
-    total = parts[:tokens] + parts[tokens : 2 * tokens] + parts[2 * tokens :]
-    layer_out[...] = (hidden[...].astype(F32) + total).astype(BF16)
-    part = lax.dot_general(
-        grad[...], rows[...], (((1,), (1,)), ((), ())), preferred_element_type=F32
-    )
+    total[...] += parts[:tokens] + parts[tokens : 2 * tokens] + parts[2 * tokens :]
+    dots = lax.dot_general(
+        rows[...], grad[...], (((1,), (1,)), ((), ())), preferred_element_type=F32
+    ).T
+    mine = jnp.where(routes[...].astype(F32) > 0.0, dots, 0.0)
+    expert = (lax.broadcasted_iota(jnp.int32, (tokens, slots), 1) + step * slots) // 8
+    column = lax.broadcasted_iota(jnp.int32, found.shape, 1)
+    sums = found[...]
+    for k in range(top):
+        own = jnp.where(expert == ids[:, k : k + 1], mine, 0.0)
+        sums = sums + jnp.where(column == k, jnp.sum(own, axis=1, keepdims=True), 0.0)
+    found[...] = sums
+
+    @pl.when(step == pl.num_programs(0) - 1)
+    def _():
+        layer_out[...] = total[...].astype(BF16)
+        gate_grad[...] = found[...].T[:top, :]
+
+
+def norm_grad_kernel(quarter, routes, rows, hidden, gain, grad, own_grad, group_grad, total):
+    step = pl.program_id(0)
+    part = jnp.dot(routes[...], rows[...], preferred_element_type=F32)
 
     @pl.when(step == 0)
     def _():
-        dots[...] = part
+        total[...] = part
 
     @pl.when(step > 0)
     def _():
-        dots[...] += part
-
-    @pl.when(step == pl.num_programs(0) - 1)
-    def _():
-        mine = jnp.where(routes[...].astype(F32) > 0.0, dots[...], 0.0)
-        expert = lax.broadcasted_iota(jnp.int32, (tokens, slots), 1) // 8
-        column = lax.broadcasted_iota(jnp.int32, (tokens, 128), 1)
-        found = jnp.zeros((tokens, 128), F32)
-        for k in range(top):
-            own = jnp.where(expert == ids[:, k : k + 1], mine, 0.0)
-            found = found + jnp.where(column == k, jnp.sum(own, axis=1, keepdims=True), 0.0)
-        gate_grad[...] = found.T[:top, :]
-
-
-def norm_grad_kernel(quarter, routes, rows, hidden, gain, grad, own_grad, gain_part, total):
-    step = pl.program_id(0)
-
-    @pl.when(step == 0)
-    def _():
-        total[...] = jnp.zeros_like(total)
-
-    total[...] += jnp.dot(routes[...], rows[...], preferred_element_type=F32)
+        total[...] += part
 
     @pl.when(step == pl.num_programs(0) - 1)
     def _():
         values = hidden[...].astype(F32)
         inverse = lax.rsqrt(jnp.mean(values * values, axis=-1, keepdims=True) + epsilon)
         unit = values * inverse
-        summed = total[...]
-        gain_part[...] = jnp.sum(summed * unit, axis=0, keepdims=True)
-        upstream = summed * gain[...]
-        own_grad[...] = (
+        upstream = total[...] * gain[...]
+        result = (
             grad[...].astype(F32)
             + inverse * (upstream - unit * jnp.mean(upstream * unit, axis=-1, keepdims=True))
         ).astype(BF16)
+        own_grad[...] = result
+        group_grad[...] = result
 
 
 def exchange(block):
     return lax.all_to_all(block, AXES, split_axis=0, concat_axis=0, tiled=True)
 
 
-def gather_group(block):
+def gather_group(block, whole):
     size = lax.axis_size("tensor")
     mine = lax.axis_index("tensor")
     rows = block.shape[0]
-    whole = jnp.zeros((size * rows, block.shape[1]), block.dtype)
-    moved = [(0, block)] + [
+    moved = [
         (step, lax.ppermute(block, "tensor", [(i, (i + step) % size) for i in range(size)]))
         for step in (1, 3, 2)
     ]
     for step, piece in moved:
-        origin = (mine - step) % size
+        origin = (mine + size - step) % size
         whole = lax.dynamic_update_slice_in_dim(whole, piece, origin * rows, 0)
     return whole
 
 
-def sum_all(value):
-    for axis in AXES:
-        size = lax.axis_size(axis)
-        step = 1
-        while step < size:
-            value = value + lax.ppermute(value, axis, [(i, i ^ step) for i in range(size)])
-            step *= 2
+def add_from(value, axis, distances):
+    size = lax.axis_size(axis)
+    others = [
+        lax.ppermute(value, axis, [(i, i ^ distance) for i in range(size)])
+        for distance in distances
+    ]
+    for other in others:
+        value = value + other
     return value
 
 
@@ -223,14 +231,17 @@
         pack_normed_kernel,
         grid_spec=pltpu.PrefetchScalarGridSpec(
             num_scalar_prefetch=1,
-            grid=(steps,),
+            grid=(1,),
             in_specs=[
                 whole(top, own),
                 pl.BlockSpec((own, width), lambda i, q: (q[0], 0)),
                 whole(1, width),
             ],
-            out_specs=pl.BlockSpec((slots // steps, width), lambda i, q: (i, 0)),
-            scratch_shapes=[pltpu.VMEM((own, width), BF16)],
+            out_specs=pl.BlockSpec(memory_space=pl.ANY),
+            scratch_shapes=[
+                pltpu.VMEM((slots, width), BF16),
+                pltpu.SemaphoreType.DMA((steps,)),
+            ],
         ),
         out_shape=jax.ShapeDtypeStruct((slots, width), BF16),
         compiler_params=params(),
@@ -272,6 +283,8 @@
     gate_pre, up_pre, act, cotan, result = lax.optimization_barrier(
         (gate_pre, up_pre, act, cotan, result)
     )
+    returned = exchange(result)
+
     sigma = jax.nn.sigmoid(gate_pre)
     silu_vals = gate_pre * sigma
     act_grad = dot(cotan, down_w, ((1,), (1,)))
@@ -279,8 +292,12 @@
     up_pgrad = (act_grad * silu_vals).astype(BF16)
     back = dot(gate_pgrad, gate_w, ((1,), (1,))) + dot(up_pgrad, up_w, ((1,), (1,)))
     back = back.astype(BF16)
+    gain_part = jnp.sum(back.astype(F32) * inputs.astype(F32), axis=0, keepdims=True) / gain
+    gain_part = add_from(gain_part, "dp", (1,))
+    gain_part = add_from(gain_part, "tensor", (1, 2, 3))
+    back, returned, gain_part = lax.optimization_barrier((back, returned, gain_part))
     back_rows = exchange(back)
-    returned = exchange(after(result, back_rows))
+    gain_part = add_from(gain_part, "dp", (2, 4, 6))
 
     gate_pgrad, up_pgrad, act_late = lax.optimization_barrier(
         (gate_pgrad, up_pgrad, act, back)
@@ -289,52 +306,22 @@
     up_wgrad = dot(inputs, up_pgrad, ((0,), (0,))).astype(BF16)
     down_grad = dot(act_late, cotan, ((0,), (0,))).astype(BF16)
 
-    own_grad, gain_part = pl.pallas_call(
-        norm_grad_kernel,
-        grid_spec=pltpu.PrefetchScalarGridSpec(
-            num_scalar_prefetch=1,
-            grid=(steps,),
-            in_specs=[
-                pl.BlockSpec((own, slots // steps), lambda i, q: (0, i)),
-                pl.BlockSpec((slots // steps, width), lambda i, q: (i, 0)),
-                pl.BlockSpec((own, width), lambda i, q: (q[0], 0)),
-                whole(1, width),
-                whole(own, width),
-            ],
-            out_specs=[whole(own, width), whole(1, width)],
-            scratch_shapes=[pltpu.VMEM((own, width), F32)],
-        ),
-        out_shape=[
-            jax.ShapeDtypeStruct((own, width), BF16),
-            jax.ShapeDtypeStruct((1, width), F32),
-        ],
-        compiler_params=params(),
-        cost_estimate=cost(2 * own * slots * width, 2 * slots * width),
-        name="norm_grad",
-    )(quarter, routes, back_rows, hidden, gain, out_grad)
-    input_grad = gather_group(own_grad)
-    gain_grad = sum_all(gain_part)[0]
-
-    parts = 2
-    columns = width // parts
+    halves = 2
     layer_out, gate_grad_t = pl.pallas_call(
         combine_kernel,
         grid_spec=pltpu.PrefetchScalarGridSpec(
             num_scalar_prefetch=1,
-            grid=(parts,),
+            grid=(halves,),
             in_specs=[
                 whole(own, top),
-                whole(own, slots),
-                whole(3 * own, slots),
-                pl.BlockSpec((slots, columns), lambda i, q: (0, i)),
-                pl.BlockSpec((own, columns), lambda i, q: (q[0], i)),
-                pl.BlockSpec((own, columns), lambda i, q: (0, i)),
+                pl.BlockSpec((own, slots // halves), lambda i, q: (0, i)),
+                pl.BlockSpec((3 * own, slots // halves), lambda i, q: (0, i)),
+                pl.BlockSpec((slots // halves, width), lambda i, q: (i, 0)),
+                pl.BlockSpec((own, width), lambda i, q: (q[0], 0)),
+                whole(own, width),
             ],
-            out_specs=[
-                pl.BlockSpec((own, columns), lambda i, q: (0, i)),
-                whole(top, own),
-            ],
-            scratch_shapes=[pltpu.VMEM((own, slots), F32)],
+            out_specs=[whole(own, width), whole(top, own)],
+            scratch_shapes=[pltpu.VMEM((own, width), F32), pltpu.VMEM((own, 128), F32)],
         ),
         out_shape=[
             jax.ShapeDtypeStruct((own, width), BF16),
@@ -344,6 +331,37 @@
         cost_estimate=cost(8 * own * slots * width, 2 * slots * width),
         name="combine",
     )(quarter, expert_ids, routes, weights, returned, hidden, out_grad)
+
+    back_rows, gate_wgrad, up_wgrad, down_grad, layer_out, gate_grad_t, gain_part = (
+        lax.optimization_barrier(
+            (back_rows, gate_wgrad, up_wgrad, down_grad, layer_out, gate_grad_t, gain_part)
+        )
+    )
+    gain_grad = add_from(add_from(gain_part, "dp", (8,)), "dp", (16,))[0]
+    own_grad, group_grad = pl.pallas_call(
+        norm_grad_kernel,
+        grid_spec=pltpu.PrefetchScalarGridSpec(
+            num_scalar_prefetch=1,
+            grid=(halves,),
+            in_specs=[
+                pl.BlockSpec((own, slots // halves), lambda i, q: (0, i)),
+                pl.BlockSpec((slots // halves, width), lambda i, q: (i, 0)),
+                pl.BlockSpec((own, width), lambda i, q: (q[0], 0)),
+                whole(1, width),
+                whole(own, width),
+            ],
+            out_specs=[whole(own, width), pl.BlockSpec((own, width), lambda i, q: (q[0], 0))],
+            scratch_shapes=[pltpu.VMEM((own, width), F32)],
+        ),
+        out_shape=[
+            jax.ShapeDtypeStruct((own, width), BF16),
+            jax.ShapeDtypeStruct(hidden.shape, BF16),
+        ],
+        compiler_params=params(),
+        cost_estimate=cost(2 * own * slots * width, 2 * slots * width),
+        name="norm_grad",
+    )(quarter, routes, back_rows, hidden, gain, out_grad)
+    input_grad = gather_group(own_grad, group_grad)
     return (
         layer_out,
         input_grad,

time: 309 us -> 265 us (0.86)
  blocking collectives: 57.8 us -> 0 us
  waiting for transfers between devices: 109 us -> 130 us
  starting transfers between devices: 50.2 us -> 44.3 us
  matrix products: 57.5 us -> 61.9 us
    all_to_all x1 -> x0, blocking collectives: 57.8 us -> none  [exchange(): return lax.all_to_all(block, AXES, split_axis=0, concat_axis=0, tiled=True)]
    all_to_all x3 -> x4, waiting for transfers between devices: 78.6 us -> 103 us  [exchange(): return lax.all_to_all(block, AXES, split_axis=0, concat_axis=0, tiled=True)]
    ppermute x3, starting transfers between devices: 16.8 us -> 4.22 us  [gather_group(): lax.ppermute(block, 'tensor', [(i, (i + step) % size) for i in range(size)])]
    all_to_all x3 -> x4, starting transfers between devices: 23.7 us -> 29.7 us  [exchange(): return lax.all_to_all(block, AXES, split_axis=0, concat_axis=0, tiled=True)]
    ppermute x7 -> x9, waiting for transfers between devices: 30.4 us -> 25.9 us  [add_from(): lax.ppermute(value, axis, [(i, i ^ distance) for i in range(size)])]
    dot_general x9, matrix products: 57.5 us -> 61.9 us  [dot(): return lax.dot_general(a, b, (dims, ((), ())), preferred_element_type=F32)]
    ppermute x7 -> x9, starting transfers between devices: 9.68 us -> 10.4 us  [add_from(): lax.ppermute(value, axis, [(i, i ^ distance) for i in range(size)])]
  transfers between devices with their start and end apart: 13 -> 16, of which waited for: 7 -> 12; matrix products, arithmetic and copies ran while one was open for 16% -> 25% of each run, Pallas kernels for 4% -> 5%
where the time goes in v4:
time: 265 us
  waiting for transfers between devices  130 us (49%)
  matrix products  61.9 us (23%)
  starting transfers between devices  44.3 us (17%)
  Pallas kernels  20.3 us (8%)
  local copies, waits for them, and re-layouts  6.39 us (2%)
    all_to_all x4, waiting for transfers between devices, exchange(): return lax.all_to_all(block, AXES, split_axis=0, concat_axis=0, tiled=True)  103 us
    dot_general x9, matrix products, dot(): return lax.dot_general(a, b, (dims, ((), ())), preferred_element_type=F32)  61.9 us
    all_to_all x4, starting transfers between devices, exchange(): return lax.all_to_all(block, AXES, split_axis=0, concat_axis=0, tiled=True)  29.7 us
    ppermute x9, waiting for transfers between devices, add_from(): lax.ppermute(value, axis, [(i, i ^ distance) for i in range(size)])  25.9 us
    ppermute x9, starting transfers between devices, add_from(): lax.ppermute(value, axis, [(i, i ^ distance) for i in range(size)])  10.4 us
    pallas_call x1, Pallas kernels, per_device(): pl.pallas_call(combine_kernel, grid_spec=pltpu.PrefetchScalarGridSpec(num...  5.36 us
  transfers between devices with their start and end apart: 16, of which 12 were waited for; matrix products, arithmetic and copies ran while one was open for 25% of the time, Pallas kernels for 5%

profile of v4, /device:TPU:0, one launch (start us, length us, event | category | flops | bytes accessed | tf_op | source)
XLA Modules:
  0.0 264.7 jit_solution(3775025527702302170)
XLA Ops:
  0.7 4.0 %pack_normed.1 = bf16[1024,2048]{1,0:T(8,128)(2,1)} custom-call(s32[1]{0:T(128)} %bitcast.quarter, s32[8,64]{1,0:T(8,128)} %bitcast.64, bf16[256,2048]{1,0:T(8,128)(2,1)} %hidden.5, f32[1,2048]{1,0:T(1,128)} %bitcast.62), custom_call_target="tpu_custom_call" | custom-call | flops 268435456 | bytes 4194304 | tf_op jit(solution)/shard_map/pack_normed/pallas_call | solution.py:230
  4.7 11.7 %all-to-all-start = ((bf16[128,8,2048]{2,1,0:T(8,128)(2,1)}), bf16[128,8,2048]{2,1,0:T(8,128)(2,1)}, u32[]{:S(2)}, u32[]{:S(2)}) async-start(bf16[128,8,2048]{2,1,0:T(8,128)(2,1)} %bitcast.59), calls=%async_computation | async-start | bytes 8388608 | tf_op jit(solution)/shard_map/all_to_all | solution.py:169
  16.4 4.7 %pack_scaled.1 = bf16[1024,2048]{1,0:T(8,128)(2,1)} custom-call(s32[8,64]{1,0:T(8,128)} %bitcast.65, f32[8,64]{1,0:T(8,128)} %bitcast.68, bf16[64,2048]{1,0:T(8,128)(2,1)} %grad.5), custom_call_target="tpu_custom_call" | custom-call | flops 268435456 | bytes 4194304 | tf_op jit(solution)/shard_map/pack_scaled/pallas_call | solution.py:253
  21.1 47.5 %all-to-all-done = bf16[128,8,2048]{2,1,0:T(8,128)(2,1)} async-done(((bf16[128,8,2048]{2,1,0:T(8,128)(2,1)}), bf16[128,8,2048]{2,1,0:T(8,128)(2,1)}, u32[]{:S(2)}, u32[]{:S(2)}) %all-to-all-start) | async-done | bytes 4194336 | tf_op jit(solution)/shard_map/all_to_all | solution.py:169
  68.6 5.8 %all-to-all-start.1 = ((bf16[128,8,2048]{2,1,0:T(8,128)(2,1)}), bf16[128,8,2048]{2,1,0:T(8,128)(2,1)}, u32[]{:S(2)}, u32[]{:S(2)}) async-start(bf16[128,8,2048]{2,1,0:T(8,128)(2,1)} %bitcast.58), calls=%async_computation.1 | async-start | bytes 8388608 | tf_op jit(solution)/shard_map/all_to_all | solution.py:169
  74.4 6.1 %fusion.8 = f32[1024,768]{1,0:T(8,128)S(1)} fusion(bf16[1,2048,768]{2,1,0:T(8,128)(2,1)} %param.13, bf16[128,8,2048]{2,1,0:T(8,128)(2,1)} %all-to-all-done), kind=kOutput, calls=%fused_computation.14 | convolution fusion | flops 3221225472 | bytes 10485760 | tf_op jit(solution)/shard_map/dot_general | solution.py:210
  80.6 8.6 %multiply_convert_fusion.2 = (bf16[1024,768]{1,0:T(8,128)(2,1)S(1)}, f32[1024,768]{1,0:T(8,128)}) fusion(f32[1024,768]{1,0:T(8,128)S(1)} %fusion.8, bf16[1,2048,768]{2,1,0:T(8,128)(2,1)S(1)} %copy-done, bf16[128,8,2048]{2,1,0:T(8,128)(2,1)} %all-to-all-done), kind=kOutput, calls=%fused_computation.19 | convolution fusion | flops 3225944064 | bytes 15204352 | tf_op jit(solution)/shard_map/dot_general | solution.py:210
  89.2 1.1 copy-done.8
  90.3 5.0 %convolution_convert_fusion = bf16[1024,2048]{1,0:T(8,128)(2,1)} fusion(bf16[1024,768]{1,0:T(8,128)(2,1)S(1)} %get-tuple-element.44, bf16[1,768,2048]{2,1,0:T(8,128)(2,1)S(1)} %copy-done.4), kind=kOutput, calls=%fused_computation.2 | convolution fusion | flops 3223322624 | bytes 8912896 | tf_op jit(solution)/shard_map/dot_general | solution.py:210
  95.3 31.3 %all-to-all-done.1 = bf16[128,8,2048]{2,1,0:T(8,128)(2,1)} async-done(((bf16[128,8,2048]{2,1,0:T(8,128)(2,1)}), bf16[128,8,2048]{2,1,0:T(8,128)(2,1)}, u32[]{:S(2)}, u32[]{:S(2)}) %all-to-all-start.1) | async-done | bytes 4194336 | tf_op jit(solution)/shard_map/all_to_all | solution.py:169
  126.6 6.0 %all-to-all-start.2 = ((bf16[128,8,2048]{2,1,0:T(8,128)(2,1)}), bf16[128,8,2048]{2,1,0:T(8,128)(2,1)}, u32[]{:S(2)}, u32[]{:S(2)}) async-start(bf16[128,8,2048]{2,1,0:T(8,128)(2,1)} %bitcast.61), calls=%async_computation.2 | async-start | bytes 8388608 | tf_op jit(solution)/shard_map/all_to_all | solution.py:169
  132.7 9.3 %multiply_convert_fusion = (bf16[1024,768]{1,0:T(8,128)(2,1)S(1)}, bf16[1024,768]{1,0:T(8,128)(2,1)S(1)}) fusion(f32[1024,768]{1,0:T(8,128)} %copy-done.11, f32[1024,768]{1,0:T(8,128)} %get-tuple-element.37, bf16[1024,2048]{1,0:T(8,128)(2,1)} %bitcast.9, bf16[1,768,2048]{2,1,0:T(8,128)(2,1)} %param.15), kind=kOutput, calls=%fused_computation.16 | convolution fusion | flops 3231449088 | bytes 16777216 | tf_op jit(solution)/shard_map/dot_general | solution.py:210
  142.0 3.4 %fusion.6 = f32[1024,2048]{1,0:T(8,128)S(1)} fusion(bf16[1024,768]{1,0:T(8,128)(2,1)S(1)} %get-tuple-element.42, bf16[1,2048,768]{2,1,0:T(8,128)(2,1)S(1)} %copy-done.5), kind=kOutput, calls=%fused_computation.12 | convolution fusion | flops 3221225472 | bytes 13107200 | tf_op jit(solution)/shard_map/dot_general | solution.py:210
  145.5 6.8 %multiply_reduce_fusion = (f32[2048]{0:T(1024)S(1)}, bf16[1024,2048]{1,0:T(8,128)(2,1)}) fusion(bf16[128,8,2048]{2,1,0:T(8,128)(2,1)} %all-to-all-done, f32[1024,2048]{1,0:T(8,128)S(1)} %fusion.6, bf16[1024,768]{1,0:T(8,128)(2,1)S(1)} %get-tuple-element.43, bf16[1,2048,768]{2,1,0:T(8,128)(2,1)S(1)} %copy-done), kind=kOutput, calls=%fused_computation | convolution fusion | flops 3233806336 | bytes 21504000 | tf_op jit(solution)/shard_map/dot_general | solution.py:210
  152.4 1.2 collective-permute-done
  153.5 2.1 collective-permute-start.3
  155.6 0.8 collective-permute-start.2
  156.4 1.3 collective-permute-start.1
  157.7 13.0 %collective-permute-done.3 = f32[1,2048]{1,0:T(1,128)S(1)} collective-permute-done((f32[1,2048]{1,0:T(1,128)S(1)}, f32[1,2048]{1,0:T(1,128)S(1)}, u32[]{:S(2)}, u32[]{:S(2)}) %collective-permute-start.3) | collective-permute-done | bytes 8224 | tf_op jit(solution)/shard_map/ppermute | solution.py:189
  170.7 2.6 collective-permute-done.2
  173.3 3.3 %collective-permute-done.1 = f32[1,2048]{1,0:T(1,128)S(1)} collective-permute-done((f32[1,2048]{1,0:T(1,128)S(1)}, f32[1,2048]{1,0:T(1,128)S(1)}, u32[]{:S(2)}, u32[]{:S(2)}) %collective-permute-start.1) | collective-permute-done | bytes 8224 | tf_op jit(solution)/shard_map/ppermute | solution.py:189
  176.7 8.0 %all-to-all-done.2 = bf16[128,8,2048]{2,1,0:T(8,128)(2,1)} async-done(((bf16[128,8,2048]{2,1,0:T(8,128)(2,1)}), bf16[128,8,2048]{2,1,0:T(8,128)(2,1)}, u32[]{:S(2)}, u32[]{:S(2)}) %all-to-all-start.2) | async-done | bytes 4194336 | tf_op jit(solution)/shard_map/all_to_all | solution.py:169
  184.7 6.1 %all-to-all-start.3 = ((bf16[128,8,2048]{2,1,0:T(8,128)(2,1)}), bf16[128,8,2048]{2,1,0:T(8,128)(2,1)}, u32[]{:S(2)}, u32[]{:S(2)}) async-start(bf16[128,8,2048]{2,1,0:T(8,128)(2,1)} %bitcast.60), calls=%async_computation.3 | async-start | bytes 8388608 | tf_op jit(solution)/shard_map/all_to_all | solution.py:169
  190.8 0.7 copy.16.probs
  191.5 0.7 copy.17.ids
  192.2 0.7 copy.15.ids
  192.9 2.1 routes.1
  195.0 2.8 %collective-permute-start.6 = (f32[1,2048]{1,0:T(1,128)S(1)}, f32[1,2048]{1,0:T(1,128)S(1)}, u32[]{:S(2)}, u32[]{:S(2)}) collective-permute-start(f32[1,2048]{1,0:T(1,128)S(1)} %add_add_fusion.1), channel_id=1, source_target_pairs={{0,24},{4,28},{8,16},{12,20},{16,8},{20,12},{24,0},{28,4},{32,56},... | collective-permute-start | bytes 24584 | tf_op jit(solution)/shard_map/ppermute | solution.py:189
  198.1 1.0 collective-permute-start.4
  199.1 7.8 %convolution_convert_fusion.1 = bf16[768,2048]{1,0:T(8,128)(2,1)} fusion(bf16[1024,768]{1,0:T(8,128)(2,1)} %copy-done.8, bf16[1024,2048]{1,0:T(8,128)(2,1)} %bitcast.9), kind=kOutput, calls=%fused_computation.3 | convolution fusion | flops 3222798336 | bytes 8912896 | tf_op jit(solution)/shard_map/dot_general | solution.py:210
  206.9 7.5 %convolution_convert_fusion.3 = bf16[2048,768]{1,0:T(8,128)(2,1)} fusion(bf16[1024,768]{1,0:T(8,128)(2,1)S(1)} %copy-done.10, bf16[128,8,2048]{2,1,0:T(8,128)(2,1)} %all-to-all-done), kind=kOutput, calls=%fused_computation.5 | convolution fusion | flops 3222798336 | bytes 8912896 | tf_op jit(solution)/shard_map/dot_general | solution.py:210
  214.4 7.4 %convolution_convert_fusion.2 = bf16[2048,768]{1,0:T(8,128)(2,1)} fusion(bf16[1024,768]{1,0:T(8,128)(2,1)S(1)} %copy-done.7, bf16[128,8,2048]{2,1,0:T(8,128)(2,1)} %all-to-all-done), kind=kOutput, calls=%fused_computation.4 | convolution fusion | flops 3222798336 | bytes 8912896 | tf_op jit(solution)/shard_map/dot_general | solution.py:210
  221.8 5.4 %combine.1 = (bf16[64,2048]{1,0:T(8,128)(2,1)}, f32[8,64]{1,0:T(8,128)}) custom-call(s32[1]{0:T(128)} %bitcast.quarter, s32[64,8]{1,0:T(8,128)} %copy.17.ids, bf16[64,1024]{1,0:T(8,128)(2,1)} %get-tuple-element.46.routes, bf16[192,1024]{1,0:T(8,128)(2,1)} %get-tuple-element.47.weights, bf16[1024,2048]{1,0:T(8,128)(2,1)} %bitcast.12.rows, ...), custom_call_target="tpu_custom_call" | custom-call | flops 1073741824 | bytes 4194304 | tf_op jit(solution)/shard_map/combine/pallas_call | solution.py:310
  227.2 15.8 %all-to-all-done.3 = bf16[128,8,2048]{2,1,0:T(8,128)(2,1)} async-done(((bf16[128,8,2048]{2,1,0:T(8,128)(2,1)}), bf16[128,8,2048]{2,1,0:T(8,128)(2,1)}, u32[]{:S(2)}, u32[]{:S(2)}) %all-to-all-start.3) | async-done | bytes 4194336 | tf_op jit(solution)/shard_map/all_to_all | solution.py:169
  243.0 4.1 %norm_grad.1 = (bf16[64,2048]{1,0:T(8,128)(2,1)}, bf16[256,2048]{1,0:T(8,128)(2,1)}) custom-call(s32[1]{0:T(128)} %bitcast.quarter, bf16[64,1024]{1,0:T(8,128)(2,1)} %get-tuple-element.46.routes, bf16[1024,2048]{1,0:T(8,128)(2,1)} %bitcast.15.rows, bf16[256,2048]{1,0:T(8,128)(2,1)} %hidden.5, f32[1,2048]{1,0:T(1,128)} %bitcast.63, bf16[64,2048]{1,0:T(8,128)(2,1)} %grad.5), custom_call_target="tpu_custom_call" | custom-call | flops 268435456 | bytes 4194304 | tf_op jit(solution)/shard_map/norm_grad/pallas_call | solution.py:341
  247.1 0.6 collective-permute-start.7
  247.7 2.6 collective-permute-start.8
  250.3 0.6 collective-permute-start.10
  251.0 3.0 %collective-permute-done.10 = f32[1,2048]{1,0:T(1,128)S(1)} collective-permute-done((f32[1,2048]{1,0:T(1,128)S(1)}, f32[1,2048]{1,0:T(1,128)S(1)}, u32[]{:S(2)}, u32[]{:S(2)}) %collective-permute-start.10) | collective-permute-done | bytes 8224 | tf_op jit(solution)/shard_map/ppermute | solution.py:189
  254.0 1.5 collective-permute-start.11
  255.5 1.0 collective-permute-start.9
  256.5 2.8 %collective-permute-done.11 = f32[1,2048]{1,0:T(1,128)S(1)} collective-permute-done((f32[1,2048]{1,0:T(1,128)S(1)}, f32[1,2048]{1,0:T(1,128)S(1)}, u32[]{:S(2)}, u32[]{:S(2)}) %collective-permute-start.11) | collective-permute-done | bytes 8224 | tf_op jit(solution)/shard_map/ppermute | solution.py:189
  259.2 0.6 add.88
  259.9 1.7 constant_dynamic-update-slice_fusion.2
  261.5 0.5 collective-permute-done.8
  262.0 0.7 constant_dynamic-update-slice_fusion.1
  262.8 1.2 collective-permute-done.9
  264.0 0.7 constant_dynamic-update-slice_fusion
  (34 shorter events, 0.5 us)
Async XLA Ops:
  0.6 79.9 %copy-start = (bf16[1,2048,768]{2,1,0:T(8,128)(2,1)S(1)}, bf16[1,2048,768]{2,1,0:T(8,128)(2,1)}, u32[]{:S(2)}) copy-start(bf16[1,2048,768]{2,1,0:T(8,128)(2,1)} %param.14) | copy-start | bytes 9437188
  4.7 63.9 %all-to-all-start = ((bf16[128,8,2048]{2,1,0:T(8,128)(2,1)}), bf16[128,8,2048]{2,1,0:T(8,128)(2,1)}, u32[]{:S(2)}, u32[]{:S(2)}) async-start(bf16[128,8,2048]{2,1,0:T(8,128)(2,1)} %bitcast.59), calls=%async_computation | async-start | bytes 8388608 | tf_op jit(solution)/shard_map/all_to_all | solution.py:169
  68.6 58.1 %all-to-all-start.1 = ((bf16[128,8,2048]{2,1,0:T(8,128)(2,1)}), bf16[128,8,2048]{2,1,0:T(8,128)(2,1)}, u32[]{:S(2)}, u32[]{:S(2)}) async-start(bf16[128,8,2048]{2,1,0:T(8,128)(2,1)} %bitcast.58), calls=%async_computation.1 | async-start | bytes 8388608 | tf_op jit(solution)/shard_map/all_to_all | solution.py:169
  80.6 8.6 %copy-start.11 = (f32[1024,768]{1,0:T(8,128)}, f32[1024,768]{1,0:T(8,128)S(1)}, u32[]{:S(2)}) copy-start(f32[1024,768]{1,0:T(8,128)S(1)} %fusion.8) | copy-start | bytes 9437188
  80.6 9.8 %copy-start.4 = (bf16[1,768,2048]{2,1,0:T(8,128)(2,1)S(1)}, bf16[1,768,2048]{2,1,0:T(8,128)(2,1)}, u32[]{:S(2)}) copy-start(bf16[1,768,2048]{2,1,0:T(8,128)(2,1)} %param.15) | copy-start | bytes 9437188
  89.2 1.1 copy-start.8
  126.6 58.1 %all-to-all-start.2 = ((bf16[128,8,2048]{2,1,0:T(8,128)(2,1)}), bf16[128,8,2048]{2,1,0:T(8,128)(2,1)}, u32[]{:S(2)}, u32[]{:S(2)}) async-start(bf16[128,8,2048]{2,1,0:T(8,128)(2,1)} %bitcast.61), calls=%async_computation.2 | async-start | bytes 8388608 | tf_op jit(solution)/shard_map/all_to_all | solution.py:169
  132.7 9.3 %copy-start.5 = (bf16[1,2048,768]{2,1,0:T(8,128)(2,1)S(1)}, bf16[1,2048,768]{2,1,0:T(8,128)(2,1)}, u32[]{:S(2)}) copy-start(bf16[1,2048,768]{2,1,0:T(8,128)(2,1)} %param.13) | copy-start | bytes 9437188
  142.0 3.5 %copy-start.9 = (bf16[1024,768]{1,0:T(8,128)(2,1)}, bf16[1024,768]{1,0:T(8,128)(2,1)S(1)}, u32[]{:S(2)}) copy-start(bf16[1024,768]{1,0:T(8,128)(2,1)S(1)} %get-tuple-element.42) | copy-start | bytes 4718596
  142.0 3.5 %copy-start.6 = (bf16[1024,768]{1,0:T(8,128)(2,1)}, bf16[1024,768]{1,0:T(8,128)(2,1)S(1)}, u32[]{:S(2)}) copy-start(bf16[1024,768]{1,0:T(8,128)(2,1)S(1)} %get-tuple-element.43) | copy-start | bytes 4718596
  145.5 6.8 %copy-start.1 = (f32[2048]{0:T(1024)S(1)}, f32[2048]{0:T(1024)}, u32[]{:S(2)}) copy-start(f32[2048]{0:T(1024)} %param.9) | copy-start | bytes 24580
  152.3 1.3 collective-permute-start
  153.5 17.2 %collective-permute-start.3 = (f32[1,2048]{1,0:T(1,128)S(1)}, f32[1,2048]{1,0:T(1,128)S(1)}, u32[]{:S(2)}, u32[]{:S(2)}) collective-permute-start(f32[1,2048]{1,0:T(1,128)S(1)} %add.74), channel_id=1, source_target_pairs={{0,3},{1,2},{2,1},{3,0},{4,7},{5,6},{6,5},{7,4},{8,11},{9,10},{10,... | collective-permute-start | bytes 24584 | tf_op jit(solution)/shard_map/ppermute | solution.py:189
  155.6 17.7 %collective-permute-start.2 = (f32[1,2048]{1,0:T(1,128)S(1)}, f32[1,2048]{1,0:T(1,128)S(1)}, u32[]{:S(2)}, u32[]{:S(2)}) collective-permute-start(f32[1,2048]{1,0:T(1,128)S(1)} %add.74), channel_id=1, source_target_pairs={{0,2},{1,3},{2,0},{3,1},{4,6},{5,7},{6,4},{7,5},{8,10},{9,11},{10,... | collective-permute-start | bytes 24584 | tf_op jit(solution)/shard_map/ppermute | solution.py:189
  156.4 20.2 %collective-permute-start.1 = (f32[1,2048]{1,0:T(1,128)S(1)}, f32[1,2048]{1,0:T(1,128)S(1)}, u32[]{:S(2)}, u32[]{:S(2)}) collective-permute-start(f32[1,2048]{1,0:T(1,128)S(1)} %add.74), channel_id=1, source_target_pairs={{0,1},{1,0},{2,3},{3,2},{4,5},{5,4},{6,7},{7,6},{8,9},{9,8},{10,11... | collective-permute-start | bytes 24584 | tf_op jit(solution)/shard_map/ppermute | solution.py:189
  184.7 6.1 %copy-start.3 = (f32[64,8]{0,1:T(8,128)S(1)}, f32[64,8]{0,1:T(8,128)}, u32[]{:S(2)}) copy-start(f32[64,8]{0,1:T(8,128)} %param.11) | copy-start | bytes 6148
  184.7 6.8 %copy-start.2 = (s32[64,8]{0,1:T(8,128)S(1)}, s32[64,8]{0,1:T(8,128)}, u32[]{:S(2)}) copy-start(s32[64,8]{0,1:T(8,128)} %param.10) | copy-start | bytes 6148
  184.7 58.3 %all-to-all-start.3 = ((bf16[128,8,2048]{2,1,0:T(8,128)(2,1)}), bf16[128,8,2048]{2,1,0:T(8,128)(2,1)}, u32[]{:S(2)}, u32[]{:S(2)}) async-start(bf16[128,8,2048]{2,1,0:T(8,128)(2,1)} %bitcast.60), calls=%async_computation.3 | async-start | bytes 8388608 | tf_op jit(solution)/shard_map/all_to_all | solution.py:169
  195.0 11.9 %copy-start.10 = (bf16[1024,768]{1,0:T(8,128)(2,1)S(1)}, bf16[1024,768]{1,0:T(8,128)(2,1)}, u32[]{:S(2)}) copy-start(bf16[1024,768]{1,0:T(8,128)(2,1)} %copy-done.9) | copy-start | bytes 4718596
  195.0 32.2 %collective-permute-start.6 = (f32[1,2048]{1,0:T(1,128)S(1)}, f32[1,2048]{1,0:T(1,128)S(1)}, u32[]{:S(2)}, u32[]{:S(2)}) collective-permute-start(f32[1,2048]{1,0:T(1,128)S(1)} %add_add_fusion.1), channel_id=1, source_target_pairs={{0,24},{4,28},{8,16},{12,20},{16,8},{20,12},{24,0},{28,4},{32,56},... | collective-permute-start | bytes 24584 | tf_op jit(solution)/shard_map/ppermute | solution.py:189
  197.7 29.4 %collective-permute-start.5 = (f32[1,2048]{1,0:T(1,128)S(1)}, f32[1,2048]{1,0:T(1,128)S(1)}, u32[]{:S(2)}, u32[]{:S(2)}) collective-permute-start(f32[1,2048]{1,0:T(1,128)S(1)} %add_add_fusion.1), channel_id=1, source_target_pairs={{0,16},{4,20},{8,24},{12,28},{16,0},{20,4},{24,8},{28,12},{32,48},... | collective-permute-start | bytes 24584 | tf_op jit(solution)/shard_map/ppermute | solution.py:189
  198.1 29.1 %collective-permute-start.4 = (f32[1,2048]{1,0:T(1,128)S(1)}, f32[1,2048]{1,0:T(1,128)S(1)}, u32[]{:S(2)}, u32[]{:S(2)}) collective-permute-start(f32[1,2048]{1,0:T(1,128)S(1)} %add_add_fusion.1), channel_id=1, source_target_pairs={{0,8},{4,12},{8,0},{12,4},{16,24},{20,28},{24,16},{28,20},{32,40},... | collective-permute-start | bytes 24584 | tf_op jit(solution)/shard_map/ppermute | solution.py:189
  206.9 7.5 %copy-start.7 = (bf16[1024,768]{1,0:T(8,128)(2,1)S(1)}, bf16[1024,768]{1,0:T(8,128)(2,1)}, u32[]{:S(2)}) copy-start(bf16[1024,768]{1,0:T(8,128)(2,1)} %copy-done.6) | copy-start | bytes 4718596
  247.1 12.7 %collective-permute-start.7 = (bf16[64,2048]{1,0:T(8,128)(2,1)}, bf16[64,2048]{1,0:T(8,128)(2,1)}, u32[]{:S(2)}, u32[]{:S(2)}) collective-permute-start(bf16[64,2048]{1,0:T(8,128)(2,1)} %get-tuple-element.55), channel_id=1, source_target_pairs={{0,1},{1,2},{2,3},{3,0},{4,5},{5,6},{6,7},{7,4},{8,9},{9,10},{10,1... | collective-permute-start | bytes 786440 | tf_op jit(solution)/shard_map/ppermute | solution.py:177
  247.7 14.3 %collective-permute-start.8 = (bf16[64,2048]{1,0:T(8,128)(2,1)}, bf16[64,2048]{1,0:T(8,128)(2,1)S(1)}, u32[]{:S(2)}, u32[]{:S(2)}) collective-permute-start(bf16[64,2048]{1,0:T(8,128)(2,1)} %get-tuple-element.55), channel_id=1, source_target_pairs={{0,3},{1,0},{2,1},{3,2},{4,7},{5,4},{6,5},{7,6},{8,11},{9,8},{10,9... | collective-permute-start | bytes 786440 | tf_op jit(solution)/shard_map/ppermute | solution.py:177
  250.3 3.7 %collective-permute-start.10 = (f32[1,2048]{1,0:T(1,128)S(1)}, f32[1,2048]{1,0:T(1,128)S(1)}, u32[]{:S(2)}, u32[]{:S(2)}) collective-permute-start(f32[1,2048]{1,0:T(1,128)S(1)} %add_add_fusion), channel_id=1, source_target_pairs={{0,32},{4,36},{8,40},{12,44},{16,48},{20,52},{24,56},{28,60},{32,0... | collective-permute-start | bytes 24584 | tf_op jit(solution)/shard_map/ppermute | solution.py:189
  254.0 5.2 %collective-permute-start.11 = (f32[1,2048]{1,0:T(1,128)S(1)}, f32[1,2048]{1,0:T(1,128)S(1)}, u32[]{:S(2)}, u32[]{:S(2)}) collective-permute-start(f32[1,2048]{1,0:T(1,128)S(1)} %add.87), channel_id=1, source_target_pairs={{0,64},{4,68},{8,72},{12,76},{16,80},{20,84},{24,88},{28,92},{32,9... | collective-permute-start | bytes 24584 | tf_op jit(solution)/shard_map/ppermute | solution.py:189
  255.5 8.5 %collective-permute-start.9 = (bf16[64,2048]{1,0:T(8,128)(2,1)}, bf16[64,2048]{1,0:T(8,128)(2,1)S(1)}, u32[]{:S(2)}, u32[]{:S(2)}) collective-permute-start(bf16[64,2048]{1,0:T(8,128)(2,1)} %get-tuple-element.55), channel_id=1, source_target_pairs={{0,2},{1,3},{2,0},{3,1},{4,6},{5,7},{6,4},{7,5},{8,10},{9,11},{10,... | collective-permute-start | bytes 786440 | tf_op jit(solution)/shard_map/ppermute | solution.py:177

commit v5 on v4

--- a/solution.py
+++ b/solution.py
@@ -180,7 +180,7 @@
     for step, piece in moved:
         origin = (mine + size - step) % size
         whole = lax.dynamic_update_slice_in_dim(whole, piece, origin * rows, 0)
-    return whole
+    return whole, moved[0][1]
 
 
 def add_from(value, axis, distances):
@@ -291,7 +291,7 @@
     gate_pgrad = (act_grad * up_pre * sigma * (1.0 + gate_pre * (1.0 - sigma))).astype(BF16)
     up_pgrad = (act_grad * silu_vals).astype(BF16)
     back = dot(gate_pgrad, gate_w, ((1,), (1,))) + dot(up_pgrad, up_w, ((1,), (1,)))
-    back = back.astype(BF16)
+    back = lax.optimization_barrier(back.astype(BF16))
     gain_part = jnp.sum(back.astype(F32) * inputs.astype(F32), axis=0, keepdims=True) / gain
     gain_part = add_from(gain_part, "dp", (1,))
     gain_part = add_from(gain_part, "tensor", (1, 2, 3))
@@ -337,7 +337,6 @@
             (back_rows, gate_wgrad, up_wgrad, down_grad, layer_out, gate_grad_t, gain_part)
         )
     )
-    gain_grad = add_from(add_from(gain_part, "dp", (8,)), "dp", (16,))[0]
     own_grad, group_grad = pl.pallas_call(
         norm_grad_kernel,
         grid_spec=pltpu.PrefetchScalarGridSpec(
@@ -361,7 +360,8 @@
         cost_estimate=cost(2 * own * slots * width, 2 * slots * width),
         name="norm_grad",
     )(quarter, routes, back_rows, hidden, gain, out_grad)
-    input_grad = gather_group(own_grad, group_grad)
+    input_grad, first = gather_group(own_grad, group_grad)
+    gain_grad = add_from(after(gain_part, first), "dp", (8, 16, 24))[0]
     return (
         layer_out,
         input_grad,

time: 265 us -> 271 us (1.023)
  other arithmetic: 0.67 us -> 6.14 us
  matrix products: 61.9 us -> 57.2 us
  waiting for transfers between devices: 130 us -> 134 us
    ppermute x3, waiting for transfers between devices: 1.75 us -> 12.2 us  [gather_group(): lax.ppermute(block, 'tensor', [(i, (i + step) % size) for i in range(size)])]
    ppermute x9 -> x10, waiting for transfers between devices: 25.9 us -> 18.6 us  [add_from(): lax.ppermute(value, axis, [(i, i ^ distance) for i in range(size)])]
    reduce_sum x0 -> x1, other arithmetic: none -> 5.47 us  [per_device(): jnp.sum(back.astype(F32) * inputs.astype(F32), axis=0, keepdims=True) / gain]
    dot_general x9, matrix products: 61.9 us -> 57.2 us  [dot(): return lax.dot_general(a, b, (dims, ((), ())), preferred_element_type=F32)]
    ppermute x9 -> x10, starting transfers between devices: 10.4 us -> 12.4 us  [add_from(): lax.ppermute(value, axis, [(i, i ^ distance) for i in range(size)])]
  transfers between devices with their start and end apart: 16 -> 17, of which waited for: 12 -> 9; matrix products, arithmetic and copies ran while one was open for 25% -> 25% of each run, Pallas kernels for 5% -> 4%
where the time goes in v5:
time: 271 us
  waiting for transfers between devices  134 us (49%)
  matrix products  57.2 us (21%)
  starting transfers between devices  45.5 us (17%)
  Pallas kernels  20.4 us (8%)
  local copies, waits for them, and re-layouts  6.41 us (2%)
  other arithmetic  6.14 us (2%)
    all_to_all x4, waiting for transfers between devices, exchange(): return lax.all_to_all(block, AXES, split_axis=0, concat_axis=0, tiled=True)  103 us
    dot_general x9, matrix products, dot(): return lax.dot_general(a, b, (dims, ((), ())), preferred_element_type=F32)  57.2 us
    all_to_all x4, starting transfers between devices, exchange(): return lax.all_to_all(block, AXES, split_axis=0, concat_axis=0, tiled=True)  29.7 us
    ppermute x10, waiting for transfers between devices, add_from(): lax.ppermute(value, axis, [(i, i ^ distance) for i in range(size)])  18.6 us
    ppermute x10, starting transfers between devices, add_from(): lax.ppermute(value, axis, [(i, i ^ distance) for i in range(size)])  12.4 us
    ppermute x3, waiting for transfers between devices, gather_group(): lax.ppermute(block, 'tensor', [(i, (i + step) % size) for i in range(size)])  12.2 us
    reduce_sum x1, other arithmetic, per_device(): jnp.sum(back.astype(F32) * inputs.astype(F32), axis=0, keepdims=True) / gain  5.47 us
  transfers between devices with their start and end apart: 17, of which 9 were waited for; matrix products, arithmetic and copies ran while one was open for 25% of the time, Pallas kernels for 4%

profile of v5, /device:TPU:0, one launch (start us, length us, event | category | flops | bytes accessed | tf_op | source)
XLA Modules:
  0.0 270.8 jit_solution(4577782995750009694)
XLA Ops:
  0.7 4.0 %pack_normed.1 = bf16[1024,2048]{1,0:T(8,128)(2,1)} custom-call(s32[1]{0:T(128)} %bitcast.quarter, s32[8,64]{1,0:T(8,128)} %bitcast.62, bf16[256,2048]{1,0:T(8,128)(2,1)} %hidden.5, f32[1,2048]{1,0:T(1,128)} %bitcast.60), custom_call_target="tpu_custom_call" | custom-call | flops 268435456 | bytes 4194304 | tf_op jit(solution)/shard_map/pack_normed/pallas_call | solution.py:230
  4.7 11.7 %all-to-all-start = ((bf16[128,8,2048]{2,1,0:T(8,128)(2,1)}), bf16[128,8,2048]{2,1,0:T(8,128)(2,1)}, u32[]{:S(2)}, u32[]{:S(2)}) async-start(bf16[128,8,2048]{2,1,0:T(8,128)(2,1)} %bitcast.58), calls=%async_computation | async-start | bytes 8388608 | tf_op jit(solution)/shard_map/all_to_all | solution.py:169
  16.4 4.7 %pack_scaled.1 = bf16[1024,2048]{1,0:T(8,128)(2,1)} custom-call(s32[8,64]{1,0:T(8,128)} %bitcast.63, f32[8,64]{1,0:T(8,128)} %bitcast.66, bf16[64,2048]{1,0:T(8,128)(2,1)} %grad.5), custom_call_target="tpu_custom_call" | custom-call | flops 268435456 | bytes 4194304 | tf_op jit(solution)/shard_map/pack_scaled/pallas_call | solution.py:253
  21.1 47.5 %all-to-all-done = bf16[128,8,2048]{2,1,0:T(8,128)(2,1)} async-done(((bf16[128,8,2048]{2,1,0:T(8,128)(2,1)}), bf16[128,8,2048]{2,1,0:T(8,128)(2,1)}, u32[]{:S(2)}, u32[]{:S(2)}) %all-to-all-start) | async-done | bytes 4194336 | tf_op jit(solution)/shard_map/all_to_all | solution.py:169
  68.6 5.8 %all-to-all-start.1 = ((bf16[128,8,2048]{2,1,0:T(8,128)(2,1)}), bf16[128,8,2048]{2,1,0:T(8,128)(2,1)}, u32[]{:S(2)}, u32[]{:S(2)}) async-start(bf16[128,8,2048]{2,1,0:T(8,128)(2,1)} %bitcast.57), calls=%async_computation.1 | async-start | bytes 8388608 | tf_op jit(solution)/shard_map/all_to_all | solution.py:169
  74.4 6.3 %fusion.8 = f32[1024,768]{1,0:T(8,128)S(1)} fusion(bf16[1,2048,768]{2,1,0:T(8,128)(2,1)} %param.13, bf16[128,8,2048]{2,1,0:T(8,128)(2,1)} %all-to-all-done), kind=kOutput, calls=%fused_computation.14 | convolution fusion | flops 3221225472 | bytes 10485760 | tf_op jit(solution)/shard_map/dot_general | solution.py:210
  80.8 8.6 %multiply_convert_fusion.2 = (bf16[1024,768]{1,0:T(8,128)(2,1)S(1)}, f32[1024,768]{1,0:T(8,128)}) fusion(f32[1024,768]{1,0:T(8,128)S(1)} %fusion.8, bf16[1,2048,768]{2,1,0:T(8,128)(2,1)S(1)} %copy-done.7, bf16[128,8,2048]{2,1,0:T(8,128)(2,1)} %all-to-all-done), kind=kOutput, calls=%fused_computation.19 | convolution fusion | flops 3225944064 | bytes 15204352 | tf_op jit(solution)/shard_map/dot_general | solution.py:210
  89.3 1.1 copy-done.9
  90.5 4.9 %convolution_convert_fusion = bf16[1024,2048]{1,0:T(8,128)(2,1)} fusion(bf16[1024,768]{1,0:T(8,128)(2,1)S(1)} %get-tuple-element.45, bf16[1,768,2048]{2,1,0:T(8,128)(2,1)S(1)} %copy-done), kind=kOutput, calls=%fused_computation.2 | convolution fusion | flops 3223322624 | bytes 8912896 | tf_op jit(solution)/shard_map/dot_general | solution.py:210
  95.4 31.2 %all-to-all-done.1 = bf16[128,8,2048]{2,1,0:T(8,128)(2,1)} async-done(((bf16[128,8,2048]{2,1,0:T(8,128)(2,1)}), bf16[128,8,2048]{2,1,0:T(8,128)(2,1)}, u32[]{:S(2)}, u32[]{:S(2)}) %all-to-all-start.1) | async-done | bytes 4194336 | tf_op jit(solution)/shard_map/all_to_all | solution.py:169
  126.6 6.0 %all-to-all-start.2 = ((bf16[128,8,2048]{2,1,0:T(8,128)(2,1)}), bf16[128,8,2048]{2,1,0:T(8,128)(2,1)}, u32[]{:S(2)}, u32[]{:S(2)}) async-start(bf16[128,8,2048]{2,1,0:T(8,128)(2,1)} %bitcast.59), calls=%async_computation.2 | async-start | bytes 8388608 | tf_op jit(solution)/shard_map/all_to_all | solution.py:169
  132.7 8.4 %multiply_convert_fusion = (bf16[1024,768]{1,0:T(8,128)(2,1)S(1)}, bf16[1024,768]{1,0:T(8,128)(2,1)S(1)}) fusion(f32[1024,768]{1,0:T(8,128)} %copy-done.13, f32[1024,768]{1,0:T(8,128)} %get-tuple-element.38, bf16[1024,2048]{1,0:T(8,128)(2,1)} %bitcast.9, bf16[1,768,2048]{2,1,0:T(8,128)(2,1)S(1)} %copy-done), kind=kOutput, calls=%fused_computation.16 | convolution fusion | flops 3231449088 | bytes 16777216 | tf_op jit(solution)/shard_map/dot_general | solution.py:210
  141.1 3.4 %fusion.6 = f32[1024,2048]{1,0:T(8,128)S(1)} fusion(bf16[1024,768]{1,0:T(8,128)(2,1)S(1)} %get-tuple-element.43, bf16[1,2048,768]{2,1,0:T(8,128)(2,1)S(1)} %copy-done.6), kind=kOutput, calls=%fused_computation.12 | convolution fusion | flops 3221225472 | bytes 13107200 | tf_op jit(solution)/shard_map/dot_general | solution.py:210
  144.6 3.7 %add_convert_fusion = bf16[1024,2048]{1,0:T(8,128)(2,1)S(1)} fusion(f32[1024,2048]{1,0:T(8,128)S(1)} %fusion.6, bf16[1024,768]{1,0:T(8,128)(2,1)S(1)} %get-tuple-element.44, bf16[1,2048,768]{2,1,0:T(8,128)(2,1)S(1)} %copy-done.8), kind=kOutput, calls=%fused_computation.1 | convolution fusion | flops 3225419776 | bytes 17301504 | tf_op jit(solution)/shard_map/dot_general | solution.py:210
  148.3 5.5 %multiply_reduce_fusion = f32[2048]{0:T(1024)S(1)} fusion(bf16[1024,2048]{1,0:T(8,128)(2,1)S(1)} %add_convert_fusion, bf16[128,8,2048]{2,1,0:T(8,128)(2,1)} %all-to-all-done), kind=kLoop, calls=%fused_computation | loop fusion | flops 8386560 | bytes 8396800 | tf_op jit(solution)/shard_map/reduce_sum | solution.py:295
  153.8 0.1 collective-permute-start
  153.9 1.2 collective-permute-done
  155.1 2.1 collective-permute-start.3
  157.2 0.8 collective-permute-start.2
  158.0 1.3 collective-permute-start.1
  159.3 11.5 %collective-permute-done.3 = f32[1,2048]{1,0:T(1,128)S(1)} collective-permute-done((f32[1,2048]{1,0:T(1,128)S(1)}, f32[1,2048]{1,0:T(1,128)S(1)}, u32[]{:S(2)}, u32[]{:S(2)}) %collective-permute-start.3) | collective-permute-done | bytes 8224 | tf_op jit(solution)/shard_map/ppermute | solution.py:189
  170.7 2.6 collective-permute-done.2
  173.4 3.3 %collective-permute-done.1 = f32[1,2048]{1,0:T(1,128)S(1)} collective-permute-done((f32[1,2048]{1,0:T(1,128)S(1)}, f32[1,2048]{1,0:T(1,128)S(1)}, u32[]{:S(2)}, u32[]{:S(2)}) %collective-permute-start.1) | collective-permute-done | bytes 8224 | tf_op jit(solution)/shard_map/ppermute | solution.py:189
  176.7 8.0 %all-to-all-done.2 = bf16[128,8,2048]{2,1,0:T(8,128)(2,1)} async-done(((bf16[128,8,2048]{2,1,0:T(8,128)(2,1)}), bf16[128,8,2048]{2,1,0:T(8,128)(2,1)}, u32[]{:S(2)}, u32[]{:S(2)}) %all-to-all-start.2) | async-done | bytes 4194336 | tf_op jit(solution)/shard_map/all_to_all | solution.py:169
  184.7 6.1 %all-to-all-start.3 = ((bf16[128,8,2048]{2,1,0:T(8,128)(2,1)}), bf16[128,8,2048]{2,1,0:T(8,128)(2,1)}, u32[]{:S(2)}, u32[]{:S(2)}) async-start(bf16[128,8,2048]{2,1,0:T(8,128)(2,1)} %bitcast.56), calls=%async_computation.3 | async-start | bytes 8388608 | tf_op jit(solution)/shard_map/all_to_all | solution.py:169
  190.8 0.7 copy.16.probs
  191.5 0.7 copy.17.ids
  192.2 0.7 copy.15.ids
  192.9 2.1 routes.1
  195.0 2.8 %collective-permute-start.6 = (f32[1,2048]{1,0:T(1,128)S(1)}, f32[1,2048]{1,0:T(1,128)S(1)}, u32[]{:S(2)}, u32[]{:S(2)}) collective-permute-start(f32[1,2048]{1,0:T(1,128)S(1)} %add_add_fusion.2), channel_id=1, source_target_pairs={{0,24},{4,28},{8,16},{12,20},{16,8},{20,12},{24,0},{28,4},{32,56},... | collective-permute-start | bytes 24584 | tf_op jit(solution)/shard_map/ppermute | solution.py:189
  197.8 0.3 collective-permute-start.5
  198.1 1.0 collective-permute-start.4
  199.1 7.0 %convolution_convert_fusion.1 = bf16[768,2048]{1,0:T(8,128)(2,1)} fusion(bf16[1024,768]{1,0:T(8,128)(2,1)S(1)} %copy-done.10, bf16[1024,2048]{1,0:T(8,128)(2,1)} %bitcast.9), kind=kOutput, calls=%fused_computation.3 | convolution fusion | flops 3222798336 | bytes 8912896 | tf_op jit(solution)/shard_map/dot_general | solution.py:210
  206.2 7.5 %convolution_convert_fusion.3 = bf16[2048,768]{1,0:T(8,128)(2,1)} fusion(bf16[1024,768]{1,0:T(8,128)(2,1)S(1)} %copy-done.12, bf16[128,8,2048]{2,1,0:T(8,128)(2,1)} %all-to-all-done), kind=kOutput, calls=%fused_computation.5 | convolution fusion | flops 3222798336 | bytes 8912896 | tf_op jit(solution)/shard_map/dot_general | solution.py:210
  213.7 7.4 %convolution_convert_fusion.2 = bf16[2048,768]{1,0:T(8,128)(2,1)} fusion(bf16[1024,768]{1,0:T(8,128)(2,1)S(1)} %copy-done.15, bf16[128,8,2048]{2,1,0:T(8,128)(2,1)} %all-to-all-done), kind=kOutput, calls=%fused_computation.4 | convolution fusion | flops 3222798336 | bytes 8912896 | tf_op jit(solution)/shard_map/dot_general | solution.py:210
  221.0 5.4 %combine.1 = (bf16[64,2048]{1,0:T(8,128)(2,1)}, f32[8,64]{1,0:T(8,128)}) custom-call(s32[1]{0:T(128)} %bitcast.quarter, s32[64,8]{1,0:T(8,128)} %copy.17.ids, bf16[64,1024]{1,0:T(8,128)(2,1)} %get-tuple-element.47.routes, bf16[192,1024]{1,0:T(8,128)(2,1)} %get-tuple-element.48.weights, bf16[1024,2048]{1,0:T(8,128)(2,1)} %bitcast.12.rows, ...), custom_call_target="tpu_custom_call" | custom-call | flops 1073741824 | bytes 4194304 | tf_op jit(solution)/shard_map/combine/pallas_call | solution.py:310
  226.4 16.6 %all-to-all-done.3 = bf16[128,8,2048]{2,1,0:T(8,128)(2,1)} async-done(((bf16[128,8,2048]{2,1,0:T(8,128)(2,1)}), bf16[128,8,2048]{2,1,0:T(8,128)(2,1)}, u32[]{:S(2)}, u32[]{:S(2)}) %all-to-all-start.3) | async-done | bytes 4194336 | tf_op jit(solution)/shard_map/all_to_all | solution.py:169
  243.0 4.3 %norm_grad.1 = (bf16[64,2048]{1,0:T(8,128)(2,1)}, bf16[256,2048]{1,0:T(8,128)(2,1)}) custom-call(s32[1]{0:T(128)} %bitcast.quarter, bf16[64,1024]{1,0:T(8,128)(2,1)} %get-tuple-element.47.routes, bf16[1024,2048]{1,0:T(8,128)(2,1)} %bitcast.15.rows, bf16[256,2048]{1,0:T(8,128)(2,1)} %hidden.5, f32[1,2048]{1,0:T(1,128)} %bitcast.61, bf16[64,2048]{1,0:T(8,128)(2,1)} %grad.5), custom_call_target="tpu_custom_call" | custom-call | flops 268435456 | bytes 4194304 | tf_op jit(solution)/shard_map/norm_grad/pallas_call | solution.py:340
  247.3 0.6 collective-permute-start.7
  247.9 2.6 collective-permute-start.8
  250.5 0.2 collective-permute-start.9
  250.7 12.2 %collective-permute-done.7 = bf16[64,2048]{1,0:T(8,128)(2,1)} collective-permute-done((bf16[64,2048]{1,0:T(8,128)(2,1)}, bf16[64,2048]{1,0:T(8,128)(2,1)}, u32[]{:S(2)}, u32[]{:S(2)}) %collective-permute-start.7) | collective-permute-done | bytes 262176 | tf_op jit(solution)/shard_map/ppermute | solution.py:177
  262.9 2.7 %collective-permute-start.11 = (f32[1,2048]{1,0:T(1,128)S(1)}, f32[1,2048]{1,0:T(1,128)S(1)}, u32[]{:S(2)}, u32[]{:S(2)}) collective-permute-start(f32[1,2048]{1,0:T(1,128)S(1)} %add_add_fusion.1), channel_id=1, source_target_pairs={{0,64},{4,68},{8,72},{12,76},{16,80},{20,84},{24,88},{28,92},{32,9... | collective-permute-start | bytes 24584 | tf_op jit(solution)/shard_map/ppermute | solution.py:189
  265.7 1.3 collective-permute-start.10
  267.0 1.7 constant_dynamic-update-slice_fusion.2
  268.7 0.7 constant_dynamic-update-slice_fusion.1
  269.4 0.7 constant_dynamic-update-slice_fusion
  270.1 0.6 add_add_fusion
  (44 shorter events, 0.2 us)
Async XLA Ops:
  0.6 89.8 %copy-start = (bf16[1,768,2048]{2,1,0:T(8,128)(2,1)S(1)}, bf16[1,768,2048]{2,1,0:T(8,128)(2,1)}, u32[]{:S(2)}) copy-start(bf16[1,768,2048]{2,1,0:T(8,128)(2,1)} %param.15) | copy-start | bytes 9437188
  4.7 63.9 %all-to-all-start = ((bf16[128,8,2048]{2,1,0:T(8,128)(2,1)}), bf16[128,8,2048]{2,1,0:T(8,128)(2,1)}, u32[]{:S(2)}, u32[]{:S(2)}) async-start(bf16[128,8,2048]{2,1,0:T(8,128)(2,1)} %bitcast.58), calls=%async_computation | async-start | bytes 8388608 | tf_op jit(solution)/shard_map/all_to_all | solution.py:169
  68.6 58.1 %all-to-all-start.1 = ((bf16[128,8,2048]{2,1,0:T(8,128)(2,1)}), bf16[128,8,2048]{2,1,0:T(8,128)(2,1)}, u32[]{:S(2)}, u32[]{:S(2)}) async-start(bf16[128,8,2048]{2,1,0:T(8,128)(2,1)} %bitcast.57), calls=%async_computation.1 | async-start | bytes 8388608 | tf_op jit(solution)/shard_map/all_to_all | solution.py:169
  74.4 6.3 %copy-start.7 = (bf16[1,2048,768]{2,1,0:T(8,128)(2,1)S(1)}, bf16[1,2048,768]{2,1,0:T(8,128)(2,1)}, u32[]{:S(2)}) copy-start(bf16[1,2048,768]{2,1,0:T(8,128)(2,1)} %param.14) | copy-start | bytes 9437188
  80.7 8.6 %copy-start.13 = (f32[1024,768]{1,0:T(8,128)}, f32[1024,768]{1,0:T(8,128)S(1)}, u32[]{:S(2)}) copy-start(f32[1024,768]{1,0:T(8,128)S(1)} %fusion.8) | copy-start | bytes 9437188
  89.3 1.1 copy-start.9
  126.6 58.1 %all-to-all-start.2 = ((bf16[128,8,2048]{2,1,0:T(8,128)(2,1)}), bf16[128,8,2048]{2,1,0:T(8,128)(2,1)}, u32[]{:S(2)}, u32[]{:S(2)}) async-start(bf16[128,8,2048]{2,1,0:T(8,128)(2,1)} %bitcast.59), calls=%async_computation.2 | async-start | bytes 8388608 | tf_op jit(solution)/shard_map/all_to_all | solution.py:169
  132.7 8.4 %copy-start.6 = (bf16[1,2048,768]{2,1,0:T(8,128)(2,1)S(1)}, bf16[1,2048,768]{2,1,0:T(8,128)(2,1)}, u32[]{:S(2)}) copy-start(bf16[1,2048,768]{2,1,0:T(8,128)(2,1)} %param.13) | copy-start | bytes 9437188
  141.1 3.5 %copy-start.11 = (bf16[1024,768]{1,0:T(8,128)(2,1)}, bf16[1024,768]{1,0:T(8,128)(2,1)S(1)}, u32[]{:S(2)}) copy-start(bf16[1024,768]{1,0:T(8,128)(2,1)S(1)} %get-tuple-element.43) | copy-start | bytes 4718596
  141.1 3.5 %copy-start.14 = (bf16[1024,768]{1,0:T(8,128)(2,1)}, bf16[1024,768]{1,0:T(8,128)(2,1)S(1)}, u32[]{:S(2)}) copy-start(bf16[1024,768]{1,0:T(8,128)(2,1)S(1)} %get-tuple-element.44) | copy-start | bytes 4718596
  141.1 3.5 %copy-start.8 = (bf16[1,2048,768]{2,1,0:T(8,128)(2,1)S(1)}, bf16[1,2048,768]{2,1,0:T(8,128)(2,1)}, u32[]{:S(2)}) copy-start(bf16[1,2048,768]{2,1,0:T(8,128)(2,1)} %param.14) | copy-start | bytes 9437188
  148.3 5.5 %copy-start.2 = (bf16[1024,2048]{1,0:T(8,128)(2,1)}, bf16[1024,2048]{1,0:T(8,128)(2,1)S(1)}, u32[]{:S(2)}) copy-start(bf16[1024,2048]{1,0:T(8,128)(2,1)S(1)} %add_convert_fusion) | copy-start | bytes 12582916
  148.3 5.5 %copy-start.3 = (f32[2048]{0:T(1024)S(1)}, f32[2048]{0:T(1024)}, u32[]{:S(2)}) copy-start(f32[2048]{0:T(1024)} %param.9) | copy-start | bytes 24580
  153.8 1.3 collective-permute-start
  155.1 15.7 %collective-permute-start.3 = (f32[1,2048]{1,0:T(1,128)S(1)}, f32[1,2048]{1,0:T(1,128)S(1)}, u32[]{:S(2)}, u32[]{:S(2)}) collective-permute-start(f32[1,2048]{1,0:T(1,128)S(1)} %add.77), channel_id=1, source_target_pairs={{0,3},{1,2},{2,1},{3,0},{4,7},{5,6},{6,5},{7,4},{8,11},{9,10},{10,... | collective-permute-start | bytes 24584 | tf_op jit(solution)/shard_map/ppermute | solution.py:189
  157.2 16.2 %collective-permute-start.2 = (f32[1,2048]{1,0:T(1,128)S(1)}, f32[1,2048]{1,0:T(1,128)S(1)}, u32[]{:S(2)}, u32[]{:S(2)}) collective-permute-start(f32[1,2048]{1,0:T(1,128)S(1)} %add.77), channel_id=1, source_target_pairs={{0,2},{1,3},{2,0},{3,1},{4,6},{5,7},{6,4},{7,5},{8,10},{9,11},{10,... | collective-permute-start | bytes 24584 | tf_op jit(solution)/shard_map/ppermute | solution.py:189
  158.0 18.7 %collective-permute-start.1 = (f32[1,2048]{1,0:T(1,128)S(1)}, f32[1,2048]{1,0:T(1,128)S(1)}, u32[]{:S(2)}, u32[]{:S(2)}) collective-permute-start(f32[1,2048]{1,0:T(1,128)S(1)} %add.77), channel_id=1, source_target_pairs={{0,1},{1,0},{2,3},{3,2},{4,5},{5,4},{6,7},{7,6},{8,9},{9,8},{10,11... | collective-permute-start | bytes 24584 | tf_op jit(solution)/shard_map/ppermute | solution.py:189
  184.7 6.1 %copy-start.5 = (f32[64,8]{0,1:T(8,128)S(1)}, f32[64,8]{0,1:T(8,128)}, u32[]{:S(2)}) copy-start(f32[64,8]{0,1:T(8,128)} %param.11) | copy-start | bytes 6148
  184.7 6.8 %copy-start.4 = (s32[64,8]{0,1:T(8,128)S(1)}, s32[64,8]{0,1:T(8,128)}, u32[]{:S(2)}) copy-start(s32[64,8]{0,1:T(8,128)} %param.10) | copy-start | bytes 6148
  184.7 14.4 %copy-start.10 = (bf16[1024,768]{1,0:T(8,128)(2,1)S(1)}, bf16[1024,768]{1,0:T(8,128)(2,1)}, u32[]{:S(2)}) copy-start(bf16[1024,768]{1,0:T(8,128)(2,1)} %copy-done.9) | copy-start | bytes 4718596
  184.7 58.3 %all-to-all-start.3 = ((bf16[128,8,2048]{2,1,0:T(8,128)(2,1)}), bf16[128,8,2048]{2,1,0:T(8,128)(2,1)}, u32[]{:S(2)}, u32[]{:S(2)}) async-start(bf16[128,8,2048]{2,1,0:T(8,128)(2,1)} %bitcast.56), calls=%async_computation.3 | async-start | bytes 8388608 | tf_op jit(solution)/shard_map/all_to_all | solution.py:169
  195.0 11.2 %copy-start.12 = (bf16[1024,768]{1,0:T(8,128)(2,1)S(1)}, bf16[1024,768]{1,0:T(8,128)(2,1)}, u32[]{:S(2)}) copy-start(bf16[1024,768]{1,0:T(8,128)(2,1)} %copy-done.11) | copy-start | bytes 4718596
  195.0 31.4 %collective-permute-start.6 = (f32[1,2048]{1,0:T(1,128)S(1)}, f32[1,2048]{1,0:T(1,128)S(1)}, u32[]{:S(2)}, u32[]{:S(2)}) collective-permute-start(f32[1,2048]{1,0:T(1,128)S(1)} %add_add_fusion.2), channel_id=1, source_target_pairs={{0,24},{4,28},{8,16},{12,20},{16,8},{20,12},{24,0},{28,4},{32,56},... | collective-permute-start | bytes 24584 | tf_op jit(solution)/shard_map/ppermute | solution.py:189
  197.8 28.6 %collective-permute-start.5 = (f32[1,2048]{1,0:T(1,128)S(1)}, f32[1,2048]{1,0:T(1,128)S(1)}, u32[]{:S(2)}, u32[]{:S(2)}) collective-permute-start(f32[1,2048]{1,0:T(1,128)S(1)} %add_add_fusion.2), channel_id=1, source_target_pairs={{0,16},{4,20},{8,24},{12,28},{16,0},{20,4},{24,8},{28,12},{32,48},... | collective-permute-start | bytes 24584 | tf_op jit(solution)/shard_map/ppermute | solution.py:189
  198.1 28.3 %collective-permute-start.4 = (f32[1,2048]{1,0:T(1,128)S(1)}, f32[1,2048]{1,0:T(1,128)S(1)}, u32[]{:S(2)}, u32[]{:S(2)}) collective-permute-start(f32[1,2048]{1,0:T(1,128)S(1)} %add_add_fusion.2), channel_id=1, source_target_pairs={{0,8},{4,12},{8,0},{12,4},{16,24},{20,28},{24,16},{28,20},{32,40},... | collective-permute-start | bytes 24584 | tf_op jit(solution)/shard_map/ppermute | solution.py:189
  206.2 7.5 %copy-start.15 = (bf16[1024,768]{1,0:T(8,128)(2,1)S(1)}, bf16[1024,768]{1,0:T(8,128)(2,1)}, u32[]{:S(2)}) copy-start(bf16[1024,768]{1,0:T(8,128)(2,1)} %copy-done.14) | copy-start | bytes 4718596
  243.0 27.7 %copy-start.1 = (bf16[1,768,2048]{2,1,0:T(8,128)(2,1)S(1)}, bf16[1,768,2048]{2,1,0:T(8,128)(2,1)}, u32[]{:S(2)}) copy-start(bf16[1,768,2048]{2,1,0:T(8,128)(2,1)} %param.15) | copy-start | bytes 9437188
  247.3 15.6 %collective-permute-start.7 = (bf16[64,2048]{1,0:T(8,128)(2,1)}, bf16[64,2048]{1,0:T(8,128)(2,1)}, u32[]{:S(2)}, u32[]{:S(2)}) collective-permute-start(bf16[64,2048]{1,0:T(8,128)(2,1)} %get-tuple-element.56), channel_id=1, source_target_pairs={{0,1},{1,2},{2,3},{3,0},{4,5},{5,6},{6,7},{7,4},{8,9},{9,10},{10,1... | collective-permute-start | bytes 786440 | tf_op jit(solution)/shard_map/ppermute | solution.py:177
  247.9 20.8 %collective-permute-start.8 = (bf16[64,2048]{1,0:T(8,128)(2,1)}, bf16[64,2048]{1,0:T(8,128)(2,1)S(1)}, u32[]{:S(2)}, u32[]{:S(2)}) collective-permute-start(bf16[64,2048]{1,0:T(8,128)(2,1)} %get-tuple-element.56), channel_id=1, source_target_pairs={{0,3},{1,0},{2,1},{3,2},{4,7},{5,4},{6,5},{7,6},{8,11},{9,8},{10,9... | collective-permute-start | bytes 786440 | tf_op jit(solution)/shard_map/ppermute | solution.py:177
  250.5 18.9 %collective-permute-start.9 = (bf16[64,2048]{1,0:T(8,128)(2,1)}, bf16[64,2048]{1,0:T(8,128)(2,1)S(1)}, u32[]{:S(2)}, u32[]{:S(2)}) collective-permute-start(bf16[64,2048]{1,0:T(8,128)(2,1)} %get-tuple-element.56), channel_id=1, source_target_pairs={{0,2},{1,3},{2,0},{3,1},{4,6},{5,7},{6,4},{7,5},{8,10},{9,11},{10,... | collective-permute-start | bytes 786440 | tf_op jit(solution)/shard_map/ppermute | solution.py:177
  262.9 7.2 %collective-permute-start.12 = (f32[1,2048]{1,0:T(1,128)S(1)}, f32[1,2048]{1,0:T(1,128)S(1)}, u32[]{:S(2)}, u32[]{:S(2)}) collective-permute-start(f32[1,2048]{1,0:T(1,128)S(1)} %add_add_fusion.1), channel_id=1, source_target_pairs={{0,96},{4,100},{8,104},{12,108},{16,112},{20,116},{24,120},{28,124... | collective-permute-start | bytes 24584 | tf_op jit(solution)/shard_map/ppermute | solution.py:189
  262.9 7.2 %collective-permute-start.11 = (f32[1,2048]{1,0:T(1,128)S(1)}, f32[1,2048]{1,0:T(1,128)S(1)}, u32[]{:S(2)}, u32[]{:S(2)}) collective-permute-start(f32[1,2048]{1,0:T(1,128)S(1)} %add_add_fusion.1), channel_id=1, source_target_pairs={{0,64},{4,68},{8,72},{12,76},{16,80},{20,84},{24,88},{28,92},{32,9... | collective-permute-start | bytes 24584 | tf_op jit(solution)/shard_map/ppermute | solution.py:189
  265.7 4.5 %collective-permute-start.10 = (f32[1,2048]{1,0:T(1,128)S(1)}, f32[1,2048]{1,0:T(1,128)S(1)}, u32[]{:S(2)}, u32[]{:S(2)}) collective-permute-start(f32[1,2048]{1,0:T(1,128)S(1)} %add_add_fusion.1), channel_id=1, source_target_pairs={{0,32},{4,36},{8,40},{12,44},{16,48},{20,52},{24,56},{28,60},{32,0... | collective-permute-start | bytes 24584 | tf_op jit(solution)/shard_map/ppermute | solution.py:189

commit v6 on v4

--- a/solution.py
+++ b/solution.py
@@ -139,7 +139,9 @@
         gate_grad[...] = found[...].T[:top, :]
 
 
-def norm_grad_kernel(quarter, routes, rows, hidden, gain, grad, own_grad, group_grad, total):
+def norm_grad_kernel(
+    quarter, routes, rows, hidden, gain, grad, upper, lower, group_grad, total
+):
     step = pl.program_id(0)
     part = jnp.dot(routes[...], rows[...], preferred_element_type=F32)
 
@@ -161,7 +163,9 @@
             grad[...].astype(F32)
             + inverse * (upstream - unit * jnp.mean(upstream * unit, axis=-1, keepdims=True))
         ).astype(BF16)
-        own_grad[...] = result
+        half = result.shape[0] // 2
+        upper[...] = result[:half]
+        lower[...] = result[half:]
         group_grad[...] = result
 
 
@@ -169,17 +173,29 @@
     return lax.all_to_all(block, AXES, split_axis=0, concat_axis=0, tiled=True)
 
 
-def gather_group(block, whole):
+def gather_group(upper, lower, whole):
     size = lax.axis_size("tensor")
     mine = lax.axis_index("tensor")
-    rows = block.shape[0]
-    moved = [
-        (step, lax.ppermute(block, "tensor", [(i, (i + step) % size) for i in range(size)]))
-        for step in (1, 3, 2)
+    half = upper.shape[0]
+    rows = 2 * half
+
+    def move(piece, step):
+        return lax.ppermute(piece, "tensor", [(i, (i + step) % size) for i in range(size)])
+
+    up_first, down_first = move(upper, 1), move(lower, size - 1)
+    up_second, down_second = move(lower, 1), move(upper, size - 1)
+    before, beyond, behind = [
+        (mine + size - step) % size * rows for step in (1, 2, size - 1)
     ]
-    for step, piece in moved:
-        origin = (mine + size - step) % size
-        whole = lax.dynamic_update_slice_in_dim(whole, piece, origin * rows, 0)
+    for piece, place in (
+        (up_first, before),
+        (up_second, before + half),
+        (down_second, behind),
+        (down_first, behind + half),
+        (move(up_first, 1), beyond),
+        (move(down_first, size - 1), beyond + half),
+    ):
+        whole = lax.dynamic_update_slice_in_dim(whole, piece, place, 0)
     return whole
 
 
@@ -291,7 +307,7 @@
     gate_pgrad = (act_grad * up_pre * sigma * (1.0 + gate_pre * (1.0 - sigma))).astype(BF16)
     up_pgrad = (act_grad * silu_vals).astype(BF16)
     back = dot(gate_pgrad, gate_w, ((1,), (1,))) + dot(up_pgrad, up_w, ((1,), (1,)))
-    back = back.astype(BF16)
+    back = lax.optimization_barrier(back.astype(BF16))
     gain_part = jnp.sum(back.astype(F32) * inputs.astype(F32), axis=0, keepdims=True) / gain
     gain_part = add_from(gain_part, "dp", (1,))
     gain_part = add_from(gain_part, "tensor", (1, 2, 3))
@@ -338,7 +354,7 @@
         )
     )
     gain_grad = add_from(add_from(gain_part, "dp", (8,)), "dp", (16,))[0]
-    own_grad, group_grad = pl.pallas_call(
+    upper, lower, group_grad = pl.pallas_call(
         norm_grad_kernel,
         grid_spec=pltpu.PrefetchScalarGridSpec(
             num_scalar_prefetch=1,
@@ -350,18 +366,23 @@
                 whole(1, width),
                 whole(own, width),
             ],
-            out_specs=[whole(own, width), pl.BlockSpec((own, width), lambda i, q: (q[0], 0))],
+            out_specs=[
+                whole(own // 2, width),
+                whole(own // 2, width),
+                pl.BlockSpec((own, width), lambda i, q: (q[0], 0)),
+            ],
             scratch_shapes=[pltpu.VMEM((own, width), F32)],
         ),
         out_shape=[
-            jax.ShapeDtypeStruct((own, width), BF16),
+            jax.ShapeDtypeStruct((own // 2, width), BF16),
+            jax.ShapeDtypeStruct((own // 2, width), BF16),
             jax.ShapeDtypeStruct(hidden.shape, BF16),
         ],
         compiler_params=params(),
         cost_estimate=cost(2 * own * slots * width, 2 * slots * width),
         name="norm_grad",
     )(quarter, routes, back_rows, hidden, gain, out_grad)
-    input_grad = gather_group(own_grad, group_grad)
+    input_grad = gather_group(upper, lower, group_grad)
     return (
         layer_out,
         input_grad,

time: 265 us -> 268 us (1.011)
  other arithmetic: 0.67 us -> 6.14 us
  matrix products: 61.9 us -> 57.3 us
  starting transfers between devices: 44.3 us -> 48.6 us
  waiting for transfers between devices: 130 us -> 127 us
    reduce_sum x0 -> x1, other arithmetic: none -> 5.47 us  [per_device(): jnp.sum(back.astype(F32) * inputs.astype(F32), axis=0, keepdims=True) / gain]
    dot_general x9, matrix products: 61.9 us -> 57.3 us  [dot(): return lax.dot_general(a, b, (dims, ((), ())), preferred_element_type=F32)]
    ppermute x3 -> x6, starting transfers between devices: 4.22 us -> 8.5 us  [move(): lax.ppermute(piece, 'tensor', [(i, (i + step) % size) for i in range(size)])]
  transfers between devices with their start and end apart: 16 -> 19, of which waited for: 12 -> 11; matrix products, arithmetic and copies ran while one was open for 25% -> 26% of each run, Pallas kernels for 5% -> 5%
where the time goes in v6:
time: 268 us
  waiting for transfers between devices  127 us (47%)
  matrix products  57.3 us (21%)
  starting transfers between devices  48.6 us (18%)
  Pallas kernels  20.4 us (8%)
  local copies, waits for them, and re-layouts  7.29 us (3%)
  other arithmetic  6.14 us (2%)
    all_to_all x4, waiting for transfers between devices, exchange(): return lax.all_to_all(block, AXES, split_axis=0, concat_axis=0, tiled=True)  103 us
    dot_general x9, matrix products, dot(): return lax.dot_general(a, b, (dims, ((), ())), preferred_element_type=F32)  57.3 us
    all_to_all x4, starting transfers between devices, exchange(): return lax.all_to_all(block, AXES, split_axis=0, concat_axis=0, tiled=True)  29.7 us
    ppermute x9, waiting for transfers between devices, add_from(): lax.ppermute(value, axis, [(i, i ^ distance) for i in range(size)])  23.3 us
    ppermute x9, starting transfers between devices, add_from(): lax.ppermute(value, axis, [(i, i ^ distance) for i in range(size)])  10.4 us
    ppermute x6, starting transfers between devices, move(): lax.ppermute(piece, 'tensor', [(i, (i + step) % size) for i in range(size)])  8.5 us
    reduce_sum x1, other arithmetic, per_device(): jnp.sum(back.astype(F32) * inputs.astype(F32), axis=0, keepdims=True) / gain  5.47 us
    pallas_call x1, Pallas kernels, per_device(): pl.pallas_call(combine_kernel, grid_spec=pltpu.PrefetchScalarGridSpec(num...  5.36 us
  transfers between devices with their start and end apart: 19, of which 11 were waited for; matrix products, arithmetic and copies ran while one was open for 26% of the time, Pallas kernels for 5%

profile of v6, /device:TPU:0, one launch (start us, length us, event | category | flops | bytes accessed | tf_op | source)
XLA Modules:
  0.0 267.6 jit_solution(12328322560442326377)
XLA Ops:
  0.7 4.0 %pack_normed.1 = bf16[1024,2048]{1,0:T(8,128)(2,1)} custom-call(s32[1]{0:T(128)} %bitcast.quarter, s32[8,64]{1,0:T(8,128)} %bitcast.62, bf16[256,2048]{1,0:T(8,128)(2,1)} %hidden.5, f32[1,2048]{1,0:T(1,128)} %bitcast.60), custom_call_target="tpu_custom_call" | custom-call | flops 268435456 | bytes 4194304 | tf_op jit(solution)/shard_map/pack_normed/pallas_call | solution.py:246
  4.7 11.7 %all-to-all-start = ((bf16[128,8,2048]{2,1,0:T(8,128)(2,1)}), bf16[128,8,2048]{2,1,0:T(8,128)(2,1)}, u32[]{:S(2)}, u32[]{:S(2)}) async-start(bf16[128,8,2048]{2,1,0:T(8,128)(2,1)} %bitcast.58), calls=%async_computation | async-start | bytes 8388608 | tf_op jit(solution)/shard_map/all_to_all | solution.py:173
  16.4 4.7 %pack_scaled.1 = bf16[1024,2048]{1,0:T(8,128)(2,1)} custom-call(s32[8,64]{1,0:T(8,128)} %bitcast.63, f32[8,64]{1,0:T(8,128)} %bitcast.66, bf16[64,2048]{1,0:T(8,128)(2,1)} %grad.5), custom_call_target="tpu_custom_call" | custom-call | flops 268435456 | bytes 4194304 | tf_op jit(solution)/shard_map/pack_scaled/pallas_call | solution.py:269
  21.0 47.5 %all-to-all-done = bf16[128,8,2048]{2,1,0:T(8,128)(2,1)} async-done(((bf16[128,8,2048]{2,1,0:T(8,128)(2,1)}), bf16[128,8,2048]{2,1,0:T(8,128)(2,1)}, u32[]{:S(2)}, u32[]{:S(2)}) %all-to-all-start) | async-done | bytes 4194336 | tf_op jit(solution)/shard_map/all_to_all | solution.py:173
  68.6 5.8 %all-to-all-start.1 = ((bf16[128,8,2048]{2,1,0:T(8,128)(2,1)}), bf16[128,8,2048]{2,1,0:T(8,128)(2,1)}, u32[]{:S(2)}, u32[]{:S(2)}) async-start(bf16[128,8,2048]{2,1,0:T(8,128)(2,1)} %bitcast.57), calls=%async_computation.1 | async-start | bytes 8388608 | tf_op jit(solution)/shard_map/all_to_all | solution.py:173
  74.5 6.3 %fusion.8 = f32[1024,768]{1,0:T(8,128)S(1)} fusion(bf16[1,2048,768]{2,1,0:T(8,128)(2,1)} %param.13, bf16[128,8,2048]{2,1,0:T(8,128)(2,1)} %all-to-all-done), kind=kOutput, calls=%fused_computation.14 | convolution fusion | flops 3221225472 | bytes 10485760 | tf_op jit(solution)/shard_map/dot_general | solution.py:226
  80.8 8.6 %multiply_convert_fusion.2 = (bf16[1024,768]{1,0:T(8,128)(2,1)S(1)}, f32[1024,768]{1,0:T(8,128)}) fusion(f32[1024,768]{1,0:T(8,128)S(1)} %fusion.8, bf16[1,2048,768]{2,1,0:T(8,128)(2,1)S(1)} %copy-done.7, bf16[128,8,2048]{2,1,0:T(8,128)(2,1)} %all-to-all-done), kind=kOutput, calls=%fused_computation.19 | convolution fusion | flops 3225944064 | bytes 15204352 | tf_op jit(solution)/shard_map/dot_general | solution.py:226
  89.3 1.1 copy-done.9
  90.5 5.0 %convolution_convert_fusion = bf16[1024,2048]{1,0:T(8,128)(2,1)} fusion(bf16[1024,768]{1,0:T(8,128)(2,1)S(1)} %get-tuple-element.45, bf16[1,768,2048]{2,1,0:T(8,128)(2,1)S(1)} %copy-done), kind=kOutput, calls=%fused_computation.2 | convolution fusion | flops 3223322624 | bytes 8912896 | tf_op jit(solution)/shard_map/dot_general | solution.py:226
  95.5 31.2 %all-to-all-done.1 = bf16[128,8,2048]{2,1,0:T(8,128)(2,1)} async-done(((bf16[128,8,2048]{2,1,0:T(8,128)(2,1)}), bf16[128,8,2048]{2,1,0:T(8,128)(2,1)}, u32[]{:S(2)}, u32[]{:S(2)}) %all-to-all-start.1) | async-done | bytes 4194336 | tf_op jit(solution)/shard_map/all_to_all | solution.py:173
  126.6 6.0 %all-to-all-start.2 = ((bf16[128,8,2048]{2,1,0:T(8,128)(2,1)}), bf16[128,8,2048]{2,1,0:T(8,128)(2,1)}, u32[]{:S(2)}, u32[]{:S(2)}) async-start(bf16[128,8,2048]{2,1,0:T(8,128)(2,1)} %bitcast.59), calls=%async_computation.2 | async-start | bytes 8388608 | tf_op jit(solution)/shard_map/all_to_all | solution.py:173
  132.7 8.4 %multiply_convert_fusion = (bf16[1024,768]{1,0:T(8,128)(2,1)S(1)}, bf16[1024,768]{1,0:T(8,128)(2,1)S(1)}) fusion(f32[1024,768]{1,0:T(8,128)} %copy-done.13, f32[1024,768]{1,0:T(8,128)} %get-tuple-element.38, bf16[1024,2048]{1,0:T(8,128)(2,1)} %bitcast.9, bf16[1,768,2048]{2,1,0:T(8,128)(2,1)S(1)} %copy-done), kind=kOutput, calls=%fused_computation.16 | convolution fusion | flops 3231449088 | bytes 16777216 | tf_op jit(solution)/shard_map/dot_general | solution.py:226
  141.1 3.4 %fusion.6 = f32[1024,2048]{1,0:T(8,128)S(1)} fusion(bf16[1024,768]{1,0:T(8,128)(2,1)S(1)} %get-tuple-element.43, bf16[1,2048,768]{2,1,0:T(8,128)(2,1)S(1)} %copy-done.6), kind=kOutput, calls=%fused_computation.12 | convolution fusion | flops 3221225472 | bytes 13107200 | tf_op jit(solution)/shard_map/dot_general | solution.py:226
  144.6 3.7 %add_convert_fusion = bf16[1024,2048]{1,0:T(8,128)(2,1)S(1)} fusion(f32[1024,2048]{1,0:T(8,128)S(1)} %fusion.6, bf16[1024,768]{1,0:T(8,128)(2,1)S(1)} %get-tuple-element.44, bf16[1,2048,768]{2,1,0:T(8,128)(2,1)S(1)} %copy-done.8), kind=kOutput, calls=%fused_computation.1 | convolution fusion | flops 3225419776 | bytes 17301504 | tf_op jit(solution)/shard_map/dot_general | solution.py:226
  148.3 5.5 %multiply_reduce_fusion = f32[2048]{0:T(1024)S(1)} fusion(bf16[1024,2048]{1,0:T(8,128)(2,1)S(1)} %add_convert_fusion, bf16[128,8,2048]{2,1,0:T(8,128)(2,1)} %all-to-all-done), kind=kLoop, calls=%fused_computation | loop fusion | flops 8386560 | bytes 8396800 | tf_op jit(solution)/shard_map/reduce_sum | solution.py:311
  153.9 1.2 collective-permute-done
  155.1 2.1 collective-permute-start.3
  157.2 0.8 collective-permute-start.2
  158.0 1.3 collective-permute-start.1
  159.3 11.5 %collective-permute-done.3 = f32[1,2048]{1,0:T(1,128)S(1)} collective-permute-done((f32[1,2048]{1,0:T(1,128)S(1)}, f32[1,2048]{1,0:T(1,128)S(1)}, u32[]{:S(2)}, u32[]{:S(2)}) %collective-permute-start.3) | collective-permute-done | bytes 8224 | tf_op jit(solution)/shard_map/ppermute | solution.py:205
  170.8 2.6 collective-permute-done.2
  173.4 3.3 %collective-permute-done.1 = f32[1,2048]{1,0:T(1,128)S(1)} collective-permute-done((f32[1,2048]{1,0:T(1,128)S(1)}, f32[1,2048]{1,0:T(1,128)S(1)}, u32[]{:S(2)}, u32[]{:S(2)}) %collective-permute-start.1) | collective-permute-done | bytes 8224 | tf_op jit(solution)/shard_map/ppermute | solution.py:205
  176.7 8.0 %all-to-all-done.2 = bf16[128,8,2048]{2,1,0:T(8,128)(2,1)} async-done(((bf16[128,8,2048]{2,1,0:T(8,128)(2,1)}), bf16[128,8,2048]{2,1,0:T(8,128)(2,1)}, u32[]{:S(2)}, u32[]{:S(2)}) %all-to-all-start.2) | async-done | bytes 4194336 | tf_op jit(solution)/shard_map/all_to_all | solution.py:173
  184.7 6.1 %all-to-all-start.3 = ((bf16[128,8,2048]{2,1,0:T(8,128)(2,1)}), bf16[128,8,2048]{2,1,0:T(8,128)(2,1)}, u32[]{:S(2)}, u32[]{:S(2)}) async-start(bf16[128,8,2048]{2,1,0:T(8,128)(2,1)} %bitcast.56), calls=%async_computation.3 | async-start | bytes 8388608 | tf_op jit(solution)/shard_map/all_to_all | solution.py:173
  190.8 0.7 copy.16.probs
  191.5 0.7 copy.17.ids
  192.2 0.7 copy.15.ids
  192.9 2.1 routes.1
  195.0 2.8 %collective-permute-start.6 = (f32[1,2048]{1,0:T(1,128)S(1)}, f32[1,2048]{1,0:T(1,128)S(1)}, u32[]{:S(2)}, u32[]{:S(2)}) collective-permute-start(f32[1,2048]{1,0:T(1,128)S(1)} %add_add_fusion.1), channel_id=1, source_target_pairs={{0,24},{4,28},{8,16},{12,20},{16,8},{20,12},{24,0},{28,4},{32,56},... | collective-permute-start | bytes 24584 | tf_op jit(solution)/shard_map/ppermute | solution.py:205
  198.1 1.0 collective-permute-start.4
  199.1 7.0 %convolution_convert_fusion.1 = bf16[768,2048]{1,0:T(8,128)(2,1)} fusion(bf16[1024,768]{1,0:T(8,128)(2,1)S(1)} %copy-done.10, bf16[1024,2048]{1,0:T(8,128)(2,1)} %bitcast.9), kind=kOutput, calls=%fused_computation.3 | convolution fusion | flops 3222798336 | bytes 8912896 | tf_op jit(solution)/shard_map/dot_general | solution.py:226
  206.1 7.5 %convolution_convert_fusion.3 = bf16[2048,768]{1,0:T(8,128)(2,1)} fusion(bf16[1024,768]{1,0:T(8,128)(2,1)S(1)} %copy-done.12, bf16[128,8,2048]{2,1,0:T(8,128)(2,1)} %all-to-all-done), kind=kOutput, calls=%fused_computation.5 | convolution fusion | flops 3222798336 | bytes 8912896 | tf_op jit(solution)/shard_map/dot_general | solution.py:226
  213.6 7.4 %convolution_convert_fusion.2 = bf16[2048,768]{1,0:T(8,128)(2,1)} fusion(bf16[1024,768]{1,0:T(8,128)(2,1)S(1)} %copy-done.15, bf16[128,8,2048]{2,1,0:T(8,128)(2,1)} %all-to-all-done), kind=kOutput, calls=%fused_computation.4 | convolution fusion | flops 3222798336 | bytes 8912896 | tf_op jit(solution)/shard_map/dot_general | solution.py:226
  221.1 5.4 %combine.1 = (bf16[64,2048]{1,0:T(8,128)(2,1)}, f32[8,64]{1,0:T(8,128)}) custom-call(s32[1]{0:T(128)} %bitcast.quarter, s32[64,8]{1,0:T(8,128)} %copy.17.ids, bf16[64,1024]{1,0:T(8,128)(2,1)} %get-tuple-element.47.routes, bf16[192,1024]{1,0:T(8,128)(2,1)} %get-tuple-element.48.weights, bf16[1024,2048]{1,0:T(8,128)(2,1)} %bitcast.12.rows, ...), custom_call_target="tpu_custom_call" | custom-call | flops 1073741824 | bytes 4194304 | tf_op jit(solution)/shard_map/combine/pallas_call | solution.py:326
  226.5 16.6 %all-to-all-done.3 = bf16[128,8,2048]{2,1,0:T(8,128)(2,1)} async-done(((bf16[128,8,2048]{2,1,0:T(8,128)(2,1)}), bf16[128,8,2048]{2,1,0:T(8,128)(2,1)}, u32[]{:S(2)}, u32[]{:S(2)}) %all-to-all-start.3) | async-done | bytes 4194336 | tf_op jit(solution)/shard_map/all_to_all | solution.py:173
  243.0 4.3 %norm_grad.1 = (bf16[32,2048]{1,0:T(8,128)(2,1)}, bf16[32,2048]{1,0:T(8,128)(2,1)}, bf16[256,2048]{1,0:T(8,128)(2,1)}) custom-call(s32[1]{0:T(128)} %bitcast.quarter, bf16[64,1024]{1,0:T(8,128)(2,1)} %get-tuple-element.47.routes, bf16[1024,2048]{1,0:T(8,128)(2,1)} %bitcast.15.rows, bf16[256,2048]{1,0:T(8,128)(2,1)} %hidden.5, f32[1,2048]{1,0:T(1,128)} %bitcast.61, ...), custom_call_target="tpu_custom_call" | custom-call | flops 268435456 | bytes 4194304 | tf_op jit(solution)/shard_map/norm_grad/pallas_call | solution.py:357
  247.9 2.6 collective-permute-start.10
  251.2 3.0 %collective-permute-done.13 = f32[1,2048]{1,0:T(1,128)S(1)} collective-permute-done((f32[1,2048]{1,0:T(1,128)S(1)}, f32[1,2048]{1,0:T(1,128)S(1)}, u32[]{:S(2)}, u32[]{:S(2)}) %collective-permute-start.13) | collective-permute-done | bytes 8224 | tf_op jit(solution)/shard_map/ppermute | solution.py:205
  254.2 1.5 collective-permute-start.14
  255.7 2.0 collective-permute-start.8
  257.7 1.7 collective-permute-done.14
  260.1 3.2 %collective-permute-start.12 = (bf16[32,2048]{1,0:T(8,128)(2,1)S(1)}, bf16[32,2048]{1,0:T(8,128)(2,1)S(1)}, u32[]{:S(2)}, u32[]{:S(2)}) collective-permute-start(bf16[32,2048]{1,0:T(8,128)(2,1)S(1)} %collective-permute-done.10), channel_id=1, source_target_pairs={{0,3},{1,0},{2,1},{3,2},{4,7},{5,4},{6,5},{7,6},{8,11},{9,8},{10,9... | collective-permute-start | bytes 393224 | tf_op jit(solution)/shard_map/ppermute | solution.py:183
  263.3 0.7 constant_dynamic-update-slice_fusion.5
  264.0 0.7 constant_dynamic-update-slice_fusion.4
  264.6 0.7 constant_dynamic-update-slice_fusion.3
  265.3 0.7 constant_dynamic-update-slice_fusion.2
  266.2 0.7 constant_dynamic-update-slice_fusion.1
  266.9 0.7 constant_dynamic-update-slice_fusion
  (52 shorter events, 2.7 us)
Async XLA Ops:
  0.6 89.8 %copy-start = (bf16[1,768,2048]{2,1,0:T(8,128)(2,1)S(1)}, bf16[1,768,2048]{2,1,0:T(8,128)(2,1)}, u32[]{:S(2)}) copy-start(bf16[1,768,2048]{2,1,0:T(8,128)(2,1)} %param.15) | copy-start | bytes 9437188
  4.7 63.9 %all-to-all-start = ((bf16[128,8,2048]{2,1,0:T(8,128)(2,1)}), bf16[128,8,2048]{2,1,0:T(8,128)(2,1)}, u32[]{:S(2)}, u32[]{:S(2)}) async-start(bf16[128,8,2048]{2,1,0:T(8,128)(2,1)} %bitcast.58), calls=%async_computation | async-start | bytes 8388608 | tf_op jit(solution)/shard_map/all_to_all | solution.py:173
  68.6 58.1 %all-to-all-start.1 = ((bf16[128,8,2048]{2,1,0:T(8,128)(2,1)}), bf16[128,8,2048]{2,1,0:T(8,128)(2,1)}, u32[]{:S(2)}, u32[]{:S(2)}) async-start(bf16[128,8,2048]{2,1,0:T(8,128)(2,1)} %bitcast.57), calls=%async_computation.1 | async-start | bytes 8388608 | tf_op jit(solution)/shard_map/all_to_all | solution.py:173
  74.4 6.3 %copy-start.7 = (bf16[1,2048,768]{2,1,0:T(8,128)(2,1)S(1)}, bf16[1,2048,768]{2,1,0:T(8,128)(2,1)}, u32[]{:S(2)}) copy-start(bf16[1,2048,768]{2,1,0:T(8,128)(2,1)} %param.14) | copy-start | bytes 9437188
  80.8 8.6 %copy-start.13 = (f32[1024,768]{1,0:T(8,128)}, f32[1024,768]{1,0:T(8,128)S(1)}, u32[]{:S(2)}) copy-start(f32[1024,768]{1,0:T(8,128)S(1)} %fusion.8) | copy-start | bytes 9437188
  89.3 1.1 copy-start.9
  126.6 58.1 %all-to-all-start.2 = ((bf16[128,8,2048]{2,1,0:T(8,128)(2,1)}), bf16[128,8,2048]{2,1,0:T(8,128)(2,1)}, u32[]{:S(2)}, u32[]{:S(2)}) async-start(bf16[128,8,2048]{2,1,0:T(8,128)(2,1)} %bitcast.59), calls=%async_computation.2 | async-start | bytes 8388608 | tf_op jit(solution)/shard_map/all_to_all | solution.py:173
  132.7 8.4 %copy-start.6 = (bf16[1,2048,768]{2,1,0:T(8,128)(2,1)S(1)}, bf16[1,2048,768]{2,1,0:T(8,128)(2,1)}, u32[]{:S(2)}) copy-start(bf16[1,2048,768]{2,1,0:T(8,128)(2,1)} %param.13) | copy-start | bytes 9437188
  141.1 3.5 %copy-start.11 = (bf16[1024,768]{1,0:T(8,128)(2,1)}, bf16[1024,768]{1,0:T(8,128)(2,1)S(1)}, u32[]{:S(2)}) copy-start(bf16[1024,768]{1,0:T(8,128)(2,1)S(1)} %get-tuple-element.43) | copy-start | bytes 4718596
  141.1 3.5 %copy-start.14 = (bf16[1024,768]{1,0:T(8,128)(2,1)}, bf16[1024,768]{1,0:T(8,128)(2,1)S(1)}, u32[]{:S(2)}) copy-start(bf16[1024,768]{1,0:T(8,128)(2,1)S(1)} %get-tuple-element.44) | copy-start | bytes 4718596
  141.1 3.5 %copy-start.8 = (bf16[1,2048,768]{2,1,0:T(8,128)(2,1)S(1)}, bf16[1,2048,768]{2,1,0:T(8,128)(2,1)}, u32[]{:S(2)}) copy-start(bf16[1,2048,768]{2,1,0:T(8,128)(2,1)} %param.14) | copy-start | bytes 9437188
  148.3 5.5 %copy-start.2 = (bf16[1024,2048]{1,0:T(8,128)(2,1)}, bf16[1024,2048]{1,0:T(8,128)(2,1)S(1)}, u32[]{:S(2)}) copy-start(bf16[1024,2048]{1,0:T(8,128)(2,1)S(1)} %add_convert_fusion) | copy-start | bytes 12582916
  148.3 5.5 %copy-start.3 = (f32[2048]{0:T(1024)S(1)}, f32[2048]{0:T(1024)}, u32[]{:S(2)}) copy-start(f32[2048]{0:T(1024)} %param.9) | copy-start | bytes 24580
  153.8 1.3 collective-permute-start
  155.1 15.7 %collective-permute-start.3 = (f32[1,2048]{1,0:T(1,128)S(1)}, f32[1,2048]{1,0:T(1,128)S(1)}, u32[]{:S(2)}, u32[]{:S(2)}) collective-permute-start(f32[1,2048]{1,0:T(1,128)S(1)} %add.98), channel_id=1, source_target_pairs={{0,3},{1,2},{2,1},{3,0},{4,7},{5,6},{6,5},{7,4},{8,11},{9,10},{10,... | collective-permute-start | bytes 24584 | tf_op jit(solution)/shard_map/ppermute | solution.py:205
  157.2 16.2 %collective-permute-start.2 = (f32[1,2048]{1,0:T(1,128)S(1)}, f32[1,2048]{1,0:T(1,128)S(1)}, u32[]{:S(2)}, u32[]{:S(2)}) collective-permute-start(f32[1,2048]{1,0:T(1,128)S(1)} %add.98), channel_id=1, source_target_pairs={{0,2},{1,3},{2,0},{3,1},{4,6},{5,7},{6,4},{7,5},{8,10},{9,11},{10,... | collective-permute-start | bytes 24584 | tf_op jit(solution)/shard_map/ppermute | solution.py:205
  158.0 18.7 %collective-permute-start.1 = (f32[1,2048]{1,0:T(1,128)S(1)}, f32[1,2048]{1,0:T(1,128)S(1)}, u32[]{:S(2)}, u32[]{:S(2)}) collective-permute-start(f32[1,2048]{1,0:T(1,128)S(1)} %add.98), channel_id=1, source_target_pairs={{0,1},{1,0},{2,3},{3,2},{4,5},{5,4},{6,7},{7,6},{8,9},{9,8},{10,11... | collective-permute-start | bytes 24584 | tf_op jit(solution)/shard_map/ppermute | solution.py:205
  184.7 6.1 %copy-start.5 = (f32[64,8]{0,1:T(8,128)S(1)}, f32[64,8]{0,1:T(8,128)}, u32[]{:S(2)}) copy-start(f32[64,8]{0,1:T(8,128)} %param.11) | copy-start | bytes 6148
  184.7 6.8 %copy-start.4 = (s32[64,8]{0,1:T(8,128)S(1)}, s32[64,8]{0,1:T(8,128)}, u32[]{:S(2)}) copy-start(s32[64,8]{0,1:T(8,128)} %param.10) | copy-start | bytes 6148
  184.7 14.4 %copy-start.10 = (bf16[1024,768]{1,0:T(8,128)(2,1)S(1)}, bf16[1024,768]{1,0:T(8,128)(2,1)}, u32[]{:S(2)}) copy-start(bf16[1024,768]{1,0:T(8,128)(2,1)} %copy-done.9) | copy-start | bytes 4718596
  184.7 58.3 %all-to-all-start.3 = ((bf16[128,8,2048]{2,1,0:T(8,128)(2,1)}), bf16[128,8,2048]{2,1,0:T(8,128)(2,1)}, u32[]{:S(2)}, u32[]{:S(2)}) async-start(bf16[128,8,2048]{2,1,0:T(8,128)(2,1)} %bitcast.56), calls=%async_computation.3 | async-start | bytes 8388608 | tf_op jit(solution)/shard_map/all_to_all | solution.py:173
  195.0 11.1 %copy-start.12 = (bf16[1024,768]{1,0:T(8,128)(2,1)S(1)}, bf16[1024,768]{1,0:T(8,128)(2,1)}, u32[]{:S(2)}) copy-start(bf16[1024,768]{1,0:T(8,128)(2,1)} %copy-done.11) | copy-start | bytes 4718596
  195.0 31.4 %collective-permute-start.6 = (f32[1,2048]{1,0:T(1,128)S(1)}, f32[1,2048]{1,0:T(1,128)S(1)}, u32[]{:S(2)}, u32[]{:S(2)}) collective-permute-start(f32[1,2048]{1,0:T(1,128)S(1)} %add_add_fusion.1), channel_id=1, source_target_pairs={{0,24},{4,28},{8,16},{12,20},{16,8},{20,12},{24,0},{28,4},{32,56},... | collective-permute-start | bytes 24584 | tf_op jit(solution)/shard_map/ppermute | solution.py:205
  197.8 28.7 %collective-permute-start.5 = (f32[1,2048]{1,0:T(1,128)S(1)}, f32[1,2048]{1,0:T(1,128)S(1)}, u32[]{:S(2)}, u32[]{:S(2)}) collective-permute-start(f32[1,2048]{1,0:T(1,128)S(1)} %add_add_fusion.1), channel_id=1, source_target_pairs={{0,16},{4,20},{8,24},{12,28},{16,0},{20,4},{24,8},{28,12},{32,48},... | collective-permute-start | bytes 24584 | tf_op jit(solution)/shard_map/ppermute | solution.py:205
  198.1 28.3 %collective-permute-start.4 = (f32[1,2048]{1,0:T(1,128)S(1)}, f32[1,2048]{1,0:T(1,128)S(1)}, u32[]{:S(2)}, u32[]{:S(2)}) collective-permute-start(f32[1,2048]{1,0:T(1,128)S(1)} %add_add_fusion.1), channel_id=1, source_target_pairs={{0,8},{4,12},{8,0},{12,4},{16,24},{20,28},{24,16},{28,20},{32,40},... | collective-permute-start | bytes 24584 | tf_op jit(solution)/shard_map/ppermute | solution.py:205
  206.1 7.5 %copy-start.15 = (bf16[1024,768]{1,0:T(8,128)(2,1)S(1)}, bf16[1024,768]{1,0:T(8,128)(2,1)}, u32[]{:S(2)}) copy-start(bf16[1024,768]{1,0:T(8,128)(2,1)} %copy-done.14) | copy-start | bytes 4718596
  243.0 24.5 %copy-start.1 = (bf16[1,768,2048]{2,1,0:T(8,128)(2,1)S(1)}, bf16[1,768,2048]{2,1,0:T(8,128)(2,1)}, u32[]{:S(2)}) copy-start(bf16[1,768,2048]{2,1,0:T(8,128)(2,1)} %param.15) | copy-start | bytes 9437188
  247.3 12.7 %collective-permute-start.7 = (bf16[32,2048]{1,0:T(8,128)(2,1)}, bf16[32,2048]{1,0:T(8,128)(2,1)S(1)}, u32[]{:S(2)}, u32[]{:S(2)}) collective-permute-start(bf16[32,2048]{1,0:T(8,128)(2,1)} %get-tuple-element.56), channel_id=1, source_target_pairs={{0,1},{1,2},{2,3},{3,0},{4,5},{5,6},{6,7},{7,4},{8,9},{9,10},{10,1... | collective-permute-start | bytes 393224 | tf_op jit(solution)/shard_map/ppermute | solution.py:183
  247.9 12.1 %collective-permute-start.10 = (bf16[32,2048]{1,0:T(8,128)(2,1)}, bf16[32,2048]{1,0:T(8,128)(2,1)S(1)}, u32[]{:S(2)}, u32[]{:S(2)}) collective-permute-start(bf16[32,2048]{1,0:T(8,128)(2,1)} %get-tuple-element.57), channel_id=1, source_target_pairs={{0,3},{1,0},{2,1},{3,2},{4,7},{5,4},{6,5},{7,6},{8,11},{9,8},{10,9... | collective-permute-start | bytes 393224 | tf_op jit(solution)/shard_map/ppermute | solution.py:183
  250.5 3.7 %collective-permute-start.13 = (f32[1,2048]{1,0:T(1,128)S(1)}, f32[1,2048]{1,0:T(1,128)S(1)}, u32[]{:S(2)}, u32[]{:S(2)}) collective-permute-start(f32[1,2048]{1,0:T(1,128)S(1)} %add_add_fusion), channel_id=1, source_target_pairs={{0,32},{4,36},{8,40},{12,44},{16,48},{20,52},{24,56},{28,60},{32,0... | collective-permute-start | bytes 24584 | tf_op jit(solution)/shard_map/ppermute | solution.py:205
  254.2 5.2 %collective-permute-start.14 = (f32[1,2048]{1,0:T(1,128)S(1)}, f32[1,2048]{1,0:T(1,128)S(1)}, u32[]{:S(2)}, u32[]{:S(2)}) collective-permute-start(f32[1,2048]{1,0:T(1,128)S(1)} %add.117), channel_id=1, source_target_pairs={{0,64},{4,68},{8,72},{12,76},{16,80},{20,84},{24,88},{28,92},{32,9... | collective-permute-start | bytes 24584 | tf_op jit(solution)/shard_map/ppermute | solution.py:205
  255.7 9.0 %collective-permute-start.9 = (bf16[32,2048]{1,0:T(8,128)(2,1)}, bf16[32,2048]{1,0:T(8,128)(2,1)S(1)}, u32[]{:S(2)}, u32[]{:S(2)}) collective-permute-start(bf16[32,2048]{1,0:T(8,128)(2,1)} %get-tuple-element.56), channel_id=1, source_target_pairs={{0,3},{1,0},{2,1},{3,2},{4,7},{5,4},{6,5},{7,6},{8,11},{9,8},{10,9... | collective-permute-start | bytes 393224 | tf_op jit(solution)/shard_map/ppermute | solution.py:183
  255.7 8.3 %collective-permute-start.8 = (bf16[32,2048]{1,0:T(8,128)(2,1)}, bf16[32,2048]{1,0:T(8,128)(2,1)S(1)}, u32[]{:S(2)}, u32[]{:S(2)}) collective-permute-start(bf16[32,2048]{1,0:T(8,128)(2,1)} %get-tuple-element.57), channel_id=1, source_target_pairs={{0,1},{1,2},{2,3},{3,0},{4,5},{5,6},{6,7},{7,4},{8,9},{9,10},{10,1... | collective-permute-start | bytes 393224 | tf_op jit(solution)/shard_map/ppermute | solution.py:183
  260.0 6.2 %collective-permute-start.11 = (bf16[32,2048]{1,0:T(8,128)(2,1)S(1)}, bf16[32,2048]{1,0:T(8,128)(2,1)S(1)}, u32[]{:S(2)}, u32[]{:S(2)}) collective-permute-start(bf16[32,2048]{1,0:T(8,128)(2,1)S(1)} %collective-permute-done.7), channel_id=1, source_target_pairs={{0,1},{1,2},{2,3},{3,0},{4,5},{5,6},{6,7},{7,4},{8,9},{9,10},{10,1... | collective-permute-start | bytes 393224 | tf_op jit(solution)/shard_map/ppermute | solution.py:183
  260.1 6.8 %collective-permute-start.12 = (bf16[32,2048]{1,0:T(8,128)(2,1)S(1)}, bf16[32,2048]{1,0:T(8,128)(2,1)S(1)}, u32[]{:S(2)}, u32[]{:S(2)}) collective-permute-start(bf16[32,2048]{1,0:T(8,128)(2,1)S(1)} %collective-permute-done.10), channel_id=1, source_target_pairs={{0,3},{1,0},{2,1},{3,2},{4,7},{5,4},{6,5},{7,6},{8,11},{9,8},{10,9... | collective-permute-start | bytes 393224 | tf_op jit(solution)/shard_map/ppermute | solution.py:183

commit v7 on v4

--- a/solution.py
+++ b/solution.py
@@ -175,7 +175,7 @@
     rows = block.shape[0]
     moved = [
         (step, lax.ppermute(block, "tensor", [(i, (i + step) % size) for i in range(size)]))
-        for step in (1, 3, 2)
+        for step in (2, 1, 3)
     ]
     for step, piece in moved:
         origin = (mine + size - step) % size
@@ -291,7 +291,7 @@
     gate_pgrad = (act_grad * up_pre * sigma * (1.0 + gate_pre * (1.0 - sigma))).astype(BF16)
     up_pgrad = (act_grad * silu_vals).astype(BF16)
     back = dot(gate_pgrad, gate_w, ((1,), (1,))) + dot(up_pgrad, up_w, ((1,), (1,)))
-    back = back.astype(BF16)
+    back = lax.optimization_barrier(back.astype(BF16))
     gain_part = jnp.sum(back.astype(F32) * inputs.astype(F32), axis=0, keepdims=True) / gain
     gain_part = add_from(gain_part, "dp", (1,))
     gain_part = add_from(gain_part, "tensor", (1, 2, 3))

time: 265 us -> 266 us (level)
  other arithmetic: 0.67 us -> 6.14 us
  matrix products: 61.9 us -> 57.3 us
    reduce_sum x0 -> x1, other arithmetic: none -> 5.47 us  [per_device(): jnp.sum(back.astype(F32) * inputs.astype(F32), axis=0, keepdims=True) / gain]
    dot_general x9, matrix products: 61.9 us -> 57.3 us  [dot(): return lax.dot_general(a, b, (dims, ((), ())), preferred_element_type=F32)]
    ppermute x9, waiting for transfers between devices: 25.9 us -> 22.2 us  [add_from(): lax.ppermute(value, axis, [(i, i ^ distance) for i in range(size)])]
  transfers between devices with their start and end apart: 16 -> 16, of which waited for: 12 -> 11; matrix products, arithmetic and copies ran while one was open for 25% -> 26% of each run, Pallas kernels for 5% -> 5%
where the time goes in v7:
time: 266 us; the launch traced here: 264 us
  waiting for transfers between devices  128 us (48%)
  matrix products  57.3 us (22%)
  starting transfers between devices  45.6 us (17%)
  Pallas kernels  20.4 us (8%)
  local copies, waits for them, and re-layouts  6.42 us (2%)
  other arithmetic  6.14 us (2%)
    all_to_all x4, waiting for transfers between devices, exchange(): return lax.all_to_all(block, AXES, split_axis=0, concat_axis=0, tiled=True)  103 us
    dot_general x9, matrix products, dot(): return lax.dot_general(a, b, (dims, ((), ())), preferred_element_type=F32)  57.3 us
    all_to_all x4, starting transfers between devices, exchange(): return lax.all_to_all(block, AXES, split_axis=0, concat_axis=0, tiled=True)  29.7 us
    ppermute x9, waiting for transfers between devices, add_from(): lax.ppermute(value, axis, [(i, i ^ distance) for i in range(size)])  22.2 us
    ppermute x9, starting transfers between devices, add_from(): lax.ppermute(value, axis, [(i, i ^ distance) for i in range(size)])  10.3 us
    ppermute x3, starting transfers between devices, gather_group(): lax.ppermute(block, 'tensor', [(i, (i + step) % size) for i in range(size)])  5.64 us
    reduce_sum x1, other arithmetic, per_device(): jnp.sum(back.astype(F32) * inputs.astype(F32), axis=0, keepdims=True) / gain  5.47 us
    pallas_call x1, Pallas kernels, per_device(): pl.pallas_call(combine_kernel, grid_spec=pltpu.PrefetchScalarGridSpec(num...  5.37 us
  transfers between devices with their start and end apart: 16, of which 11 were waited for; matrix products, arithmetic and copies ran while one was open for 26% of the time, Pallas kernels for 5%

profile of v7, /device:TPU:0, one launch (start us, length us, event | category | flops | bytes accessed | tf_op | source)
XLA Modules:
  0.0 264.3 jit_solution(2133710943717758449)
XLA Ops:
  0.7 4.0 %pack_normed.1 = bf16[1024,2048]{1,0:T(8,128)(2,1)} custom-call(s32[1]{0:T(128)} %bitcast.quarter, s32[8,64]{1,0:T(8,128)} %bitcast.62, bf16[256,2048]{1,0:T(8,128)(2,1)} %hidden.5, f32[1,2048]{1,0:T(1,128)} %bitcast.60), custom_call_target="tpu_custom_call" | custom-call | flops 268435456 | bytes 4194304 | tf_op jit(solution)/shard_map/pack_normed/pallas_call | solution.py:230
  4.7 11.7 %all-to-all-start = ((bf16[128,8,2048]{2,1,0:T(8,128)(2,1)}), bf16[128,8,2048]{2,1,0:T(8,128)(2,1)}, u32[]{:S(2)}, u32[]{:S(2)}) async-start(bf16[128,8,2048]{2,1,0:T(8,128)(2,1)} %bitcast.58), calls=%async_computation | async-start | bytes 8388608 | tf_op jit(solution)/shard_map/all_to_all | solution.py:169
  16.4 4.7 %pack_scaled.1 = bf16[1024,2048]{1,0:T(8,128)(2,1)} custom-call(s32[8,64]{1,0:T(8,128)} %bitcast.63, f32[8,64]{1,0:T(8,128)} %bitcast.66, bf16[64,2048]{1,0:T(8,128)(2,1)} %grad.5), custom_call_target="tpu_custom_call" | custom-call | flops 268435456 | bytes 4194304 | tf_op jit(solution)/shard_map/pack_scaled/pallas_call | solution.py:253
  21.1 47.5 %all-to-all-done = bf16[128,8,2048]{2,1,0:T(8,128)(2,1)} async-done(((bf16[128,8,2048]{2,1,0:T(8,128)(2,1)}), bf16[128,8,2048]{2,1,0:T(8,128)(2,1)}, u32[]{:S(2)}, u32[]{:S(2)}) %all-to-all-start) | async-done | bytes 4194336 | tf_op jit(solution)/shard_map/all_to_all | solution.py:169
  68.6 5.9 %all-to-all-start.1 = ((bf16[128,8,2048]{2,1,0:T(8,128)(2,1)}), bf16[128,8,2048]{2,1,0:T(8,128)(2,1)}, u32[]{:S(2)}, u32[]{:S(2)}) async-start(bf16[128,8,2048]{2,1,0:T(8,128)(2,1)} %bitcast.57), calls=%async_computation.1 | async-start | bytes 8388608 | tf_op jit(solution)/shard_map/all_to_all | solution.py:169
  74.4 6.3 %fusion.8 = f32[1024,768]{1,0:T(8,128)S(1)} fusion(bf16[1,2048,768]{2,1,0:T(8,128)(2,1)} %param.13, bf16[128,8,2048]{2,1,0:T(8,128)(2,1)} %all-to-all-done), kind=kOutput, calls=%fused_computation.14 | convolution fusion | flops 3221225472 | bytes 10485760 | tf_op jit(solution)/shard_map/dot_general | solution.py:210
  80.7 8.6 %multiply_convert_fusion.2 = (bf16[1024,768]{1,0:T(8,128)(2,1)S(1)}, f32[1024,768]{1,0:T(8,128)}) fusion(f32[1024,768]{1,0:T(8,128)S(1)} %fusion.8, bf16[1,2048,768]{2,1,0:T(8,128)(2,1)S(1)} %copy-done.7, bf16[128,8,2048]{2,1,0:T(8,128)(2,1)} %all-to-all-done), kind=kOutput, calls=%fused_computation.19 | convolution fusion | flops 3225944064 | bytes 15204352 | tf_op jit(solution)/shard_map/dot_general | solution.py:210
  89.3 1.1 copy-done.9
  90.4 5.0 %convolution_convert_fusion = bf16[1024,2048]{1,0:T(8,128)(2,1)} fusion(bf16[1024,768]{1,0:T(8,128)(2,1)S(1)} %get-tuple-element.44, bf16[1,768,2048]{2,1,0:T(8,128)(2,1)S(1)} %copy-done), kind=kOutput, calls=%fused_computation.2 | convolution fusion | flops 3223322624 | bytes 8912896 | tf_op jit(solution)/shard_map/dot_general | solution.py:210
  95.5 31.2 %all-to-all-done.1 = bf16[128,8,2048]{2,1,0:T(8,128)(2,1)} async-done(((bf16[128,8,2048]{2,1,0:T(8,128)(2,1)}), bf16[128,8,2048]{2,1,0:T(8,128)(2,1)}, u32[]{:S(2)}, u32[]{:S(2)}) %all-to-all-start.1) | async-done | bytes 4194336 | tf_op jit(solution)/shard_map/all_to_all | solution.py:169
  126.6 6.0 %all-to-all-start.2 = ((bf16[128,8,2048]{2,1,0:T(8,128)(2,1)}), bf16[128,8,2048]{2,1,0:T(8,128)(2,1)}, u32[]{:S(2)}, u32[]{:S(2)}) async-start(bf16[128,8,2048]{2,1,0:T(8,128)(2,1)} %bitcast.59), calls=%async_computation.2 | async-start | bytes 8388608 | tf_op jit(solution)/shard_map/all_to_all | solution.py:169
  132.7 8.4 %multiply_convert_fusion = (bf16[1024,768]{1,0:T(8,128)(2,1)S(1)}, bf16[1024,768]{1,0:T(8,128)(2,1)S(1)}) fusion(f32[1024,768]{1,0:T(8,128)} %copy-done.13, f32[1024,768]{1,0:T(8,128)} %get-tuple-element.37, bf16[1024,2048]{1,0:T(8,128)(2,1)} %bitcast.9, bf16[1,768,2048]{2,1,0:T(8,128)(2,1)S(1)} %copy-done), kind=kOutput, calls=%fused_computation.16 | convolution fusion | flops 3231449088 | bytes 16777216 | tf_op jit(solution)/shard_map/dot_general | solution.py:210
  141.1 3.4 %fusion.6 = f32[1024,2048]{1,0:T(8,128)S(1)} fusion(bf16[1024,768]{1,0:T(8,128)(2,1)S(1)} %get-tuple-element.42, bf16[1,2048,768]{2,1,0:T(8,128)(2,1)S(1)} %copy-done.6), kind=kOutput, calls=%fused_computation.12 | convolution fusion | flops 3221225472 | bytes 13107200 | tf_op jit(solution)/shard_map/dot_general | solution.py:210
  144.6 3.7 %add_convert_fusion = bf16[1024,2048]{1,0:T(8,128)(2,1)S(1)} fusion(f32[1024,2048]{1,0:T(8,128)S(1)} %fusion.6, bf16[1024,768]{1,0:T(8,128)(2,1)S(1)} %get-tuple-element.43, bf16[1,2048,768]{2,1,0:T(8,128)(2,1)S(1)} %copy-done.8), kind=kOutput, calls=%fused_computation.1 | convolution fusion | flops 3225419776 | bytes 17301504 | tf_op jit(solution)/shard_map/dot_general | solution.py:210
  148.3 5.5 %multiply_reduce_fusion = f32[2048]{0:T(1024)S(1)} fusion(bf16[1024,2048]{1,0:T(8,128)(2,1)S(1)} %add_convert_fusion, bf16[128,8,2048]{2,1,0:T(8,128)(2,1)} %all-to-all-done), kind=kLoop, calls=%fused_computation | loop fusion | flops 8386560 | bytes 8396800 | tf_op jit(solution)/shard_map/reduce_sum | solution.py:295
  153.9 1.2 collective-permute-done
  155.1 2.1 collective-permute-start.3
  157.1 0.8 collective-permute-start.2
  157.9 1.3 collective-permute-start.1
  159.3 11.5 %collective-permute-done.3 = f32[1,2048]{1,0:T(1,128)S(1)} collective-permute-done((f32[1,2048]{1,0:T(1,128)S(1)}, f32[1,2048]{1,0:T(1,128)S(1)}, u32[]{:S(2)}, u32[]{:S(2)}) %collective-permute-start.3) | collective-permute-done | bytes 8224 | tf_op jit(solution)/shard_map/ppermute | solution.py:189
  170.7 2.6 collective-permute-done.2
  173.3 3.3 %collective-permute-done.1 = f32[1,2048]{1,0:T(1,128)S(1)} collective-permute-done((f32[1,2048]{1,0:T(1,128)S(1)}, f32[1,2048]{1,0:T(1,128)S(1)}, u32[]{:S(2)}, u32[]{:S(2)}) %collective-permute-start.1) | collective-permute-done | bytes 8224 | tf_op jit(solution)/shard_map/ppermute | solution.py:189
  176.7 8.0 %all-to-all-done.2 = bf16[128,8,2048]{2,1,0:T(8,128)(2,1)} async-done(((bf16[128,8,2048]{2,1,0:T(8,128)(2,1)}), bf16[128,8,2048]{2,1,0:T(8,128)(2,1)}, u32[]{:S(2)}, u32[]{:S(2)}) %all-to-all-start.2) | async-done | bytes 4194336 | tf_op jit(solution)/shard_map/all_to_all | solution.py:169
  184.7 6.1 %all-to-all-start.3 = ((bf16[128,8,2048]{2,1,0:T(8,128)(2,1)}), bf16[128,8,2048]{2,1,0:T(8,128)(2,1)}, u32[]{:S(2)}, u32[]{:S(2)}) async-start(bf16[128,8,2048]{2,1,0:T(8,128)(2,1)} %bitcast.56), calls=%async_computation.3 | async-start | bytes 8388608 | tf_op jit(solution)/shard_map/all_to_all | solution.py:169
  190.8 0.7 copy.16.probs
  191.5 0.7 copy.17.ids
  192.2 0.7 copy.15.ids
  192.9 2.1 routes.1
  195.0 2.8 %collective-permute-start.6 = (f32[1,2048]{1,0:T(1,128)S(1)}, f32[1,2048]{1,0:T(1,128)S(1)}, u32[]{:S(2)}, u32[]{:S(2)}) collective-permute-start(f32[1,2048]{1,0:T(1,128)S(1)} %add_add_fusion.1), channel_id=1, source_target_pairs={{0,24},{4,28},{8,16},{12,20},{16,8},{20,12},{24,0},{28,4},{32,56},... | collective-permute-start | bytes 24584 | tf_op jit(solution)/shard_map/ppermute | solution.py:189
  198.1 1.0 collective-permute-start.4
  199.1 7.0 %convolution_convert_fusion.1 = bf16[768,2048]{1,0:T(8,128)(2,1)} fusion(bf16[1024,768]{1,0:T(8,128)(2,1)S(1)} %copy-done.10, bf16[1024,2048]{1,0:T(8,128)(2,1)} %bitcast.9), kind=kOutput, calls=%fused_computation.3 | convolution fusion | flops 3222798336 | bytes 8912896 | tf_op jit(solution)/shard_map/dot_general | solution.py:210
  206.1 7.5 %convolution_convert_fusion.3 = bf16[2048,768]{1,0:T(8,128)(2,1)} fusion(bf16[1024,768]{1,0:T(8,128)(2,1)S(1)} %copy-done.12, bf16[128,8,2048]{2,1,0:T(8,128)(2,1)} %all-to-all-done), kind=kOutput, calls=%fused_computation.5 | convolution fusion | flops 3222798336 | bytes 8912896 | tf_op jit(solution)/shard_map/dot_general | solution.py:210
  213.6 7.4 %convolution_convert_fusion.2 = bf16[2048,768]{1,0:T(8,128)(2,1)} fusion(bf16[1024,768]{1,0:T(8,128)(2,1)S(1)} %copy-done.15, bf16[128,8,2048]{2,1,0:T(8,128)(2,1)} %all-to-all-done), kind=kOutput, calls=%fused_computation.4 | convolution fusion | flops 3222798336 | bytes 8912896 | tf_op jit(solution)/shard_map/dot_general | solution.py:210
  221.0 5.4 %combine.1 = (bf16[64,2048]{1,0:T(8,128)(2,1)}, f32[8,64]{1,0:T(8,128)}) custom-call(s32[1]{0:T(128)} %bitcast.quarter, s32[64,8]{1,0:T(8,128)} %copy.17.ids, bf16[64,1024]{1,0:T(8,128)(2,1)} %get-tuple-element.46.routes, bf16[192,1024]{1,0:T(8,128)(2,1)} %get-tuple-element.47.weights, bf16[1024,2048]{1,0:T(8,128)(2,1)} %bitcast.12.rows, ...), custom_call_target="tpu_custom_call" | custom-call | flops 1073741824 | bytes 4194304 | tf_op jit(solution)/shard_map/combine/pallas_call | solution.py:310
  226.5 16.6 %all-to-all-done.3 = bf16[128,8,2048]{2,1,0:T(8,128)(2,1)} async-done(((bf16[128,8,2048]{2,1,0:T(8,128)(2,1)}), bf16[128,8,2048]{2,1,0:T(8,128)(2,1)}, u32[]{:S(2)}, u32[]{:S(2)}) %all-to-all-start.3) | async-done | bytes 4194336 | tf_op jit(solution)/shard_map/all_to_all | solution.py:169
  243.0 4.3 %norm_grad.1 = (bf16[64,2048]{1,0:T(8,128)(2,1)}, bf16[256,2048]{1,0:T(8,128)(2,1)}) custom-call(s32[1]{0:T(128)} %bitcast.quarter, bf16[64,1024]{1,0:T(8,128)(2,1)} %get-tuple-element.46.routes, bf16[1024,2048]{1,0:T(8,128)(2,1)} %bitcast.15.rows, bf16[256,2048]{1,0:T(8,128)(2,1)} %hidden.5, f32[1,2048]{1,0:T(1,128)} %bitcast.61, bf16[64,2048]{1,0:T(8,128)(2,1)} %grad.5), custom_call_target="tpu_custom_call" | custom-call | flops 268435456 | bytes 4194304 | tf_op jit(solution)/shard_map/norm_grad/pallas_call | solution.py:341
  247.3 1.4 collective-permute-start.7
  248.7 1.0 collective-permute-start.8
  249.7 0.7 collective-permute-start.10
  250.4 2.9 %collective-permute-done.10 = f32[1,2048]{1,0:T(1,128)S(1)} collective-permute-done((f32[1,2048]{1,0:T(1,128)S(1)}, f32[1,2048]{1,0:T(1,128)S(1)}, u32[]{:S(2)}, u32[]{:S(2)}) %collective-permute-start.10) | collective-permute-done | bytes 8224 | tf_op jit(solution)/shard_map/ppermute | solution.py:189
  253.4 1.3 collective-permute-start.11
  254.6 3.2 %collective-permute-start.9 = (bf16[64,2048]{1,0:T(8,128)(2,1)}, bf16[64,2048]{1,0:T(8,128)(2,1)S(1)}, u32[]{:S(2)}, u32[]{:S(2)}) collective-permute-start(bf16[64,2048]{1,0:T(8,128)(2,1)} %get-tuple-element.55), channel_id=1, source_target_pairs={{0,3},{1,0},{2,1},{3,2},{4,7},{5,4},{6,5},{7,6},{8,11},{9,8},{10,9... | collective-permute-start | bytes 786440 | tf_op jit(solution)/shard_map/ppermute | solution.py:177
  257.8 0.7 collective-permute-done.11
  258.6 0.6 add.88
  259.2 1.7 constant_dynamic-update-slice_fusion.2
  260.9 2.0 collective-permute-done.8
  262.9 0.7 constant_dynamic-update-slice_fusion.1
  263.6 0.7 constant_dynamic-update-slice_fusion
  (43 shorter events, 0.6 us)
Async XLA Ops:
  0.6 89.8 %copy-start = (bf16[1,768,2048]{2,1,0:T(8,128)(2,1)S(1)}, bf16[1,768,2048]{2,1,0:T(8,128)(2,1)}, u32[]{:S(2)}) copy-start(bf16[1,768,2048]{2,1,0:T(8,128)(2,1)} %param.15) | copy-start | bytes 9437188
  4.7 63.9 %all-to-all-start = ((bf16[128,8,2048]{2,1,0:T(8,128)(2,1)}), bf16[128,8,2048]{2,1,0:T(8,128)(2,1)}, u32[]{:S(2)}, u32[]{:S(2)}) async-start(bf16[128,8,2048]{2,1,0:T(8,128)(2,1)} %bitcast.58), calls=%async_computation | async-start | bytes 8388608 | tf_op jit(solution)/shard_map/all_to_all | solution.py:169
  68.6 58.1 %all-to-all-start.1 = ((bf16[128,8,2048]{2,1,0:T(8,128)(2,1)}), bf16[128,8,2048]{2,1,0:T(8,128)(2,1)}, u32[]{:S(2)}, u32[]{:S(2)}) async-start(bf16[128,8,2048]{2,1,0:T(8,128)(2,1)} %bitcast.57), calls=%async_computation.1 | async-start | bytes 8388608 | tf_op jit(solution)/shard_map/all_to_all | solution.py:169
  74.4 6.3 %copy-start.7 = (bf16[1,2048,768]{2,1,0:T(8,128)(2,1)S(1)}, bf16[1,2048,768]{2,1,0:T(8,128)(2,1)}, u32[]{:S(2)}) copy-start(bf16[1,2048,768]{2,1,0:T(8,128)(2,1)} %param.14) | copy-start | bytes 9437188
  80.7 8.6 %copy-start.13 = (f32[1024,768]{1,0:T(8,128)}, f32[1024,768]{1,0:T(8,128)S(1)}, u32[]{:S(2)}) copy-start(f32[1024,768]{1,0:T(8,128)S(1)} %fusion.8) | copy-start | bytes 9437188
  89.3 1.1 copy-start.9
  126.6 58.1 %all-to-all-start.2 = ((bf16[128,8,2048]{2,1,0:T(8,128)(2,1)}), bf16[128,8,2048]{2,1,0:T(8,128)(2,1)}, u32[]{:S(2)}, u32[]{:S(2)}) async-start(bf16[128,8,2048]{2,1,0:T(8,128)(2,1)} %bitcast.59), calls=%async_computation.2 | async-start | bytes 8388608 | tf_op jit(solution)/shard_map/all_to_all | solution.py:169
  132.7 8.4 %copy-start.6 = (bf16[1,2048,768]{2,1,0:T(8,128)(2,1)S(1)}, bf16[1,2048,768]{2,1,0:T(8,128)(2,1)}, u32[]{:S(2)}) copy-start(bf16[1,2048,768]{2,1,0:T(8,128)(2,1)} %param.13) | copy-start | bytes 9437188
  141.1 3.5 %copy-start.11 = (bf16[1024,768]{1,0:T(8,128)(2,1)}, bf16[1024,768]{1,0:T(8,128)(2,1)S(1)}, u32[]{:S(2)}) copy-start(bf16[1024,768]{1,0:T(8,128)(2,1)S(1)} %get-tuple-element.42) | copy-start | bytes 4718596
  141.1 3.5 %copy-start.14 = (bf16[1024,768]{1,0:T(8,128)(2,1)}, bf16[1024,768]{1,0:T(8,128)(2,1)S(1)}, u32[]{:S(2)}) copy-start(bf16[1024,768]{1,0:T(8,128)(2,1)S(1)} %get-tuple-element.43) | copy-start | bytes 4718596
  141.1 3.5 %copy-start.8 = (bf16[1,2048,768]{2,1,0:T(8,128)(2,1)S(1)}, bf16[1,2048,768]{2,1,0:T(8,128)(2,1)}, u32[]{:S(2)}) copy-start(bf16[1,2048,768]{2,1,0:T(8,128)(2,1)} %param.14) | copy-start | bytes 9437188
  148.3 5.5 %copy-start.2 = (bf16[1024,2048]{1,0:T(8,128)(2,1)}, bf16[1024,2048]{1,0:T(8,128)(2,1)S(1)}, u32[]{:S(2)}) copy-start(bf16[1024,2048]{1,0:T(8,128)(2,1)S(1)} %add_convert_fusion) | copy-start | bytes 12582916
  148.3 5.5 %copy-start.3 = (f32[2048]{0:T(1024)S(1)}, f32[2048]{0:T(1024)}, u32[]{:S(2)}) copy-start(f32[2048]{0:T(1024)} %param.9) | copy-start | bytes 24580
  153.8 1.3 collective-permute-start
  155.1 15.7 %collective-permute-start.3 = (f32[1,2048]{1,0:T(1,128)S(1)}, f32[1,2048]{1,0:T(1,128)S(1)}, u32[]{:S(2)}, u32[]{:S(2)}) collective-permute-start(f32[1,2048]{1,0:T(1,128)S(1)} %add.74), channel_id=1, source_target_pairs={{0,3},{1,2},{2,1},{3,0},{4,7},{5,6},{6,5},{7,4},{8,11},{9,10},{10,... | collective-permute-start | bytes 24584 | tf_op jit(solution)/shard_map/ppermute | solution.py:189
  157.1 16.2 %collective-permute-start.2 = (f32[1,2048]{1,0:T(1,128)S(1)}, f32[1,2048]{1,0:T(1,128)S(1)}, u32[]{:S(2)}, u32[]{:S(2)}) collective-permute-start(f32[1,2048]{1,0:T(1,128)S(1)} %add.74), channel_id=1, source_target_pairs={{0,2},{1,3},{2,0},{3,1},{4,6},{5,7},{6,4},{7,5},{8,10},{9,11},{10,... | collective-permute-start | bytes 24584 | tf_op jit(solution)/shard_map/ppermute | solution.py:189
  157.9 18.7 %collective-permute-start.1 = (f32[1,2048]{1,0:T(1,128)S(1)}, f32[1,2048]{1,0:T(1,128)S(1)}, u32[]{:S(2)}, u32[]{:S(2)}) collective-permute-start(f32[1,2048]{1,0:T(1,128)S(1)} %add.74), channel_id=1, source_target_pairs={{0,1},{1,0},{2,3},{3,2},{4,5},{5,4},{6,7},{7,6},{8,9},{9,8},{10,11... | collective-permute-start | bytes 24584 | tf_op jit(solution)/shard_map/ppermute | solution.py:189
  184.7 6.1 %copy-start.5 = (f32[64,8]{0,1:T(8,128)S(1)}, f32[64,8]{0,1:T(8,128)}, u32[]{:S(2)}) copy-start(f32[64,8]{0,1:T(8,128)} %param.11) | copy-start | bytes 6148
  184.7 6.8 %copy-start.4 = (s32[64,8]{0,1:T(8,128)S(1)}, s32[64,8]{0,1:T(8,128)}, u32[]{:S(2)}) copy-start(s32[64,8]{0,1:T(8,128)} %param.10) | copy-start | bytes 6148
  184.7 14.4 %copy-start.10 = (bf16[1024,768]{1,0:T(8,128)(2,1)S(1)}, bf16[1024,768]{1,0:T(8,128)(2,1)}, u32[]{:S(2)}) copy-start(bf16[1024,768]{1,0:T(8,128)(2,1)} %copy-done.9) | copy-start | bytes 4718596
  184.7 58.3 %all-to-all-start.3 = ((bf16[128,8,2048]{2,1,0:T(8,128)(2,1)}), bf16[128,8,2048]{2,1,0:T(8,128)(2,1)}, u32[]{:S(2)}, u32[]{:S(2)}) async-start(bf16[128,8,2048]{2,1,0:T(8,128)(2,1)} %bitcast.56), calls=%async_computation.3 | async-start | bytes 8388608 | tf_op jit(solution)/shard_map/all_to_all | solution.py:169
  195.0 11.1 %copy-start.12 = (bf16[1024,768]{1,0:T(8,128)(2,1)S(1)}, bf16[1024,768]{1,0:T(8,128)(2,1)}, u32[]{:S(2)}) copy-start(bf16[1024,768]{1,0:T(8,128)(2,1)} %copy-done.11) | copy-start | bytes 4718596
  195.0 31.4 %collective-permute-start.6 = (f32[1,2048]{1,0:T(1,128)S(1)}, f32[1,2048]{1,0:T(1,128)S(1)}, u32[]{:S(2)}, u32[]{:S(2)}) collective-permute-start(f32[1,2048]{1,0:T(1,128)S(1)} %add_add_fusion.1), channel_id=1, source_target_pairs={{0,24},{4,28},{8,16},{12,20},{16,8},{20,12},{24,0},{28,4},{32,56},... | collective-permute-start | bytes 24584 | tf_op jit(solution)/shard_map/ppermute | solution.py:189
  197.8 28.7 %collective-permute-start.5 = (f32[1,2048]{1,0:T(1,128)S(1)}, f32[1,2048]{1,0:T(1,128)S(1)}, u32[]{:S(2)}, u32[]{:S(2)}) collective-permute-start(f32[1,2048]{1,0:T(1,128)S(1)} %add_add_fusion.1), channel_id=1, source_target_pairs={{0,16},{4,20},{8,24},{12,28},{16,0},{20,4},{24,8},{28,12},{32,48},... | collective-permute-start | bytes 24584 | tf_op jit(solution)/shard_map/ppermute | solution.py:189
  198.1 28.3 %collective-permute-start.4 = (f32[1,2048]{1,0:T(1,128)S(1)}, f32[1,2048]{1,0:T(1,128)S(1)}, u32[]{:S(2)}, u32[]{:S(2)}) collective-permute-start(f32[1,2048]{1,0:T(1,128)S(1)} %add_add_fusion.1), channel_id=1, source_target_pairs={{0,8},{4,12},{8,0},{12,4},{16,24},{20,28},{24,16},{28,20},{32,40},... | collective-permute-start | bytes 24584 | tf_op jit(solution)/shard_map/ppermute | solution.py:189
  206.1 7.5 %copy-start.15 = (bf16[1024,768]{1,0:T(8,128)(2,1)S(1)}, bf16[1024,768]{1,0:T(8,128)(2,1)}, u32[]{:S(2)}) copy-start(bf16[1024,768]{1,0:T(8,128)(2,1)} %copy-done.14) | copy-start | bytes 4718596
  243.0 21.3 %copy-start.1 = (bf16[1,768,2048]{2,1,0:T(8,128)(2,1)S(1)}, bf16[1,768,2048]{2,1,0:T(8,128)(2,1)}, u32[]{:S(2)}) copy-start(bf16[1,768,2048]{2,1,0:T(8,128)(2,1)} %param.15) | copy-start | bytes 9437188
  247.3 11.9 %collective-permute-start.7 = (bf16[64,2048]{1,0:T(8,128)(2,1)}, bf16[64,2048]{1,0:T(8,128)(2,1)}, u32[]{:S(2)}, u32[]{:S(2)}) collective-permute-start(bf16[64,2048]{1,0:T(8,128)(2,1)} %get-tuple-element.55), channel_id=1, source_target_pairs={{0,2},{1,3},{2,0},{3,1},{4,6},{5,7},{6,4},{7,5},{8,10},{9,11},{10,... | collective-permute-start | bytes 786440 | tf_op jit(solution)/shard_map/ppermute | solution.py:177
  248.7 14.2 %collective-permute-start.8 = (bf16[64,2048]{1,0:T(8,128)(2,1)}, bf16[64,2048]{1,0:T(8,128)(2,1)S(1)}, u32[]{:S(2)}, u32[]{:S(2)}) collective-permute-start(bf16[64,2048]{1,0:T(8,128)(2,1)} %get-tuple-element.55), channel_id=1, source_target_pairs={{0,1},{1,2},{2,3},{3,0},{4,5},{5,6},{6,7},{7,4},{8,9},{9,10},{10,1... | collective-permute-start | bytes 786440 | tf_op jit(solution)/shard_map/ppermute | solution.py:177
  249.7 3.7 %collective-permute-start.10 = (f32[1,2048]{1,0:T(1,128)S(1)}, f32[1,2048]{1,0:T(1,128)S(1)}, u32[]{:S(2)}, u32[]{:S(2)}) collective-permute-start(f32[1,2048]{1,0:T(1,128)S(1)} %add_add_fusion), channel_id=1, source_target_pairs={{0,32},{4,36},{8,40},{12,44},{16,48},{20,52},{24,56},{28,60},{32,0... | collective-permute-start | bytes 24584 | tf_op jit(solution)/shard_map/ppermute | solution.py:189
  253.4 5.2 %collective-permute-start.11 = (f32[1,2048]{1,0:T(1,128)S(1)}, f32[1,2048]{1,0:T(1,128)S(1)}, u32[]{:S(2)}, u32[]{:S(2)}) collective-permute-start(f32[1,2048]{1,0:T(1,128)S(1)} %add.87), channel_id=1, source_target_pairs={{0,64},{4,68},{8,72},{12,76},{16,80},{20,84},{24,88},{28,92},{32,9... | collective-permute-start | bytes 24584 | tf_op jit(solution)/shard_map/ppermute | solution.py:189
  254.6 9.0 %collective-permute-start.9 = (bf16[64,2048]{1,0:T(8,128)(2,1)}, bf16[64,2048]{1,0:T(8,128)(2,1)S(1)}, u32[]{:S(2)}, u32[]{:S(2)}) collective-permute-start(bf16[64,2048]{1,0:T(8,128)(2,1)} %get-tuple-element.55), channel_id=1, source_target_pairs={{0,3},{1,0},{2,1},{3,2},{4,7},{5,4},{6,5},{7,6},{8,11},{9,8},{10,9... | collective-permute-start | bytes 786440 | tf_op jit(solution)/shard_map/ppermute | solution.py:177

commit v8 on v7

--- a/solution.py
+++ b/solution.py
@@ -297,7 +297,7 @@
     gain_part = add_from(gain_part, "tensor", (1, 2, 3))
     back, returned, gain_part = lax.optimization_barrier((back, returned, gain_part))
     back_rows = exchange(back)
-    gain_part = add_from(gain_part, "dp", (2, 4, 6))
+    gain_part = add_from(add_from(gain_part, "dp", (2, 4, 6)), "dp", (8,))
 
     gate_pgrad, up_pgrad, act_late = lax.optimization_barrier(
         (gate_pgrad, up_pgrad, act, back)
@@ -337,7 +337,7 @@
             (back_rows, gate_wgrad, up_wgrad, down_grad, layer_out, gate_grad_t, gain_part)
         )
     )
-    gain_grad = add_from(add_from(gain_part, "dp", (8,)), "dp", (16,))[0]
+    gain_grad = add_from(gain_part, "dp", (16,))[0]
     own_grad, group_grad = pl.pallas_call(
         norm_grad_kernel,
         grid_spec=pltpu.PrefetchScalarGridSpec(

time: 266 us -> 266 us (level)
  waiting for transfers between devices: 128 us -> 120 us
  starting transfers between devices: 45.6 us -> 53.3 us
    all_to_all x4, waiting for transfers between devices: 103 us -> 92.7 us  [exchange(): return lax.all_to_all(block, AXES, split_axis=0, concat_axis=0, tiled=True)]
    ppermute x9, starting transfers between devices: 10.3 us -> 16.4 us  [add_from(): lax.ppermute(value, axis, [(i, i ^ distance) for i in range(size)])]
where the time goes in v8:
time: 266 us; the launch traced here: 265 us
  waiting for transfers between devices  120 us (45%)
  matrix products  57.3 us (22%)
  starting transfers between devices  53.3 us (20%)
  Pallas kernels  20.4 us (8%)
  local copies, waits for them, and re-layouts  6.42 us (2%)
  other arithmetic  6.14 us (2%)
    all_to_all x4, waiting for transfers between devices, exchange(): return lax.all_to_all(block, AXES, split_axis=0, concat_axis=0, tiled=True)  92.7 us
    dot_general x9, matrix products, dot(): return lax.dot_general(a, b, (dims, ((), ())), preferred_element_type=F32)  57.3 us
    all_to_all x4, starting transfers between devices, exchange(): return lax.all_to_all(block, AXES, split_axis=0, concat_axis=0, tiled=True)  29.7 us
    ppermute x9, waiting for transfers between devices, add_from(): lax.ppermute(value, axis, [(i, i ^ distance) for i in range(size)])  24.9 us
    ppermute x9, starting transfers between devices, add_from(): lax.ppermute(value, axis, [(i, i ^ distance) for i in range(size)])  16.4 us
    ppermute x3, starting transfers between devices, gather_group(): lax.ppermute(block, 'tensor', [(i, (i + step) % size) for i in range(size)])  7.19 us
    reduce_sum x1, other arithmetic, per_device(): jnp.sum(back.astype(F32) * inputs.astype(F32), axis=0, keepdims=True) / gain  5.47 us
    pallas_call x1, Pallas kernels, per_device(): pl.pallas_call(combine_kernel, grid_spec=pltpu.PrefetchScalarGridSpec(num...  5.36 us
  transfers between devices with their start and end apart: 16, of which 11 were waited for; matrix products, arithmetic and copies ran while one was open for 26% of the time, Pallas kernels for 5%

profile of v8, /device:TPU:0, one launch (start us, length us, event | category | flops | bytes accessed | tf_op | source)
XLA Modules:
  0.0 264.5 jit_solution(6433393883418493382)
XLA Ops:
  0.7 4.0 %pack_normed.1 = bf16[1024,2048]{1,0:T(8,128)(2,1)} custom-call(s32[1]{0:T(128)} %bitcast.quarter, s32[8,64]{1,0:T(8,128)} %bitcast.62, bf16[256,2048]{1,0:T(8,128)(2,1)} %hidden.5, f32[1,2048]{1,0:T(1,128)} %bitcast.60), custom_call_target="tpu_custom_call" | custom-call | flops 268435456 | bytes 4194304 | tf_op jit(solution)/shard_map/pack_normed/pallas_call | solution.py:230
  4.7 11.7 %all-to-all-start = ((bf16[128,8,2048]{2,1,0:T(8,128)(2,1)}), bf16[128,8,2048]{2,1,0:T(8,128)(2,1)}, u32[]{:S(2)}, u32[]{:S(2)}) async-start(bf16[128,8,2048]{2,1,0:T(8,128)(2,1)} %bitcast.58), calls=%async_computation | async-start | bytes 8388608 | tf_op jit(solution)/shard_map/all_to_all | solution.py:169
  16.4 4.7 %pack_scaled.1 = bf16[1024,2048]{1,0:T(8,128)(2,1)} custom-call(s32[8,64]{1,0:T(8,128)} %bitcast.63, f32[8,64]{1,0:T(8,128)} %bitcast.66, bf16[64,2048]{1,0:T(8,128)(2,1)} %grad.5), custom_call_target="tpu_custom_call" | custom-call | flops 268435456 | bytes 4194304 | tf_op jit(solution)/shard_map/pack_scaled/pallas_call | solution.py:253
  21.1 47.5 %all-to-all-done = bf16[128,8,2048]{2,1,0:T(8,128)(2,1)} async-done(((bf16[128,8,2048]{2,1,0:T(8,128)(2,1)}), bf16[128,8,2048]{2,1,0:T(8,128)(2,1)}, u32[]{:S(2)}, u32[]{:S(2)}) %all-to-all-start) | async-done | bytes 4194336 | tf_op jit(solution)/shard_map/all_to_all | solution.py:169
  68.6 5.9 %all-to-all-start.1 = ((bf16[128,8,2048]{2,1,0:T(8,128)(2,1)}), bf16[128,8,2048]{2,1,0:T(8,128)(2,1)}, u32[]{:S(2)}, u32[]{:S(2)}) async-start(bf16[128,8,2048]{2,1,0:T(8,128)(2,1)} %bitcast.57), calls=%async_computation.1 | async-start | bytes 8388608 | tf_op jit(solution)/shard_map/all_to_all | solution.py:169
  74.4 6.3 %fusion.8 = f32[1024,768]{1,0:T(8,128)S(1)} fusion(bf16[1,2048,768]{2,1,0:T(8,128)(2,1)} %param.13, bf16[128,8,2048]{2,1,0:T(8,128)(2,1)} %all-to-all-done), kind=kOutput, calls=%fused_computation.14 | convolution fusion | flops 3221225472 | bytes 10485760 | tf_op jit(solution)/shard_map/dot_general | solution.py:210
  80.7 8.6 %multiply_convert_fusion.2 = (bf16[1024,768]{1,0:T(8,128)(2,1)S(1)}, f32[1024,768]{1,0:T(8,128)}) fusion(f32[1024,768]{1,0:T(8,128)S(1)} %fusion.8, bf16[1,2048,768]{2,1,0:T(8,128)(2,1)S(1)} %copy-done.7, bf16[128,8,2048]{2,1,0:T(8,128)(2,1)} %all-to-all-done), kind=kOutput, calls=%fused_computation.19 | convolution fusion | flops 3225944064 | bytes 15204352 | tf_op jit(solution)/shard_map/dot_general | solution.py:210
  89.3 1.1 copy-done.9
  90.4 5.0 %convolution_convert_fusion = bf16[1024,2048]{1,0:T(8,128)(2,1)} fusion(bf16[1024,768]{1,0:T(8,128)(2,1)S(1)} %get-tuple-element.44, bf16[1,768,2048]{2,1,0:T(8,128)(2,1)S(1)} %copy-done), kind=kOutput, calls=%fused_computation.2 | convolution fusion | flops 3223322624 | bytes 8912896 | tf_op jit(solution)/shard_map/dot_general | solution.py:210
  95.5 31.2 %all-to-all-done.1 = bf16[128,8,2048]{2,1,0:T(8,128)(2,1)} async-done(((bf16[128,8,2048]{2,1,0:T(8,128)(2,1)}), bf16[128,8,2048]{2,1,0:T(8,128)(2,1)}, u32[]{:S(2)}, u32[]{:S(2)}) %all-to-all-start.1) | async-done | bytes 4194336 | tf_op jit(solution)/shard_map/all_to_all | solution.py:169
  126.6 6.0 %all-to-all-start.2 = ((bf16[128,8,2048]{2,1,0:T(8,128)(2,1)}), bf16[128,8,2048]{2,1,0:T(8,128)(2,1)}, u32[]{:S(2)}, u32[]{:S(2)}) async-start(bf16[128,8,2048]{2,1,0:T(8,128)(2,1)} %bitcast.59), calls=%async_computation.2 | async-start | bytes 8388608 | tf_op jit(solution)/shard_map/all_to_all | solution.py:169
  132.7 8.4 %multiply_convert_fusion = (bf16[1024,768]{1,0:T(8,128)(2,1)S(1)}, bf16[1024,768]{1,0:T(8,128)(2,1)S(1)}) fusion(f32[1024,768]{1,0:T(8,128)} %copy-done.13, f32[1024,768]{1,0:T(8,128)} %get-tuple-element.37, bf16[1024,2048]{1,0:T(8,128)(2,1)} %bitcast.9, bf16[1,768,2048]{2,1,0:T(8,128)(2,1)S(1)} %copy-done), kind=kOutput, calls=%fused_computation.16 | convolution fusion | flops 3231449088 | bytes 16777216 | tf_op jit(solution)/shard_map/dot_general | solution.py:210
  141.1 3.4 %fusion.6 = f32[1024,2048]{1,0:T(8,128)S(1)} fusion(bf16[1024,768]{1,0:T(8,128)(2,1)S(1)} %get-tuple-element.42, bf16[1,2048,768]{2,1,0:T(8,128)(2,1)S(1)} %copy-done.6), kind=kOutput, calls=%fused_computation.12 | convolution fusion | flops 3221225472 | bytes 13107200 | tf_op jit(solution)/shard_map/dot_general | solution.py:210
  144.6 3.7 %add_convert_fusion = bf16[1024,2048]{1,0:T(8,128)(2,1)S(1)} fusion(f32[1024,2048]{1,0:T(8,128)S(1)} %fusion.6, bf16[1024,768]{1,0:T(8,128)(2,1)S(1)} %get-tuple-element.43, bf16[1,2048,768]{2,1,0:T(8,128)(2,1)S(1)} %copy-done.8), kind=kOutput, calls=%fused_computation.1 | convolution fusion | flops 3225419776 | bytes 17301504 | tf_op jit(solution)/shard_map/dot_general | solution.py:210
  148.3 5.5 %multiply_reduce_fusion = f32[2048]{0:T(1024)S(1)} fusion(bf16[1024,2048]{1,0:T(8,128)(2,1)S(1)} %add_convert_fusion, bf16[128,8,2048]{2,1,0:T(8,128)(2,1)} %all-to-all-done), kind=kLoop, calls=%fused_computation | loop fusion | flops 8386560 | bytes 8396800 | tf_op jit(solution)/shard_map/reduce_sum | solution.py:295
  153.9 1.2 collective-permute-done
  155.1 2.1 collective-permute-start.3
  157.1 0.8 collective-permute-start.2
  157.9 1.3 collective-permute-start.1
  159.3 11.5 %collective-permute-done.3 = f32[1,2048]{1,0:T(1,128)S(1)} collective-permute-done((f32[1,2048]{1,0:T(1,128)S(1)}, f32[1,2048]{1,0:T(1,128)S(1)}, u32[]{:S(2)}, u32[]{:S(2)}) %collective-permute-start.3) | collective-permute-done | bytes 8224 | tf_op jit(solution)/shard_map/ppermute | solution.py:189
  170.7 2.6 collective-permute-done.2
  173.3 3.3 %collective-permute-done.1 = f32[1,2048]{1,0:T(1,128)S(1)} collective-permute-done((f32[1,2048]{1,0:T(1,128)S(1)}, f32[1,2048]{1,0:T(1,128)S(1)}, u32[]{:S(2)}, u32[]{:S(2)}) %collective-permute-start.1) | collective-permute-done | bytes 8224 | tf_op jit(solution)/shard_map/ppermute | solution.py:189
  176.7 8.0 %all-to-all-done.2 = bf16[128,8,2048]{2,1,0:T(8,128)(2,1)} async-done(((bf16[128,8,2048]{2,1,0:T(8,128)(2,1)}), bf16[128,8,2048]{2,1,0:T(8,128)(2,1)}, u32[]{:S(2)}, u32[]{:S(2)}) %all-to-all-start.2) | async-done | bytes 4194336 | tf_op jit(solution)/shard_map/all_to_all | solution.py:169
  184.7 6.1 %all-to-all-start.3 = ((bf16[128,8,2048]{2,1,0:T(8,128)(2,1)}), bf16[128,8,2048]{2,1,0:T(8,128)(2,1)}, u32[]{:S(2)}, u32[]{:S(2)}) async-start(bf16[128,8,2048]{2,1,0:T(8,128)(2,1)} %bitcast.56), calls=%async_computation.3 | async-start | bytes 8388608 | tf_op jit(solution)/shard_map/all_to_all | solution.py:169
  190.8 0.7 copy.16.probs
  191.5 0.7 copy.17.ids
  192.2 0.7 copy.15.ids
  192.9 2.1 routes.1
  195.0 2.8 %collective-permute-start.6 = (f32[1,2048]{1,0:T(1,128)S(1)}, f32[1,2048]{1,0:T(1,128)S(1)}, u32[]{:S(2)}, u32[]{:S(2)}) collective-permute-start(f32[1,2048]{1,0:T(1,128)S(1)} %add_add_fusion.1), channel_id=1, source_target_pairs={{0,24},{4,28},{8,16},{12,20},{16,8},{20,12},{24,0},{28,4},{32,56},... | collective-permute-start | bytes 24584 | tf_op jit(solution)/shard_map/ppermute | solution.py:189
  197.8 0.3 collective-permute-start.5
  198.1 1.0 collective-permute-start.4
  199.1 7.0 %convolution_convert_fusion.1 = bf16[768,2048]{1,0:T(8,128)(2,1)} fusion(bf16[1024,768]{1,0:T(8,128)(2,1)S(1)} %copy-done.10, bf16[1024,2048]{1,0:T(8,128)(2,1)} %bitcast.9), kind=kOutput, calls=%fused_computation.3 | convolution fusion | flops 3222798336 | bytes 8912896 | tf_op jit(solution)/shard_map/dot_general | solution.py:210
  206.1 7.5 %convolution_convert_fusion.3 = bf16[2048,768]{1,0:T(8,128)(2,1)} fusion(bf16[1024,768]{1,0:T(8,128)(2,1)S(1)} %copy-done.12, bf16[128,8,2048]{2,1,0:T(8,128)(2,1)} %all-to-all-done), kind=kOutput, calls=%fused_computation.5 | convolution fusion | flops 3222798336 | bytes 8912896 | tf_op jit(solution)/shard_map/dot_general | solution.py:210
  213.6 7.4 %convolution_convert_fusion.2 = bf16[2048,768]{1,0:T(8,128)(2,1)} fusion(bf16[1024,768]{1,0:T(8,128)(2,1)S(1)} %copy-done.15, bf16[128,8,2048]{2,1,0:T(8,128)(2,1)} %all-to-all-done), kind=kOutput, calls=%fused_computation.4 | convolution fusion | flops 3222798336 | bytes 8912896 | tf_op jit(solution)/shard_map/dot_general | solution.py:210
  221.0 0.2 collective-permute-done.6
  221.2 4.3 %collective-permute-start.7 = (f32[1,2048]{1,0:T(1,128)S(1)}, f32[1,2048]{1,0:T(1,128)S(1)}, u32[]{:S(2)}, u32[]{:S(2)}) collective-permute-start(f32[1,2048]{1,0:T(1,128)S(1)} %add_add_fusion), channel_id=1, source_target_pairs={{0,32},{4,36},{8,40},{12,44},{16,48},{20,52},{24,56},{28,60},{32,0... | collective-permute-start | bytes 24584 | tf_op jit(solution)/shard_map/ppermute | solution.py:189
  225.5 5.4 %combine.1 = (bf16[64,2048]{1,0:T(8,128)(2,1)}, f32[8,64]{1,0:T(8,128)}) custom-call(s32[1]{0:T(128)} %bitcast.quarter, s32[64,8]{1,0:T(8,128)} %copy.17.ids, bf16[64,1024]{1,0:T(8,128)(2,1)} %get-tuple-element.46.routes, bf16[192,1024]{1,0:T(8,128)(2,1)} %get-tuple-element.47.weights, bf16[1024,2048]{1,0:T(8,128)(2,1)} %bitcast.12.rows, ...), custom_call_target="tpu_custom_call" | custom-call | flops 1073741824 | bytes 4194304 | tf_op jit(solution)/shard_map/combine/pallas_call | solution.py:310
  230.9 6.1 %collective-permute-done.7 = f32[1,2048]{1,0:T(1,128)S(1)} collective-permute-done((f32[1,2048]{1,0:T(1,128)S(1)}, f32[1,2048]{1,0:T(1,128)S(1)}, u32[]{:S(2)}, u32[]{:S(2)}) %collective-permute-start.7) | collective-permute-done | bytes 8224 | tf_op jit(solution)/shard_map/ppermute | solution.py:189
  237.0 6.0 %all-to-all-done.3 = bf16[128,8,2048]{2,1,0:T(8,128)(2,1)} async-done(((bf16[128,8,2048]{2,1,0:T(8,128)(2,1)}), bf16[128,8,2048]{2,1,0:T(8,128)(2,1)}, u32[]{:S(2)}, u32[]{:S(2)}) %all-to-all-start.3) | async-done | bytes 4194336 | tf_op jit(solution)/shard_map/all_to_all | solution.py:169
  243.0 4.3 %norm_grad.1 = (bf16[64,2048]{1,0:T(8,128)(2,1)}, bf16[256,2048]{1,0:T(8,128)(2,1)}) custom-call(s32[1]{0:T(128)} %bitcast.quarter, bf16[64,1024]{1,0:T(8,128)(2,1)} %get-tuple-element.46.routes, bf16[1024,2048]{1,0:T(8,128)(2,1)} %bitcast.15.rows, bf16[256,2048]{1,0:T(8,128)(2,1)} %hidden.5, f32[1,2048]{1,0:T(1,128)} %bitcast.61, bf16[64,2048]{1,0:T(8,128)(2,1)} %grad.5), custom_call_target="tpu_custom_call" | custom-call | flops 268435456 | bytes 4194304 | tf_op jit(solution)/shard_map/norm_grad/pallas_call | solution.py:341
  247.3 3.9 %collective-permute-start.8 = (bf16[64,2048]{1,0:T(8,128)(2,1)}, bf16[64,2048]{1,0:T(8,128)(2,1)}, u32[]{:S(2)}, u32[]{:S(2)}) collective-permute-start(bf16[64,2048]{1,0:T(8,128)(2,1)} %get-tuple-element.55), channel_id=1, source_target_pairs={{0,2},{1,3},{2,0},{3,1},{4,6},{5,7},{6,4},{7,5},{8,10},{9,11},{10,... | collective-permute-start | bytes 786440 | tf_op jit(solution)/shard_map/ppermute | solution.py:177
  251.2 3.8 %collective-permute-start.11 = (f32[1,2048]{1,0:T(1,128)S(1)}, f32[1,2048]{1,0:T(1,128)S(1)}, u32[]{:S(2)}, u32[]{:S(2)}) collective-permute-start(f32[1,2048]{1,0:T(1,128)S(1)} %add.81), channel_id=1, source_target_pairs={{0,64},{4,68},{8,72},{12,76},{16,80},{20,84},{24,88},{28,92},{32,9... | collective-permute-start | bytes 24584 | tf_op jit(solution)/shard_map/ppermute | solution.py:189
  255.0 3.2 %collective-permute-start.10 = (bf16[64,2048]{1,0:T(8,128)(2,1)}, bf16[64,2048]{1,0:T(8,128)(2,1)S(1)}, u32[]{:S(2)}, u32[]{:S(2)}) collective-permute-start(bf16[64,2048]{1,0:T(8,128)(2,1)} %get-tuple-element.55), channel_id=1, source_target_pairs={{0,3},{1,0},{2,1},{3,2},{4,7},{5,4},{6,5},{7,6},{8,11},{9,8},{10,9... | collective-permute-start | bytes 786440 | tf_op jit(solution)/shard_map/ppermute | solution.py:177
  258.2 0.6 add.88
  258.8 1.7 constant_dynamic-update-slice_fusion.2
  260.5 2.6 collective-permute-done.9
  263.1 0.7 constant_dynamic-update-slice_fusion.1
  263.8 0.7 constant_dynamic-update-slice_fusion
  (43 shorter events, 0.2 us)
Async XLA Ops:
  0.6 89.8 %copy-start = (bf16[1,768,2048]{2,1,0:T(8,128)(2,1)S(1)}, bf16[1,768,2048]{2,1,0:T(8,128)(2,1)}, u32[]{:S(2)}) copy-start(bf16[1,768,2048]{2,1,0:T(8,128)(2,1)} %param.15) | copy-start | bytes 9437188
  4.7 63.9 %all-to-all-start = ((bf16[128,8,2048]{2,1,0:T(8,128)(2,1)}), bf16[128,8,2048]{2,1,0:T(8,128)(2,1)}, u32[]{:S(2)}, u32[]{:S(2)}) async-start(bf16[128,8,2048]{2,1,0:T(8,128)(2,1)} %bitcast.58), calls=%async_computation | async-start | bytes 8388608 | tf_op jit(solution)/shard_map/all_to_all | solution.py:169
  68.6 58.1 %all-to-all-start.1 = ((bf16[128,8,2048]{2,1,0:T(8,128)(2,1)}), bf16[128,8,2048]{2,1,0:T(8,128)(2,1)}, u32[]{:S(2)}, u32[]{:S(2)}) async-start(bf16[128,8,2048]{2,1,0:T(8,128)(2,1)} %bitcast.57), calls=%async_computation.1 | async-start | bytes 8388608 | tf_op jit(solution)/shard_map/all_to_all | solution.py:169
  74.4 6.3 %copy-start.7 = (bf16[1,2048,768]{2,1,0:T(8,128)(2,1)S(1)}, bf16[1,2048,768]{2,1,0:T(8,128)(2,1)}, u32[]{:S(2)}) copy-start(bf16[1,2048,768]{2,1,0:T(8,128)(2,1)} %param.14) | copy-start | bytes 9437188
  80.7 8.6 %copy-start.13 = (f32[1024,768]{1,0:T(8,128)}, f32[1024,768]{1,0:T(8,128)S(1)}, u32[]{:S(2)}) copy-start(f32[1024,768]{1,0:T(8,128)S(1)} %fusion.8) | copy-start | bytes 9437188
  89.3 1.1 copy-start.9
  126.6 58.1 %all-to-all-start.2 = ((bf16[128,8,2048]{2,1,0:T(8,128)(2,1)}), bf16[128,8,2048]{2,1,0:T(8,128)(2,1)}, u32[]{:S(2)}, u32[]{:S(2)}) async-start(bf16[128,8,2048]{2,1,0:T(8,128)(2,1)} %bitcast.59), calls=%async_computation.2 | async-start | bytes 8388608 | tf_op jit(solution)/shard_map/all_to_all | solution.py:169
  132.7 8.4 %copy-start.6 = (bf16[1,2048,768]{2,1,0:T(8,128)(2,1)S(1)}, bf16[1,2048,768]{2,1,0:T(8,128)(2,1)}, u32[]{:S(2)}) copy-start(bf16[1,2048,768]{2,1,0:T(8,128)(2,1)} %param.13) | copy-start | bytes 9437188
  141.1 3.5 %copy-start.11 = (bf16[1024,768]{1,0:T(8,128)(2,1)}, bf16[1024,768]{1,0:T(8,128)(2,1)S(1)}, u32[]{:S(2)}) copy-start(bf16[1024,768]{1,0:T(8,128)(2,1)S(1)} %get-tuple-element.42) | copy-start | bytes 4718596
  141.1 3.5 %copy-start.14 = (bf16[1024,768]{1,0:T(8,128)(2,1)}, bf16[1024,768]{1,0:T(8,128)(2,1)S(1)}, u32[]{:S(2)}) copy-start(bf16[1024,768]{1,0:T(8,128)(2,1)S(1)} %get-tuple-element.43) | copy-start | bytes 4718596
  141.1 3.5 %copy-start.8 = (bf16[1,2048,768]{2,1,0:T(8,128)(2,1)S(1)}, bf16[1,2048,768]{2,1,0:T(8,128)(2,1)}, u32[]{:S(2)}) copy-start(bf16[1,2048,768]{2,1,0:T(8,128)(2,1)} %param.14) | copy-start | bytes 9437188
  148.3 5.5 %copy-start.2 = (bf16[1024,2048]{1,0:T(8,128)(2,1)}, bf16[1024,2048]{1,0:T(8,128)(2,1)S(1)}, u32[]{:S(2)}) copy-start(bf16[1024,2048]{1,0:T(8,128)(2,1)S(1)} %add_convert_fusion) | copy-start | bytes 12582916
  148.3 5.5 %copy-start.3 = (f32[2048]{0:T(1024)S(1)}, f32[2048]{0:T(1024)}, u32[]{:S(2)}) copy-start(f32[2048]{0:T(1024)} %param.9) | copy-start | bytes 24580
  153.8 1.3 collective-permute-start
  155.1 15.7 %collective-permute-start.3 = (f32[1,2048]{1,0:T(1,128)S(1)}, f32[1,2048]{1,0:T(1,128)S(1)}, u32[]{:S(2)}, u32[]{:S(2)}) collective-permute-start(f32[1,2048]{1,0:T(1,128)S(1)} %add.74), channel_id=1, source_target_pairs={{0,3},{1,2},{2,1},{3,0},{4,7},{5,6},{6,5},{7,4},{8,11},{9,10},{10,... | collective-permute-start | bytes 24584 | tf_op jit(solution)/shard_map/ppermute | solution.py:189
  157.1 16.2 %collective-permute-start.2 = (f32[1,2048]{1,0:T(1,128)S(1)}, f32[1,2048]{1,0:T(1,128)S(1)}, u32[]{:S(2)}, u32[]{:S(2)}) collective-permute-start(f32[1,2048]{1,0:T(1,128)S(1)} %add.74), channel_id=1, source_target_pairs={{0,2},{1,3},{2,0},{3,1},{4,6},{5,7},{6,4},{7,5},{8,10},{9,11},{10,... | collective-permute-start | bytes 24584 | tf_op jit(solution)/shard_map/ppermute | solution.py:189
  157.9 18.7 %collective-permute-start.1 = (f32[1,2048]{1,0:T(1,128)S(1)}, f32[1,2048]{1,0:T(1,128)S(1)}, u32[]{:S(2)}, u32[]{:S(2)}) collective-permute-start(f32[1,2048]{1,0:T(1,128)S(1)} %add.74), channel_id=1, source_target_pairs={{0,1},{1,0},{2,3},{3,2},{4,5},{5,4},{6,7},{7,6},{8,9},{9,8},{10,11... | collective-permute-start | bytes 24584 | tf_op jit(solution)/shard_map/ppermute | solution.py:189
  184.7 6.1 %copy-start.5 = (f32[64,8]{0,1:T(8,128)S(1)}, f32[64,8]{0,1:T(8,128)}, u32[]{:S(2)}) copy-start(f32[64,8]{0,1:T(8,128)} %param.11) | copy-start | bytes 6148
  184.7 6.8 %copy-start.4 = (s32[64,8]{0,1:T(8,128)S(1)}, s32[64,8]{0,1:T(8,128)}, u32[]{:S(2)}) copy-start(s32[64,8]{0,1:T(8,128)} %param.10) | copy-start | bytes 6148
  184.7 14.4 %copy-start.10 = (bf16[1024,768]{1,0:T(8,128)(2,1)S(1)}, bf16[1024,768]{1,0:T(8,128)(2,1)}, u32[]{:S(2)}) copy-start(bf16[1024,768]{1,0:T(8,128)(2,1)} %copy-done.9) | copy-start | bytes 4718596
  184.7 58.3 %all-to-all-start.3 = ((bf16[128,8,2048]{2,1,0:T(8,128)(2,1)}), bf16[128,8,2048]{2,1,0:T(8,128)(2,1)}, u32[]{:S(2)}, u32[]{:S(2)}) async-start(bf16[128,8,2048]{2,1,0:T(8,128)(2,1)} %bitcast.56), calls=%async_computation.3 | async-start | bytes 8388608 | tf_op jit(solution)/shard_map/all_to_all | solution.py:169
  195.0 11.1 %copy-start.12 = (bf16[1024,768]{1,0:T(8,128)(2,1)S(1)}, bf16[1024,768]{1,0:T(8,128)(2,1)}, u32[]{:S(2)}) copy-start(bf16[1024,768]{1,0:T(8,128)(2,1)} %copy-done.11) | copy-start | bytes 4718596
  195.0 26.2 %collective-permute-start.6 = (f32[1,2048]{1,0:T(1,128)S(1)}, f32[1,2048]{1,0:T(1,128)S(1)}, u32[]{:S(2)}, u32[]{:S(2)}) collective-permute-start(f32[1,2048]{1,0:T(1,128)S(1)} %add_add_fusion.1), channel_id=1, source_target_pairs={{0,24},{4,28},{8,16},{12,20},{16,8},{20,12},{24,0},{28,4},{32,56},... | collective-permute-start | bytes 24584 | tf_op jit(solution)/shard_map/ppermute | solution.py:189
  197.8 23.4 %collective-permute-start.5 = (f32[1,2048]{1,0:T(1,128)S(1)}, f32[1,2048]{1,0:T(1,128)S(1)}, u32[]{:S(2)}, u32[]{:S(2)}) collective-permute-start(f32[1,2048]{1,0:T(1,128)S(1)} %add_add_fusion.1), channel_id=1, source_target_pairs={{0,16},{4,20},{8,24},{12,28},{16,0},{20,4},{24,8},{28,12},{32,48},... | collective-permute-start | bytes 24584 | tf_op jit(solution)/shard_map/ppermute | solution.py:189
  198.1 23.1 %collective-permute-start.4 = (f32[1,2048]{1,0:T(1,128)S(1)}, f32[1,2048]{1,0:T(1,128)S(1)}, u32[]{:S(2)}, u32[]{:S(2)}) collective-permute-start(f32[1,2048]{1,0:T(1,128)S(1)} %add_add_fusion.1), channel_id=1, source_target_pairs={{0,8},{4,12},{8,0},{12,4},{16,24},{20,28},{24,16},{28,20},{32,40},... | collective-permute-start | bytes 24584 | tf_op jit(solution)/shard_map/ppermute | solution.py:189
  206.1 7.5 %copy-start.15 = (bf16[1024,768]{1,0:T(8,128)(2,1)S(1)}, bf16[1024,768]{1,0:T(8,128)(2,1)}, u32[]{:S(2)}) copy-start(bf16[1024,768]{1,0:T(8,128)(2,1)} %copy-done.14) | copy-start | bytes 4718596
  221.2 15.8 %collective-permute-start.7 = (f32[1,2048]{1,0:T(1,128)S(1)}, f32[1,2048]{1,0:T(1,128)S(1)}, u32[]{:S(2)}, u32[]{:S(2)}) collective-permute-start(f32[1,2048]{1,0:T(1,128)S(1)} %add_add_fusion), channel_id=1, source_target_pairs={{0,32},{4,36},{8,40},{12,44},{16,48},{20,52},{24,56},{28,60},{32,0... | collective-permute-start | bytes 24584 | tf_op jit(solution)/shard_map/ppermute | solution.py:189
  243.0 21.5 %copy-start.1 = (bf16[1,768,2048]{2,1,0:T(8,128)(2,1)S(1)}, bf16[1,768,2048]{2,1,0:T(8,128)(2,1)}, u32[]{:S(2)}) copy-start(bf16[1,768,2048]{2,1,0:T(8,128)(2,1)} %param.15) | copy-start | bytes 9437188
  247.3 11.6 %collective-permute-start.8 = (bf16[64,2048]{1,0:T(8,128)(2,1)}, bf16[64,2048]{1,0:T(8,128)(2,1)}, u32[]{:S(2)}, u32[]{:S(2)}) collective-permute-start(bf16[64,2048]{1,0:T(8,128)(2,1)} %get-tuple-element.55), channel_id=1, source_target_pairs={{0,2},{1,3},{2,0},{3,1},{4,6},{5,7},{6,4},{7,5},{8,10},{9,11},{10,... | collective-permute-start | bytes 786440 | tf_op jit(solution)/shard_map/ppermute | solution.py:177
  251.2 11.9 %collective-permute-start.9 = (bf16[64,2048]{1,0:T(8,128)(2,1)}, bf16[64,2048]{1,0:T(8,128)(2,1)S(1)}, u32[]{:S(2)}, u32[]{:S(2)}) collective-permute-start(bf16[64,2048]{1,0:T(8,128)(2,1)} %get-tuple-element.55), channel_id=1, source_target_pairs={{0,1},{1,2},{2,3},{3,0},{4,5},{5,6},{6,7},{7,4},{8,9},{9,10},{10,1... | collective-permute-start | bytes 786440 | tf_op jit(solution)/shard_map/ppermute | solution.py:177
  251.2 7.0 %collective-permute-start.11 = (f32[1,2048]{1,0:T(1,128)S(1)}, f32[1,2048]{1,0:T(1,128)S(1)}, u32[]{:S(2)}, u32[]{:S(2)}) collective-permute-start(f32[1,2048]{1,0:T(1,128)S(1)} %add.81), channel_id=1, source_target_pairs={{0,64},{4,68},{8,72},{12,76},{16,80},{20,84},{24,88},{28,92},{32,9... | collective-permute-start | bytes 24584 | tf_op jit(solution)/shard_map/ppermute | solution.py:189
  255.0 8.8 %collective-permute-start.10 = (bf16[64,2048]{1,0:T(8,128)(2,1)}, bf16[64,2048]{1,0:T(8,128)(2,1)S(1)}, u32[]{:S(2)}, u32[]{:S(2)}) collective-permute-start(bf16[64,2048]{1,0:T(8,128)(2,1)} %get-tuple-element.55), channel_id=1, source_target_pairs={{0,3},{1,0},{2,1},{3,2},{4,7},{5,4},{6,5},{7,6},{8,11},{9,8},{10,9... | collective-permute-start | bytes 786440 | tf_op jit(solution)/shard_map/ppermute | solution.py:177
